TPU v7x, 32 devices: a whole 2x2x4 slice. The times are simulated.
32 devices in a mesh: ctx: 16 (over z, y, x), wt: 2 (over core).
Axes of the slice: x: 2, y: 2, z: 4, core: 2. Of those that a mesh axis runs over, the one named last changes fastest.
Arguments:
- tokens: bfloat16 [4096, 2048], P('ctx'), may hold values from -6 to 6
- layer_input: bfloat16 [4096, 256], P('ctx'), may hold values from -6 to 6
- out_grad: bfloat16 [4096, 2048], P('ctx'), may hold values from -6 to 6
- block_device: int32 [1, 16], replicated, may hold values from 0 to 15, each once within a row
- adapter_pick: int32 [1, 8], replicated, may hold values from 0 to 7, as said below
- norm_gains: bfloat16 [6, 2048], replicated, may hold values from 0.25 to 1.75
- head_norm_gains: bfloat16 [2, 256], replicated, may hold values from 0.25 to 1.75
- query_weight: bfloat16 [2048, 2048], P('ctx', 'wt'), may hold values from -0.125 to 0.125
- key_matrix: bfloat16 [2048, 512], P('ctx', 'wt'), may hold values from -0.125 to 0.125
- value_matrix: bfloat16 [2048, 512], P('ctx', 'wt'), may hold values from -0.125 to 0.125
- gate_weight: bfloat16 [2048, 8192], P('ctx', 'wt'), may hold values from -0.125 to 0.125
- up_weight: bfloat16 [2048, 8192], P('ctx', 'wt'), may hold values from -0.125 to 0.125
- out_weight: bfloat16 [2048, 2048], P('wt', 'ctx'), may hold values from -0.125 to 0.125
- down_weight: bfloat16 [8192, 2048], P('wt', 'ctx'), may hold values from -0.0625 to 0.0625
- laurel_left: bfloat16 [2048, 64], replicated, may hold values from -0.125 to 0.125
- laurel_right: bfloat16 [64, 2048], replicated, may hold values from -0.75 to 0.75
- layer_gate: bfloat16 [2048, 256], replicated, may hold values from -0.125 to 0.125
- layer_lift: bfloat16 [256, 2048], replicated, may hold values from -0.375 to 0.375
- query_shrink: bfloat16 [128, 2048], replicated, may hold values from -0.125 to 0.125
- key_shrink: bfloat16 [128, 2048], replicated, may hold values from -0.125 to 0.125
- value_shrink: bfloat16 [128, 2048], replicated, may hold values from -0.125 to 0.125
- gate_shrink: bfloat16 [128, 2048], replicated, may hold values from -0.125 to 0.125
- up_shrink: bfloat16 [128, 2048], replicated, may hold values from -0.125 to 0.125
- out_shrink: bfloat16 [128, 2048], P(None, 'wt'), may hold values from -0.125 to 0.125
- down_shrink: bfloat16 [128, 8192], P(None, 'wt'), may hold values from -0.0625 to 0.0625
- query_expand: bfloat16 [128, 2048], P(None, 'wt'), may hold values from -1.5 to 1.5
- key_widen_maps: bfloat16 [128, 512], P(None, 'wt'), may hold values from -1.5 to 1.5
- value_widen_maps: bfloat16 [128, 512], P(None, 'wt'), may hold values from -1.5 to 1.5
- gate_expand: bfloat16 [128, 8192], P(None, 'wt'), may hold values from -1.5 to 1.5
- up_expand: bfloat16 [128, 8192], P(None, 'wt'), may hold values from -1.5 to 1.5
- out_expand: bfloat16 [128, 2048], replicated, may hold values from -1.5 to 1.5
- down_expand: bfloat16 [128, 2048], replicated, may hold values from -1.5 to 1.5
Outputs:
- layer_output: bfloat16 [4096, 2048], P('ctx')
- input_grad: float32 [4096, 2048], P('ctx')
- layer_input_grad: float32 [4096, 256], P('ctx')
- query_shrink_grad: float32 [128, 2048], P(('ctx', 'wt'))
- key_shrink_grad: float32 [128, 2048], P(('ctx', 'wt'))
- value_shrink_grad: float32 [128, 2048], P(('ctx', 'wt'))
- gate_shrink_grad: float32 [128, 2048], P(('ctx', 'wt'))
- up_shrink_grad: float32 [128, 2048], P(('ctx', 'wt'))
- out_shrink_grad: float32 [128, 2048], P('ctx', 'wt')
- down_shrink_grad: float32 [128, 8192], P('ctx', 'wt')
- query_expand_grad: float32 [128, 2048], P('ctx', 'wt')
- key_expand_grad: float32 [128, 512], P('ctx', 'wt')
- value_expand_grad: float32 [128, 512], P('ctx', 'wt')
- gate_expand_grad: float32 [128, 8192], P('ctx', 'wt')
- up_expand_grad: float32 [128, 8192], P('ctx', 'wt')
- out_expand_grad: float32 [128, 2048], P(('ctx', 'wt'))
- down_expand_grad: float32 [128, 2048], P(('ctx', 'wt'))
Inputs may be any that keep to these rules, and one draw needn't show every extreme that they name: Each row of block_device names every index along ctx once: block b of group g (its tokens b * 256 to b * 256 + 255) is held by index block_device[g, b]. `adapter_pick`: column c names the adapter of continuation c + 1 of the group; the continuations of one group have different adapters.
All inputs are finite; a program needn't handle non-finite values.
Results may differ from a plain program's by a relative error of at most 0.019.
Values may be sent and summed in bfloat16 or wider, within the bound.
No kernel may reach another device: no remote copies, remote signals or barrier semaphores. Data moves between devices by JAX's collectives and lax.ppermute only.
A program may use at most 256 MiB of HBM per device.

v0:
```python
import math

import jax
import jax.numpy as jnp
from jax import lax
from jax.sharding import PartitionSpec as P

QUERY_HEADS = 8
KEY_VALUE_HEADS = 2
ADAPTER_COUNT = 8
ADAPTER_RANK = 16
PROMPT = 2048
CONT = 256


EPS = 1e-06
THETA = 1000000.0
FLOOR = -1e30
ROOT_HALF = 0.5**0.5
HIGHEST = lax.Precision.HIGHEST


def normalized(inputs, norm_gain):
    return inputs * lax.rsqrt(jnp.mean(inputs * inputs, axis=-1, keepdims=True) + EPS) * norm_gain


def norm_pull(inputs, norm_gain, upstream):
    return jax.vjp(lambda inner: normalized(inner, norm_gain), inputs)[1](upstream)[0]


def rotary_applied(inputs, rotary_angles):
    half_width = inputs.shape[-1] // 2
    cosine = jnp.cos(rotary_angles)[:, None, :]
    sine_term = jnp.sin(rotary_angles)[:, None, :]
    first_half = inputs[..., :half_width]
    second_half = inputs[..., half_width:]
    return jnp.concatenate(
        [
            first_half * cosine - second_half * sine_term,
            second_half * cosine + first_half * sine_term,
        ],
        axis=-1,
    )


def segment_of(positions):
    return jnp.where(positions < PROMPT, 0, 1 + (positions - PROMPT) // CONT)


def glu_form(gate_in, up_in):
    return jax.nn.gelu(gate_in, approximate=True) * up_in


def product(left_side, right_side):
    return jnp.dot(left_side, right_side, preferred_element_type=jnp.float32)


def against(left_side, right_side):
    return lax.dot_general(
        left_side, right_side, (((1,), (1,)), ((), ())), preferred_element_type=jnp.float32
    )


def precise(left_side, right_side):
    return jnp.dot(left_side, right_side.astype(jnp.float32), precision=HIGHEST)


def local(
    tokens,
    layer_input,
    out_grad,
    block_device,
    adapter_pick,
    norm_gains,
    head_norm_gains,
    query_weight,
    key_matrix,
    value_matrix,
    gate_weight,
    up_weight,
    out_weight,
    down_weight,
    laurel_left,
    laurel_right,
    layer_gate,
    layer_lift,
    query_shrink,
    key_shrink,
    value_shrink,
    gate_shrink,
    up_shrink,
    out_shrink,
    down_shrink,
    query_expand,
    key_widen_maps,
    value_widen_maps,
    gate_expand,
    up_expand,
    out_expand,
    down_expand,
):
    count_ctx = lax.axis_size("ctx")
    groups = block_device.shape[0]
    local_rows = tokens.shape[0]
    block_len = local_rows // groups
    head_dim = head_norm_gains.shape[1]
    kv_width = key_matrix.shape[1]
    kv_local = kv_width // head_dim
    group_portion = QUERY_HEADS // KEY_VALUE_HEADS
    keys_len = PROMPT + CONT
    my_index = lax.axis_index("ctx")
    group_ids = jnp.arange(groups, dtype=jnp.int32)
    device_ids = jnp.arange(count_ctx, dtype=jnp.int32)
    my_block = jnp.sum(jnp.where(block_device == my_index, device_ids[None, :], 0), axis=1)
    positions = my_block[:, None] * block_len + jnp.arange(block_len, dtype=jnp.int32)[None, :]
    segments = segment_of(positions)
    seq_pos = jnp.where(positions < PROMPT, positions, PROMPT + (positions - PROMPT) % CONT)
    cont_of_row = jnp.maximum(segments - 1, 0)
    picked = jnp.where(
        segments == 0, -1, jnp.take_along_axis(adapter_pick, cont_of_row, axis=1)
    ).reshape(-1)
    select = (
        jnp.arange(ADAPTER_COUNT * ADAPTER_RANK, dtype=jnp.int32)[None, :] // ADAPTER_RANK
        == picked[:, None]
    ).astype(jnp.float32)
    frequency = THETA ** (-2.0 * jnp.arange(head_dim // 2, dtype=jnp.float32) / head_dim)
    rotary_angles = seq_pos.reshape(-1).astype(jnp.float32)[:, None] * frequency[None, :]
    cont_index = jnp.maximum(segments[:, 0] - 1, 0)
    prompt_pos = jnp.broadcast_to(jnp.arange(PROMPT, dtype=jnp.int32)[None, :], (groups, PROMPT))
    tail_pos = PROMPT + cont_index[:, None] * CONT + jnp.arange(CONT, dtype=jnp.int32)[None, :]
    key_pos = jnp.concatenate([prompt_pos, tail_pos], axis=1)
    key_segments = segment_of(key_pos)
    allowed = (key_pos[:, None, :] <= positions[:, :, None]) & (
        (key_segments[:, None, :] == 0) | (key_segments[:, None, :] == segments[:, :, None])
    )
    key_device = jnp.take_along_axis(block_device, key_pos // block_len, axis=1)
    key_offset = key_pos % block_len
    gains = norm_gains.astype(jnp.float32)
    query_gain = head_norm_gains[0].astype(jnp.float32)
    key_gain = head_norm_gains[1].astype(jnp.float32)

    def query_piece(projected):
        return rotary_applied(
            normalized(projected.reshape(local_rows, -1, head_dim), query_gain), rotary_angles
        ) * head_dim ** (-0.5)

    def key_piece(projected):
        return rotary_applied(
            normalized(projected.reshape(local_rows, -1, head_dim), key_gain), rotary_angles
        ).reshape(local_rows, -1)

    def value_piece(projected):
        return normalized(projected.reshape(local_rows, -1, head_dim), 1.0).reshape(local_rows, -1)

    tokens_wide = tokens.astype(jnp.float32)
    first_norm = normalized(tokens_wide, gains[0])
    first_low = first_norm.astype(jnp.bfloat16)
    rows_kept = (
        lax.all_gather(query_weight, "ctx", axis=0, tiled=True),
        lax.all_gather(key_matrix, "ctx", axis=0, tiled=True),
        lax.all_gather(value_matrix, "ctx", axis=0, tiled=True),
        lax.all_gather(gate_weight, "ctx", axis=0, tiled=True),
        lax.all_gather(up_weight, "ctx", axis=0, tiled=True),
    )
    cols_kept = (
        lax.all_gather(out_weight, "ctx", axis=1, tiled=True),
        lax.all_gather(down_weight, "ctx", axis=1, tiled=True),
    )
    full_query, full_key, full_value, full_gate, full_up = rows_kept
    full_out, full_down = cols_kept
    rank_query = select * against(first_low, query_shrink)
    rank_key = select * against(first_low, key_shrink)
    rank_value = select * against(first_low, value_shrink)
    query_proj = product(first_low, full_query) + precise(rank_query, query_expand)
    key_projected = product(first_low, full_key) + precise(rank_key, key_widen_maps)
    value_projected = product(first_low, full_value) + precise(rank_value, value_widen_maps)
    query_low = query_piece(query_proj).astype(jnp.bfloat16)
    key_low = key_piece(key_projected).astype(jnp.bfloat16)
    value_low = value_piece(value_projected).astype(jnp.bfloat16)
    key_all, value_all = (
        lax.all_gather(key_low, "ctx", axis=0, tiled=True),
        lax.all_gather(value_low, "ctx", axis=0, tiled=True),
    )

    def group_keys(spread):
        shaped = spread.reshape(count_ctx, groups, block_len, kv_width)
        return shaped[key_device, group_ids[:, None], key_offset]

    per_step = math.gcd(groups, max(1, 512 // (group_portion * block_len)))
    step_count = groups // per_step
    query_grouped = query_low.reshape(
        step_count, per_step, block_len, kv_local, group_portion, head_dim
    )
    keys_grouped = group_keys(key_all).reshape(step_count, per_step, keys_len, kv_local, head_dim)
    values_grouped = group_keys(value_all).reshape(
        step_count, per_step, keys_len, kv_local, head_dim
    )
    allowed_grouped = allowed.reshape(step_count, per_step, block_len, keys_len)

    def scores_of(query_part, key_part, allow_part):
        raw_scores = jnp.einsum(
            "pqgsd,pkgd->pgsqk", query_part, key_part, preferred_element_type=jnp.float32
        )
        return jnp.where(allow_part[:, None, None], raw_scores, FLOOR)

    def attend(members):
        query_part, key_part, value_part, allow_part = members
        scores = scores_of(query_part, key_part, allow_part)
        row_max = jnp.max(scores, axis=-1, keepdims=True)
        exponent = jnp.exp(scores - row_max)
        running = jnp.sum(exponent, axis=-1, keepdims=True)
        chances = (exponent / running).astype(jnp.bfloat16)
        mixed = jnp.einsum(
            "pgsqk,pkgd->pqgsd", chances, value_part, preferred_element_type=jnp.float32
        )
        return (mixed, row_max + jnp.log(running))

    mixed, log_total = lax.map(
        attend, (query_grouped, keys_grouped, values_grouped, allowed_grouped)
    )
    heads_low = mixed.reshape(local_rows, -1).astype(jnp.bfloat16)
    rank_out = select * against(heads_low, out_shrink)
    attn_total = lax.psum(product(heads_low, full_out) + precise(rank_out, out_expand), "wt")
    laurel_rank = product(first_low, laurel_left).astype(jnp.bfloat16)
    laurel_back = product(laurel_rank, laurel_right)
    mid_stream = (
        tokens_wide
        + normalized(attn_total, gains[1])
        + first_norm
        + normalized(laurel_back, gains[2])
    ) * ROOT_HALF
    second_low = normalized(mid_stream, gains[3]).astype(jnp.bfloat16)
    rank_gate = select * against(second_low, gate_shrink)
    rank_up = select * against(second_low, up_shrink)
    gate_proj = product(second_low, full_gate) + precise(rank_gate, gate_expand)
    up_proj = product(second_low, full_up) + precise(rank_up, up_expand)
    hidden_low = glu_form(gate_proj, up_proj).astype(jnp.bfloat16)
    rank_down = select * against(hidden_low, down_shrink)
    ffn_total = lax.psum(
        (product(hidden_low, full_down) + precise(rank_down, down_expand)).astype(jnp.bfloat16),
        "wt",
    ).astype(jnp.float32)
    after_ffn = mid_stream + normalized(ffn_total, gains[4])
    layer_pre = product(after_ffn.astype(jnp.bfloat16), layer_gate)
    layer_wide = layer_input.astype(jnp.float32)
    gated_low = glu_form(layer_pre, layer_wide).astype(jnp.bfloat16)
    layer_back = product(gated_low, layer_lift)
    result = after_ffn + normalized(layer_back, gains[5])
    upstream = out_grad.astype(jnp.float32)
    grad_layer_back = norm_pull(layer_back, gains[5], upstream).astype(jnp.bfloat16)
    grad_gated = against(grad_layer_back, layer_lift)
    grad_pre, layer_input_grad = jax.vjp(glu_form, layer_pre, layer_wide)[1](grad_gated)
    grad_after = upstream + against(grad_pre.astype(jnp.bfloat16), layer_gate)
    grad_ffn = norm_pull(ffn_total, gains[4], grad_after).astype(jnp.bfloat16)
    grad_rank_down = select * against(grad_ffn, down_expand)
    down_expand_grad = precise(rank_down.T, grad_ffn)
    down_shrink_grad = precise(grad_rank_down.T, hidden_low)
    grad_hidden = against(grad_ffn, lax.all_gather(down_weight, "ctx", axis=1, tiled=True))
    grad_hidden = grad_hidden + precise(grad_rank_down, down_shrink)
    grad_gate, grad_up = jax.vjp(glu_form, gate_proj, up_proj)[1](grad_hidden)
    grad_gate = grad_gate.astype(jnp.bfloat16)
    grad_up = grad_up.astype(jnp.bfloat16)
    gate_expand_grad = precise(rank_gate.T, grad_gate)
    up_expand_grad = precise(rank_up.T, grad_up)
    grad_rank_gate = select * against(grad_gate, gate_expand)
    grad_rank_up = select * against(grad_up, up_expand)
    gate_shrink_grad = precise(grad_rank_gate.T, second_low)
    up_shrink_grad = precise(grad_rank_up.T, second_low)
    shard_pieces = lax.all_gather((gate_weight, up_weight), "ctx", axis=0, tiled=True)
    ffn_input_part = against(grad_gate, shard_pieces[0]) + against(grad_up, shard_pieces[1])
    ffn_input_part = (
        ffn_input_part + precise(grad_rank_gate, gate_shrink) + precise(grad_rank_up, up_shrink)
    )
    grad_second = lax.psum(ffn_input_part.astype(jnp.bfloat16), "wt").astype(jnp.float32)
    grad_mid = grad_after + norm_pull(mid_stream, gains[3], grad_second)
    grad_scaled = grad_mid * ROOT_HALF
    grad_attn = norm_pull(attn_total, gains[1], grad_scaled).astype(jnp.bfloat16)
    grad_laurel_back = norm_pull(laurel_back, gains[2], grad_scaled).astype(jnp.bfloat16)
    grad_laurel_rank = against(grad_laurel_back, laurel_right).astype(jnp.bfloat16)
    grad_first = grad_scaled + against(grad_laurel_rank, laurel_left)
    out_expand_grad = precise(rank_out.T, grad_attn)
    grad_rank_out = select * against(grad_attn, out_expand)
    out_shrink_grad = precise(grad_rank_out.T, heads_low)
    grad_heads = against(grad_attn, lax.all_gather(out_weight, "ctx", axis=1, tiled=True))
    grad_heads = (grad_heads + precise(grad_rank_out, out_shrink)).astype(jnp.bfloat16)
    grad_heads_grouped = grad_heads.reshape(
        step_count, per_step, block_len, kv_local, group_portion, head_dim
    )

    def attend_back(members):
        query_part, key_part, value_part, allow_part, log_part, grad_part = members
        scores = scores_of(query_part, key_part, allow_part)
        chances = jnp.exp(scores - log_part)
        chances_low = chances.astype(jnp.bfloat16)
        grad_chances = jnp.einsum(
            "pqgsd,pkgd->pgsqk", grad_part, value_part, preferred_element_type=jnp.float32
        )
        inner = jnp.sum(chances * grad_chances, axis=-1, keepdims=True)
        grad_scores = (chances * (grad_chances - inner)).astype(jnp.bfloat16)
        grad_query = jnp.einsum(
            "pgsqk,pkgd->pqgsd", grad_scores, key_part, preferred_element_type=jnp.float32
        )
        grad_key = jnp.einsum(
            "pgsqk,pqgsd->pkgd", grad_scores, query_part, preferred_element_type=jnp.float32
        )
        grad_value = jnp.einsum(
            "pgsqk,pqgsd->pkgd", chances_low, grad_part, preferred_element_type=jnp.float32
        )
        return (grad_query, grad_key, grad_value)

    grad_queries, grad_keys, grad_values = lax.map(
        attend_back,
        (
            query_grouped,
            keys_grouped,
            values_grouped,
            allowed_grouped,
            log_total,
            grad_heads_grouped,
        ),
    )

    def spread_out(grads):
        empty = jnp.zeros((count_ctx, groups, block_len, kv_width), jnp.float32)
        placed = empty.at[key_device, group_ids[:, None], key_offset].set(
            grads.reshape(groups, keys_len, kv_width)
        )
        return placed.reshape(count_ctx * local_rows, kv_width)

    grad_key_own, grad_value_own = (
        lax.psum_scatter(spread_out(grad_keys), "ctx", scatter_dimension=0, tiled=True),
        lax.psum_scatter(spread_out(grad_values), "ctx", scatter_dimension=0, tiled=True),
    )
    grad_query_proj = jax.vjp(query_piece, query_proj)[1](
        grad_queries.reshape(local_rows, -1, head_dim)
    )[0].astype(jnp.bfloat16)
    grad_key_proj = jax.vjp(key_piece, key_projected)[1](grad_key_own)[0].astype(jnp.bfloat16)
    grad_value_proj = jax.vjp(value_piece, value_projected)[1](grad_value_own)[0].astype(
        jnp.bfloat16
    )
    query_expand_grad = precise(rank_query.T, grad_query_proj)
    key_expand_grad = precise(rank_key.T, grad_key_proj)
    value_expand_grad = precise(rank_value.T, grad_value_proj)
    grad_rank_query = select * against(grad_query_proj, query_expand)
    grad_rank_key = select * against(grad_key_proj, key_widen_maps)
    grad_rank_value = select * against(grad_value_proj, value_widen_maps)
    query_shrink_grad = precise(grad_rank_query.T, first_low)
    key_shrink_grad = precise(grad_rank_key.T, first_low)
    value_shrink_grad = precise(grad_rank_value.T, first_low)
    shard_pieces = lax.all_gather(
        (query_weight, key_matrix, value_matrix), "ctx", axis=0, tiled=True
    )
    attn_input_part = (
        against(grad_query_proj, shard_pieces[0])
        + against(grad_key_proj, shard_pieces[1])
        + against(grad_value_proj, shard_pieces[2])
    )
    attn_input_part = (
        attn_input_part
        + precise(grad_rank_query, query_shrink)
        + precise(grad_rank_key, key_shrink)
        + precise(grad_rank_value, value_shrink)
    )
    grad_first = grad_first + lax.psum(attn_input_part.astype(jnp.bfloat16), "wt").astype(
        jnp.float32
    )
    input_grad = grad_scaled + norm_pull(tokens_wide, gains[0], grad_first)
    split_grads = (
        lax.psum_scatter(query_expand_grad, "ctx", scatter_dimension=0, tiled=True),
        lax.psum_scatter(key_expand_grad, "ctx", scatter_dimension=0, tiled=True),
        lax.psum_scatter(value_expand_grad, "ctx", scatter_dimension=0, tiled=True),
        lax.psum_scatter(gate_expand_grad, "ctx", scatter_dimension=0, tiled=True),
        lax.psum_scatter(up_expand_grad, "ctx", scatter_dimension=0, tiled=True),
        lax.psum_scatter(out_shrink_grad, "ctx", scatter_dimension=0, tiled=True),
        lax.psum_scatter(down_shrink_grad, "ctx", scatter_dimension=0, tiled=True),
    )
    shared_grads = (
        lax.psum_scatter(query_shrink_grad, ("ctx", "wt"), scatter_dimension=0, tiled=True),
        lax.psum_scatter(key_shrink_grad, ("ctx", "wt"), scatter_dimension=0, tiled=True),
        lax.psum_scatter(value_shrink_grad, ("ctx", "wt"), scatter_dimension=0, tiled=True),
        lax.psum_scatter(gate_shrink_grad, ("ctx", "wt"), scatter_dimension=0, tiled=True),
        lax.psum_scatter(up_shrink_grad, ("ctx", "wt"), scatter_dimension=0, tiled=True),
        lax.psum_scatter(out_expand_grad, ("ctx", "wt"), scatter_dimension=0, tiled=True),
        lax.psum_scatter(down_expand_grad, ("ctx", "wt"), scatter_dimension=0, tiled=True),
    )
    return (
        result.astype(jnp.bfloat16),
        input_grad,
        layer_input_grad,
        shared_grads[0],
        shared_grads[1],
        shared_grads[2],
        shared_grads[3],
        shared_grads[4],
        split_grads[5],
        split_grads[6],
        split_grads[0],
        split_grads[1],
        split_grads[2],
        split_grads[3],
        split_grads[4],
        shared_grads[5],
        shared_grads[6],
    )


def solution(mesh):
    in_specs = (
        P("ctx", None),
        P("ctx", None),
        P("ctx", None),
        P(),
        P(),
        P(),
        P(),
        P("ctx", "wt"),
        P("ctx", "wt"),
        P("ctx", "wt"),
        P("ctx", "wt"),
        P("ctx", "wt"),
        P("wt", "ctx"),
        P("wt", "ctx"),
        P(),
        P(),
        P(),
        P(),
        P(),
        P(),
        P(),
        P(),
        P(),
        P(None, "wt"),
        P(None, "wt"),
        P(None, "wt"),
        P(None, "wt"),
        P(None, "wt"),
        P(None, "wt"),
        P(None, "wt"),
        P(),
        P(),
    )
    out_specs = (
        P("ctx", None),
        P("ctx", None),
        P("ctx", None),
        P(("ctx", "wt"), None),
        P(("ctx", "wt"), None),
        P(("ctx", "wt"), None),
        P(("ctx", "wt"), None),
        P(("ctx", "wt"), None),
        P("ctx", "wt"),
        P("ctx", "wt"),
        P("ctx", "wt"),
        P("ctx", "wt"),
        P("ctx", "wt"),
        P("ctx", "wt"),
        P("ctx", "wt"),
        P(("ctx", "wt"), None),
        P(("ctx", "wt"), None),
    )
    return jax.shard_map(local, mesh=mesh, in_specs=in_specs, out_specs=out_specs, check_vma=False)
```

profile of v0, /device:TPU:16, one launch (start us, length us, event | category | flops | bytes accessed | tf_op | source)
XLA Modules:
  0.0 2196.2 jit_solution(6704266606662887971)
XLA Ops:
  24.5 41.0 %all-gather.15.cloned.1.call-done = bf16[2048,256]{1,0:T(8,128)(2,1)} async-done(((bf16[128,256]{1,0:T(8,128)(2,1)}), bf16[2048,256]{1,0:T(8,128)(2,1)}) %all-gather.15.cloned.1.call-update) | async-done | bytes 1048592 | tf_op jit(solution)/shard_map/all_gather | solution.py:160
  70.5 51.9 %all-gather.11.cloned.1.call-done = bf16[2048,256]{1,0:T(8,128)(2,1)} async-done(((bf16[128,256]{1,0:T(8,128)(2,1)}), bf16[2048,256]{1,0:T(8,128)(2,1)}) %all-gather.11.cloned.1.call-update) | async-done | bytes 1048592 | tf_op jit(solution)/shard_map/all_gather | solution.py:161
  151.1 37.7 %all-gather.27.cloned.1.call-done = bf16[4096,1,256]{0,2,1:T(8,128)(2,1)} async-done(((bf16[256,1,256]{0,2,1:T(8,128)(2,1)}), bf16[4096,1,256]{0,2,1:T(8,128)(2,1)}) %all-gather.27.cloned.1.call-update) | async-done | bytes 2097168 | tf_op jit(solution)/shard_map/all_gather | solution.py:181
  192.9 27.7 %gather_fusion.1 = bf16[2304,256]{1,0:T(8,128)(2,1)} fusion(bf16[16,1,256,256]{3,2,1,0:T(8,128)(2,1)} %bitcast.275, s32[2304]{0:T(1024)S(1)} %fusion.130), kind=kCustom, calls=%fused_computation.1 | custom fusion | bytes 2386944 | tf_op jit(solution)/shard_map/gather | solution.py:187
  220.6 35.0 %all-gather.13.cloned.1.call-done = bf16[4096,256]{0,1:T(8,128)(2,1)} async-done(((bf16[256,256]{0,1:T(8,128)(2,1)}), bf16[4096,256]{0,1:T(8,128)(2,1)}) %all-gather.13.cloned.1.call-update) | async-done | bytes 2097168 | tf_op jit(solution)/shard_map/all_gather | solution.py:182
  259.6 27.8 %gather_fusion = bf16[2304,256]{1,0:T(8,128)(2,1)} fusion(bf16[16,1,256,256]{3,2,1,0:T(8,128)(2,1)} %bitcast.274, s32[2304]{0:T(1024)S(1)} %fusion.130), kind=kCustom, calls=%fused_computation | custom fusion | bytes 2386944 | tf_op jit(solution)/shard_map/gather | solution.py:187
  287.5 47.2 %all-gather.17.cloned.1.call-done = bf16[2048,1024]{1,0:T(8,128)(2,1)} async-done(((bf16[128,1024]{1,0:T(8,128)(2,1)}), bf16[2048,1024]{1,0:T(8,128)(2,1)}) %all-gather.17.cloned.1.call-update) | async-done | bytes 4194320 | tf_op jit(solution)/shard_map/all_gather | solution.py:159
  362.8 62.0 %all-gather.19.cloned.1.call-done = bf16[1024,2048]{1,0:T(8,128)(2,1)} async-done(((bf16[1024,128]{1,0:T(8,128)(2,1)}), bf16[1024,2048]{1,0:T(8,128)(2,1)}) %all-gather.19.cloned.1.call-update) | async-done | bytes 4194320 | tf_op jit(solution)/shard_map/all_gather | solution.py:166
  435.7 15.8 all-reduce.18.cloned.1.call-done
  459.3 187.0 %all-gather.21.cloned.1.call-done = bf16[2048,4096]{1,0:T(8,128)(2,1)} async-done(((bf16[128,4096]{1,0:T(8,128)(2,1)}), bf16[2048,4096]{1,0:T(8,128)(2,1)}) %all-gather.21.cloned.1.call-update) | async-done | bytes 16777232 | tf_op jit(solution)/shard_map/all_gather | solution.py:162
  646.3 8.8 fusion.191
  659.1 180.2 %all-gather.23.cloned.1.call-done = bf16[2048,4096]{1,0:T(8,128)(2,1)} async-done(((bf16[128,4096]{1,0:T(8,128)(2,1)}), bf16[2048,4096]{1,0:T(8,128)(2,1)}) %all-gather.23.cloned.1.call-update) | async-done | bytes 16777232 | tf_op jit(solution)/shard_map/all_gather | solution.py:163
  855.2 234.8 %all-gather.25.cloned.1.call-done = bf16[4096,2048]{1,0:T(8,128)(2,1)} async-done(((bf16[4096,128]{1,0:T(8,128)(2,1)}), bf16[4096,2048]{1,0:T(8,128)(2,1)}) %all-gather.25.cloned.1.call-update) | async-done | bytes 16777232 | tf_op jit(solution)/shard_map/all_gather | solution.py:167
  1101.2 18.9 all-reduce.20.cloned.1.call-done
  1132.1 12.7 fusion.194
  1144.9 8.8 multiply_convert_fusion
  1157.7 12.3 fusion.195
  1170.0 12.9 convolution_add_fusion.14
  1188.4 20.3 all-reduce.22.cloned.1.call-done
  1233.0 15.6 scatter_custom_fusion.1
  1262.1 10.9 fusion.9
  1281.3 15.6 scatter_custom_fusion
  1319.8 29.0 %reduce-scatter.12.cloned.1.call-done = f32[256,256]{0,1:T(8,128)} async-done(((f32[4096,256]{0,1:T(8,128)}), f32[256,256]{0,1:T(8,128)}) %reduce-scatter.12.cloned.1.call-update) | async-done | bytes 262160 | tf_op jit(solution)/shard_map/reduce_scatter | solution.py:332
  1351.7 94.1 %reduce-scatter.10.cloned.1.call-done = f32[256,256]{0,1:T(8,128)} async-done(((f32[4096,256]{0,1:T(8,128)}), f32[256,256]{0,1:T(8,128)}) %reduce-scatter.10.cloned.1.call-update) | async-done | bytes 262160 | tf_op jit(solution)/shard_map/reduce_scatter | solution.py:331
  1494.4 159.8 %all-reduce.26.cloned.1.call-done = (f32[128,2048]{1,0:T(8,128)}, f32[128,2048]{1,0:T(8,128)}, f32[128,2048]{1,0:T(8,128)}, f32[128,2048]{1,0:T(8,128)}, f32[128...) async-done(((f32[128,2048]{1,0:T(8,128)}, f32[128,2048]{1,0:T(8,128)}, f32[128,2048]{1,0:T(8,128)}, f32[128,2048]{1,0:T(8,128)}, f32[128,2048]{1,0:T(8,128)}, ...) | async-done | bytes 7340048
  1664.4 57.6 %reduce-scatter.14.cloned.1.call-done = f32[8,1024]{1,0:T(8,128)} async-done(((f32[128,1024]{1,0:T(8,128)}), f32[8,1024]{1,0:T(8,128)}) %reduce-scatter.14.cloned.1.call-update) | async-done | bytes 32784 | tf_op jit(solution)/shard_map/reduce_scatter | solution.py:374
  1722.0 75.7 %reduce-scatter.18.cloned.1.call-done = f32[8,1024]{1,0:T(8,128)} async-done(((f32[128,1024]{1,0:T(8,128)}), f32[8,1024]{1,0:T(8,128)}) %reduce-scatter.18.cloned.1.call-update) | async-done | bytes 32784 | tf_op jit(solution)/shard_map/reduce_scatter | solution.py:369
  1797.7 81.0 %reduce-scatter.16.cloned.1.call-done = f32[8,4096]{1,0:T(8,128)} async-done(((f32[128,4096]{1,0:T(8,128)}), f32[8,4096]{1,0:T(8,128)}) %reduce-scatter.16.cloned.1.call-update) | async-done | bytes 131088 | tf_op jit(solution)/shard_map/reduce_scatter | solution.py:375
  1878.7 81.2 %reduce-scatter.26.cloned.1.call-done = f32[8,4096]{1,0:T(8,128)} async-done(((f32[128,4096]{1,0:T(8,128)}), f32[8,4096]{1,0:T(8,128)}) %reduce-scatter.26.cloned.1.call-update) | async-done | bytes 131088 | tf_op jit(solution)/shard_map/reduce_scatter | solution.py:373
  1959.9 80.5 %reduce-scatter.24.cloned.1.call-done = f32[8,4096]{1,0:T(8,128)} async-done(((f32[128,4096]{1,0:T(8,128)}), f32[8,4096]{1,0:T(8,128)}) %reduce-scatter.24.cloned.1.call-update) | async-done | bytes 131088 | tf_op jit(solution)/shard_map/reduce_scatter | solution.py:372
  2040.5 73.9 %reduce-scatter.22.cloned.1.call-done = f32[8,256]{1,0:T(8,128)} async-done(((f32[128,256]{1,0:T(8,128)}), f32[8,256]{1,0:T(8,128)}) %reduce-scatter.22.cloned.1.call-update) | async-done | bytes 8208 | tf_op jit(solution)/shard_map/reduce_scatter | solution.py:371
  2114.4 75.1 %reduce-scatter.20.cloned.1.call-done = f32[8,256]{1,0:T(8,128)} async-done(((f32[128,256]{1,0:T(8,128)}), f32[8,256]{1,0:T(8,128)}) %reduce-scatter.20.cloned.1.call-update) | async-done | bytes 8208 | tf_op jit(solution)/shard_map/reduce_scatter | solution.py:370
  (511 shorter events, 281.1 us)
Async XLA Ops:
  7.2 846.7 %copy-start = (bf16[128,4096]{1,0:T(8,128)(2,1)S(1)}, bf16[128,4096]{1,0:T(8,128)(2,1)}, u32[]{:S(2)}) copy-start(bf16[128,4096]{1,0:T(8,128)(2,1)} %param.56) | copy-start | bytes 3145732
  7.2 58.3 %all-gather.15.cloned.1.call-start = ((), (), s32[]{:S(2)}) async-start(), calls=%async_computation.11 | async-start | bytes 1114112 | tf_op jit(solution)/shard_map/all_gather | solution.py:160
  8.0 114.4 %all-gather.11.cloned.1.call-start = ((), (), s32[]{:S(2)}) async-start(), calls=%async_computation.9 | async-start | bytes 1114112 | tf_op jit(solution)/shard_map/all_gather | solution.py:161
  8.7 180.2 %all-gather.27.cloned.1.call-start = ((), (), s32[]{:S(2)}) async-start(), calls=%async_computation.30 | async-start | bytes 2228224 | tf_op jit(solution)/shard_map/all_gather | solution.py:181
  12.9 440.6 %copy-start.94 = (f32[256]{0:T(256)}, f32[256]{0:T(256)S(1)}, u32[]{:S(2)}) copy-start(f32[256]{0:T(256)S(1)} %fusion.138) | copy-start | bytes 3076
  22.6 430.9 %copy-start.90 = (f32[1,2048]{1,0:T(1,128)}, f32[1,2048]{1,0:T(1,128)S(1)}, u32[]{:S(2)}) copy-start(f32[1,2048]{1,0:T(1,128)S(1)} %get-tuple-element.112) | copy-start | bytes 24580
  22.6 430.9 %copy-start.92 = (f32[1,2048]{1,0:T(1,128)}, f32[1,2048]{1,0:T(1,128)S(1)}, u32[]{:S(2)}) copy-start(f32[1,2048]{1,0:T(1,128)S(1)} %get-tuple-element.111) | copy-start | bytes 24580
  69.9 185.7 %all-gather.13.cloned.1.call-start = ((), (), s32[]{:S(2)}) async-start(), calls=%async_computation.10 | async-start | bytes 2228224 | tf_op jit(solution)/shard_map/all_gather | solution.py:182
  126.0 208.7 %all-gather.17.cloned.1.call-start = ((), (), s32[]{:S(2)}) async-start(), calls=%async_computation.12 | async-start | bytes 4456448 | tf_op jit(solution)/shard_map/all_gather | solution.py:159
  126.6 298.1 %all-gather.19.cloned.1.call-start = ((), (), s32[]{:S(2)}) async-start(), calls=%async_computation.13 | async-start | bytes 4456448 | tf_op jit(solution)/shard_map/all_gather | solution.py:166
  127.2 324.3 %all-reduce.18.cloned.1.call-start = ((), (), s32[]{:S(2)}) async-start(), calls=%async_computation.14 | async-start | bytes 4194304 | tf_op jit(solution)/shard_map/psum | solution.py:223
  148.3 199.8 %copy-start.48 = (f32[256,128]{0,1:T(8,128)}, f32[256,128]{0,1:T(8,128)S(1)}, u32[]{:S(2)}) copy-start(f32[256,128]{0,1:T(8,128)S(1)} %get-tuple-element.116) | copy-start | bytes 393220
  148.3 199.8 %copy-start.50 = (f32[256,128]{0,1:T(8,128)}, f32[256,128]{0,1:T(8,128)S(1)}, u32[]{:S(2)}) copy-start(f32[256,128]{0,1:T(8,128)S(1)} %get-tuple-element.117) | copy-start | bytes 393220
  148.8 189.4 %copy-start.75 = (f32[256,128]{1,0:T(8,128)}, f32[256,128]{1,0:T(8,128)S(1)}, u32[]{:S(2)}) copy-start(f32[256,128]{1,0:T(8,128)S(1)} %convolution_select_fusion.11) | copy-start | bytes 393220
  430.8 215.5 %all-gather.21.cloned.1.call-start = ((), (), s32[]{:S(2)}) async-start(), calls=%async_computation.15 | async-start | bytes 17825792 | tf_op jit(solution)/shard_map/all_gather | solution.py:162
  431.5 407.8 %all-gather.23.cloned.1.call-start = ((), (), s32[]{:S(2)}) async-start(), calls=%async_computation.16 | async-start | bytes 17825792 | tf_op jit(solution)/shard_map/all_gather | solution.py:163
  432.3 657.8 %all-gather.25.cloned.1.call-start = ((), (), s32[]{:S(2)}) async-start(), calls=%async_computation.17 | async-start | bytes 17825792 | tf_op jit(solution)/shard_map/all_gather | solution.py:167
  432.8 687.3 %all-reduce.20.cloned.1.call-start = ((), (), s32[]{:S(2)}) async-start(), calls=%async_computation.18 | async-start | bytes 2097152 | tf_op jit(solution)/shard_map/psum | solution.py:239
  1101.0 107.6 %all-reduce.22.cloned.1.call-start = ((), (), s32[]{:S(2)}) async-start(), calls=%async_computation.19 | async-start | bytes 2097152 | tf_op jit(solution)/shard_map/psum | solution.py:274
  1187.7 161.1 %reduce-scatter.12.cloned.1.call-start = ((), (), s32[]{:S(2)}) async-start(), calls=%async_computation.21 | async-start | bytes 4456448 | tf_op jit(solution)/shard_map/reduce_scatter | solution.py:332
  1254.3 191.5 %reduce-scatter.10.cloned.1.call-start = ((), (), s32[]{:S(2)}) async-start(), calls=%async_computation.20 | async-start | bytes 4456448 | tf_op jit(solution)/shard_map/reduce_scatter | solution.py:331
  1302.7 180.4 %all-reduce.24.cloned.1.call-start = ((), (), s32[]{:S(2)}) async-start(), calls=%async_computation.22 | async-start | bytes 2097152 | tf_op jit(solution)/shard_map/psum | solution.py:364
  1317.1 133.8 %copy-start.54 = (f32[256,128]{1,0:T(8,128)}, f32[256,128]{1,0:T(8,128)S(1)}, u32[]{:S(2)}) copy-start(f32[256,128]{1,0:T(8,128)S(1)} %convolution_select_fusion) | copy-start | bytes 393220
  1455.6 198.5 %all-reduce.26.cloned.1.call-start = ((), (), s32[]{:S(2)}) async-start(), calls=%async_computation.31 | async-start | bytes 14680064
  1463.9 258.1 %reduce-scatter.14.cloned.1.call-start = ((), (), s32[]{:S(2)}) async-start(), calls=%async_computation.23 | async-start | bytes 557056 | tf_op jit(solution)/shard_map/reduce_scatter | solution.py:374
  1466.4 331.2 %reduce-scatter.18.cloned.1.call-start = ((), (), s32[]{:S(2)}) async-start(), calls=%async_computation.25 | async-start | bytes 557056 | tf_op jit(solution)/shard_map/reduce_scatter | solution.py:369
  1468.0 410.7 %reduce-scatter.16.cloned.1.call-start = ((), (), s32[]{:S(2)}) async-start(), calls=%async_computation.24 | async-start | bytes 2228224 | tf_op jit(solution)/shard_map/reduce_scatter | solution.py:375
  1472.0 487.9 %reduce-scatter.26.cloned.1.call-start = ((), (), s32[]{:S(2)}) async-start(), calls=%async_computation.29 | async-start | bytes 2228224 | tf_op jit(solution)/shard_map/reduce_scatter | solution.py:373
  1476.1 564.3 %reduce-scatter.24.cloned.1.call-start = ((), (), s32[]{:S(2)}) async-start(), calls=%async_computation.28 | async-start | bytes 2228224 | tf_op jit(solution)/shard_map/reduce_scatter | solution.py:372
  1480.2 634.1 %reduce-scatter.22.cloned.1.call-start = ((), (), s32[]{:S(2)}) async-start(), calls=%async_computation.27 | async-start | bytes 139264 | tf_op jit(solution)/shard_map/reduce_scatter | solution.py:371
  1482.0 707.4 %reduce-scatter.20.cloned.1.call-start = ((), (), s32[]{:S(2)}) async-start(), calls=%async_computation.26 | async-start | bytes 139264 | tf_op jit(solution)/shard_map/reduce_scatter | solution.py:370
  1489.2 700.2 %copy-start.1 = (bf16[128,4096]{1,0:T(8,128)(2,1)S(1)}, bf16[128,4096]{1,0:T(8,128)(2,1)}, u32[]{:S(2)}) copy-start(bf16[128,4096]{1,0:T(8,128)(2,1)} %param.56) | copy-start | bytes 3145732
  (138 other events, 2687.7 us)
Sparse Core Ops, SparseCore 0:
  10.8 54.6 all-gather.14
  68.2 54.0 all-gather.10
  125.7 63.1 all-gather.26
  192.0 63.5 all-gather.12
  258.2 76.4 all-gather.16
  337.3 87.3 all-gather.18
  430.9 20.5 all-reduce.17
  454.6 191.6 all-gather.20
  649.5 189.7 all-gather.22
  842.2 247.8 all-gather.24
  1101.1 18.9 all-reduce.19
  1187.8 20.7 all-reduce.21
  1254.4 94.2 reduce-scatter.11
  1351.0 94.7 reduce-scatter.9
  1455.7 21.1 all-reduce.23
  1483.2 170.8 all-reduce.25
  1656.8 65.1 reduce-scatter.13
  1724.7 72.9 reduce-scatter.17
  1800.5 78.1 reduce-scatter.15
  1881.4 78.4 reduce-scatter.25
  1962.8 77.6 reduce-scatter.23
  2043.3 71.0 reduce-scatter.21
  2117.3 72.1 reduce-scatter.19
where the time goes:
time: 2220 us; the launch traced here: 2200 us
  waiting for transfers between devices  1740 us (78%)
  matrix products  201 us (9%)
  local copies, waits for them, and re-layouts  158 us (7%)
  other arithmetic  68 us (3%)
  between operations  22.2 us (1%)
    all_gather x1, waiting for transfers between devices, local(): lax.all_gather(down_weight, 'ctx', axis=1, tiled=True)  235 us
    all_gather x1, waiting for transfers between devices, local(): lax.all_gather(gate_weight, 'ctx', axis=0, tiled=True)  187 us
    all_gather x1, waiting for transfers between devices, local(): lax.all_gather(up_weight, 'ctx', axis=0, tiled=True)  180 us
    unnamed x24, waiting for transfers between devices  164 us
    reduce_scatter x1, waiting for transfers between devices, local(): lax.psum_scatter(spread_out(grad_keys), 'ctx', scatter_dimension=0, tiled...  94.1 us
    reduce_scatter x1, waiting for transfers between devices, local(): lax.psum_scatter(up_expand_grad, 'ctx', scatter_dimension=0, tiled=True)  81.2 us
    reduce_scatter x1, waiting for transfers between devices, local(): lax.psum_scatter(down_shrink_grad, 'ctx', scatter_dimension=0, tiled=True)  81 us
    reduce_scatter x1, waiting for transfers between devices, local(): lax.psum_scatter(gate_expand_grad, 'ctx', scatter_dimension=0, tiled=True)  80.5 us
  transfers between devices with their start and end apart: 23, of which 22 were waited for; matrix products, arithmetic and copies ran while one was open for 13% of the time, Pallas kernels for 0%

commit v1 on v0

v1 whole, which is shorter than its diff:
```python
import jax
import jax.numpy as jnp
from jax import lax
from jax.experimental import pallas as pl
from jax.experimental.pallas import tpu as pltpu
from jax.sharding import PartitionSpec as P

QUERY_HEADS = 8
KEY_VALUE_HEADS = 2
ADAPTER_COUNT = 8
ADAPTER_RANK = 16
PROMPT = 2048
CONT = 256

EPS = 1e-06
THETA = 1000000.0
ROOT_HALF = 0.5**0.5
F32 = jnp.float32
BF16 = jnp.bfloat16
SWAP = [(0, 1), (1, 0)]


def normalized(inputs, norm_gain):
    return inputs * lax.rsqrt(jnp.mean(inputs * inputs, axis=-1, keepdims=True) + EPS) * norm_gain


def norm_pull(inputs, norm_gain, upstream):
    return jax.vjp(lambda inner: normalized(inner, norm_gain), inputs)[1](upstream)[0]


def rotary_applied(inputs, cosine, sine_term):
    half_width = inputs.shape[-1] // 2
    first_half = inputs[..., :half_width]
    second_half = inputs[..., half_width:]
    return jnp.concatenate(
        [
            first_half * cosine - second_half * sine_term,
            second_half * cosine + first_half * sine_term,
        ],
        axis=-1,
    )


def glu_form(gate_in, up_in):
    return jax.nn.gelu(gate_in, approximate=True) * up_in


def product(left_side, right_side):
    return jnp.dot(left_side, right_side, preferred_element_type=F32)


def against(left_side, right_side):
    return lax.dot_general(
        left_side, right_side, (((1,), (1,)), ((), ())), preferred_element_type=F32
    )


def summed(left_side, right_side):
    return lax.dot_general(
        left_side, right_side, (((0,), (0,)), ((), ())), preferred_element_type=F32
    )


def low(value):
    return value.astype(BF16)


def attend_kernel(count_ref, kslot_ref, vslot_ref, q_ref, k_ref, v_ref, o_ref, lse_ref, acc, tot, *, heads, dim):
    group = pl.program_id(0)
    count = count_ref[group]
    rows = q_ref.shape[0]
    fold = tot.shape[-1]
    acc[...] = jnp.zeros_like(acc)
    tot[...] = jnp.zeros_like(tot)

    def step(index, masked):
        keys = k_ref[kslot_ref[group, index], 0]
        values = v_ref[vslot_ref[group, index], 0]
        for head in range(heads):
            lanes = slice(head * dim, (head + 1) * dim)
            scores = against(q_ref[:, lanes], keys)
            weights = jnp.exp(scores)
            if masked:
                row = lax.broadcasted_iota(jnp.int32, scores.shape, 0)
                col = lax.broadcasted_iota(jnp.int32, scores.shape, 1)
                weights = jnp.where(col <= row, weights, 0.0)
            part = weights[:, :fold]
            for start in range(fold, rows, fold):
                part = part + weights[:, start : start + fold]
            tot[head] += part
            acc[:, lanes] += product(low(weights), values)

    def body(index, carry):
        step(index, False)
        return carry

    lax.fori_loop(0, count - 1, body, 0)
    step(count - 1, True)
    lane = lax.broadcasted_iota(jnp.int32, lse_ref.shape, 1)
    lse = jnp.zeros(lse_ref.shape, F32)
    for head in range(heads):
        lanes = slice(head * dim, (head + 1) * dim)
        total = jnp.sum(tot[head], axis=-1, keepdims=True)
        o_ref[:, lanes] = low(acc[:, lanes] / total)
        lse = jnp.where(lane == head, jnp.log(total), lse)
    lse_ref[...] = lse


def attend_back_kernel(
    count_ref, kslot_ref, vslot_ref, dslot_ref, q_ref, k_ref, v_ref, o_ref, lse_ref, g_ref, dq_ref, dkv_ref, delta, *, heads, dim
):
    group = pl.program_id(0)
    count = count_ref[group]
    dq_ref[...] = jnp.zeros_like(dq_ref)
    dkv_ref[...] = jnp.zeros_like(dkv_ref)
    for head in range(heads):
        lanes = slice(head * dim, (head + 1) * dim)
        delta[head] = jnp.sum(
            o_ref[:, lanes].astype(F32) * g_ref[:, lanes].astype(F32), axis=-1, keepdims=True
        )

    def step(index, masked):
        keys = k_ref[kslot_ref[group, index], 0]
        values = v_ref[vslot_ref[group, index], 0]
        slot = dslot_ref[group, index]
        dk = jnp.zeros(keys.shape, F32)
        dv = jnp.zeros(values.shape, F32)
        for head in range(heads):
            lanes = slice(head * dim, (head + 1) * dim)
            queries = q_ref[:, lanes]
            upstream = g_ref[:, lanes]
            scores = against(queries, keys)
            weights = jnp.exp(scores - lse_ref[:, head : head + 1])
            if masked:
                row = lax.broadcasted_iota(jnp.int32, scores.shape, 0)
                col = lax.broadcasted_iota(jnp.int32, scores.shape, 1)
                weights = jnp.where(col <= row, weights, 0.0)
            grad_weights = against(upstream, values)
            grad_scores = low(weights * (grad_weights - delta[head]))
            dq_ref[:, lanes] += product(grad_scores, keys)
            dk += summed(grad_scores, queries)
            dv += summed(low(weights), upstream)
        dkv_ref[slot, 0, :, :dim] = low(dk)
        dkv_ref[slot, 0, :, dim:] = low(dv)

    def body(index, carry):
        step(index, False)
        return carry

    lax.fori_loop(0, count - 1, body, 0)
    step(count - 1, True)


def attend(tables, queries, key_all, value_all, groups, heads, dim):
    count, kslot, vslot = tables
    slots, _, block, _ = key_all.shape
    rows = queries.shape[0]
    fold = min(128, block)
    whole = pl.BlockSpec((slots, 1, block, dim), lambda g, *_: (0, g, 0, 0))
    mine = pl.BlockSpec((block, heads * dim), lambda g, *_: (g, 0))
    return pl.pallas_call(
        lambda *refs: attend_kernel(*refs, heads=heads, dim=dim),
        grid_spec=pltpu.PrefetchScalarGridSpec(
            num_scalar_prefetch=3,
            grid=(groups,),
            in_specs=[mine, whole, whole],
            out_specs=[mine, pl.BlockSpec((block, 128), lambda g, *_: (g, 0))],
            scratch_shapes=[
                pltpu.VMEM((block, heads * dim), F32),
                pltpu.VMEM((heads, block, fold), F32),
            ],
        ),
        out_shape=[
            jax.ShapeDtypeStruct((rows, heads * dim), BF16),
            jax.ShapeDtypeStruct((rows, 128), F32),
        ],
        compiler_params=pltpu.CompilerParams(vmem_limit_bytes=40 * 2**20),
        cost_estimate=pl.CostEstimate(
            flops=4 * rows * heads * dim * 2304, bytes_accessed=6 * 2**20, transcendentals=rows * heads * 2304
        ),
    )(count, kslot, vslot, queries, key_all, value_all)


def attend_back(tables, dslot, queries, key_all, value_all, heads_low, lse, grads, groups, heads, dim):
    count, kslot, vslot = tables
    slots, _, block, _ = key_all.shape
    rows = queries.shape[0]
    whole = pl.BlockSpec((slots, 1, block, dim), lambda g, *_: (0, g, 0, 0))
    mine = pl.BlockSpec((block, heads * dim), lambda g, *_: (g, 0))
    return pl.pallas_call(
        lambda *refs: attend_back_kernel(*refs, heads=heads, dim=dim),
        grid_spec=pltpu.PrefetchScalarGridSpec(
            num_scalar_prefetch=4,
            grid=(groups,),
            in_specs=[mine, whole, whole, mine, pl.BlockSpec((block, 128), lambda g, *_: (g, 0)), mine],
            out_specs=[mine, pl.BlockSpec((slots, 1, block, 2 * dim), lambda g, *_: (0, g, 0, 0))],
            scratch_shapes=[pltpu.VMEM((heads, block, 1), F32)],
        ),
        out_shape=[
            jax.ShapeDtypeStruct((rows, heads * dim), F32),
            jax.ShapeDtypeStruct((slots, groups, block, 2 * dim), BF16),
        ],
        compiler_params=pltpu.CompilerParams(vmem_limit_bytes=48 * 2**20),
        cost_estimate=pl.CostEstimate(
            flops=10 * rows * heads * dim * 2304, bytes_accessed=12 * 2**20, transcendentals=rows * heads * 2304
        ),
    )(count, kslot, vslot, dslot, queries, key_all, value_all, heads_low, lse, grads)


def local(
    tokens,
    layer_input,
    out_grad,
    block_device,
    adapter_pick,
    norm_gains,
    head_norm_gains,
    query_weight,
    key_matrix,
    value_matrix,
    gate_weight,
    up_weight,
    out_weight,
    down_weight,
    laurel_left,
    laurel_right,
    layer_gate,
    layer_lift,
    query_shrink,
    key_shrink,
    value_shrink,
    gate_shrink,
    up_shrink,
    out_shrink,
    down_shrink,
    query_expand,
    key_widen_maps,
    value_widen_maps,
    gate_expand,
    up_expand,
    out_expand,
    down_expand,
):
    count_ctx = lax.axis_size("ctx")
    bit_count = count_ctx.bit_length() - 1
    groups = block_device.shape[0]
    local_rows, width = tokens.shape
    block_len = local_rows // groups
    half_rows = local_rows // 2
    head_dim = head_norm_gains.shape[1]
    heads_local = query_weight.shape[1] // head_dim
    adapter_width = ADAPTER_COUNT * ADAPTER_RANK
    model_block = width // count_ctx
    hidden_slice = gate_weight.shape[1] // 4
    me = lax.axis_index("ctx")
    core = lax.axis_index("wt")

    team_groups = [
        [base + 2 * t for t in range(4)] for base in range(count_ctx) if (base >> 1) & 3 == 0
    ]
    plane_groups = [[base + t for t in range(4)] for base in range(0, count_ctx, 4)]
    column_groups = [[base + 4 * t for t in range(count_ctx // 4)] for base in range(4)]
    spread_bits = list(range(3, bit_count)) + [0]
    team_base = me - 2 * ((me >> 1) & 3)
    team_place = (me >> 1) & 3

    def flip(value, bit):
        return lax.ppermute(value, "ctx", [(i, i ^ (1 << bit)) for i in range(count_ctx)])

    def other_core(value):
        return lax.ppermute(value, "wt", SWAP)

    def own_half(value):
        return lax.dynamic_slice_in_dim(value, core * half_rows, half_rows, 0)

    def other_half(value):
        return lax.dynamic_slice_in_dim(value, (1 - core) * half_rows, half_rows, 0)

    def both_halves(own, other):
        return jnp.where(
            core == 0, jnp.concatenate([own, other], axis=0), jnp.concatenate([other, own], axis=0)
        )

    def column_blocks(value, places):
        return jnp.concatenate(
            [
                lax.dynamic_slice_in_dim(value, place * model_block, model_block, 1)
                for place in places
            ],
            axis=1,
        )

    def stage_mask(position, stages):
        return sum(((position >> i) & 1) << bit for i, bit in enumerate(stages))

    def stage_position(owner, stages):
        return sum((((owner ^ me) >> bit) & 1) << i for i, bit in enumerate(stages))

    def all_stages(first, last):
        return list(range(2, bit_count)) + [first, last]

    weight_stages = all_stages(0, 1)
    weight_order = [me ^ stage_mask(j, weight_stages) for j in range(count_ctx)]
    weight_back = [stage_position(b, weight_stages) for b in range(count_ctx)]
    piece_masks = [0]
    for bit in spread_bits:
        piece_masks = piece_masks + [mask | (1 << bit) for mask in piece_masks]
    team_order = [(team_base ^ mask) + 2 * t for mask in piece_masks for t in range(4)]
    team_back = [
        4 * sum((((b ^ me) >> bit) & 1) << i for i, bit in enumerate(spread_bits)) + ((b >> 1) & 3)
        for b in range(count_ctx)
    ]

    def gather_slabs(shard, stages):
        slab = shard
        for bit in stages[:-1]:
            slab = jnp.concatenate([slab, flip(slab, bit)], axis=0)
        return slab, flip(slab, stages[-1])

    def team_pieces(shard):
        split = shard.reshape(model_block, 4, hidden_slice).transpose(1, 0, 2)
        piece = lax.all_to_all(split, "ctx", 0, 0, axis_index_groups=team_groups, tiled=True)
        pieces = [piece.reshape(4 * model_block, hidden_slice)]
        for bit in spread_bits:
            pieces = pieces + [flip(piece, bit) for piece in pieces]
        return pieces

    prompt_blocks = PROMPT // block_len
    cont_blocks = CONT // block_len
    device_ids = jnp.arange(count_ctx, dtype=jnp.int32)
    block_of = jnp.sum(
        jnp.where(block_device[None] == device_ids[:, None, None], device_ids[None, None, :], 0),
        axis=2,
    )
    cont_of = (block_of - prompt_blocks) // cont_blocks
    pick_of = jnp.sum(
        jnp.where(
            cont_of[:, :, None] == jnp.arange(adapter_pick.shape[1], dtype=jnp.int32),
            adapter_pick[None],
            0,
        ),
        axis=2,
    )
    pick_of = jnp.where(block_of < prompt_blocks, -1, pick_of)

    def picks_at(device):
        return jnp.sum(jnp.where(device_ids[:, None] == device, pick_of, 0), axis=0)

    def select_rows(picks):
        rows = jnp.repeat(picks, block_len)
        return (
            jnp.arange(adapter_width, dtype=jnp.int32)[None, :] // ADAPTER_RANK == rows[:, None]
        ).astype(F32)

    select = select_rows(picks_at(me))
    select_own = own_half(select)
    team_select = [select_rows(picks_at(team_base + 2 * t)) for t in range(4)]
    select_near = jnp.concatenate([own_half(part) for part in team_select], axis=0)
    select_far = jnp.concatenate([other_half(part) for part in team_select], axis=0)

    my_block = jnp.sum(jnp.where(device_ids[:, None] == me, block_of, 0), axis=0)
    positions = (
        my_block[:, None] * block_len + jnp.arange(block_len, dtype=jnp.int32)[None, :]
    ).reshape(-1)
    seq_pos = jnp.where(positions < PROMPT, positions, PROMPT + (positions - PROMPT) % CONT)
    frequency = THETA ** (-2.0 * jnp.arange(head_dim // 2, dtype=F32) / head_dim)
    rotary_angles = seq_pos.astype(F32)[:, None] * frequency[None, :]
    cosine = jnp.cos(rotary_angles)[:, None, :]
    sine_term = jnp.sin(rotary_angles)[:, None, :]
    cont_start = prompt_blocks + (my_block - prompt_blocks) // cont_blocks * cont_blocks
    is_prompt = my_block < prompt_blocks
    visible_count = jnp.where(
        is_prompt, my_block + 1, prompt_blocks + my_block - cont_start + 1
    ).astype(jnp.int32)
    entries = jnp.arange(prompt_blocks + cont_blocks, dtype=jnp.int32)
    visible_block = jnp.where(
        is_prompt[:, None] | (entries < prompt_blocks)[None, :],
        entries[None, :],
        cont_start[:, None] + entries[None, :] - prompt_blocks,
    )
    visible_device = jnp.sum(
        jnp.where(
            visible_block[:, :, None] == device_ids[None, None, :], block_device[:, None, :], 0
        ),
        axis=2,
    )
    key_stages, value_stages = all_stages(0, 1), all_stages(1, 0)
    key_slot = stage_position(visible_device, key_stages).astype(jnp.int32)
    value_slot = stage_position(visible_device, value_stages).astype(jnp.int32)
    grad_slot = (
        (visible_device % 4) * (count_ctx // 4) + visible_device // 4
    ).astype(jnp.int32)
    tables = (visible_count, key_slot, value_slot)

    gains = norm_gains.astype(F32)
    query_gain = head_norm_gains[0].astype(F32)
    key_gain = head_norm_gains[1].astype(F32)

    def query_piece(projected):
        return (
            rotary_applied(
                normalized(projected.reshape(local_rows, -1, head_dim), query_gain),
                cosine,
                sine_term,
            )
            * head_dim ** (-0.5)
        ).reshape(local_rows, -1)

    def key_piece(projected):
        return rotary_applied(
            normalized(projected.reshape(local_rows, -1, head_dim), key_gain), cosine, sine_term
        ).reshape(local_rows, -1)

    def value_piece(projected):
        return normalized(projected.reshape(local_rows, -1, head_dim), 1.0).reshape(local_rows, -1)

    kv_slabs = gather_slabs(jnp.concatenate([key_matrix, value_matrix], axis=1), weight_stages)
    query_slabs = gather_slabs(query_weight, weight_stages)
    out_slabs = gather_slabs(out_weight.T, weight_stages)
    gate_pieces = team_pieces(gate_weight)
    up_pieces = team_pieces(up_weight)
    down_pieces = team_pieces(down_weight.T)

    def slab_product(value, slabs):
        middle = value.shape[1] // 2
        return product(value[:, :middle], slabs[0]) + product(value[:, middle:], slabs[1])

    def slab_against(value, slabs):
        return jnp.concatenate([against(value, slabs[0]), against(value, slabs[1])], axis=1)

    def piece_product(value, pieces):
        rows = pieces[0].shape[0]
        total = product(value[:, :rows], pieces[0])
        for i in range(1, len(pieces)):
            total = total + product(value[:, i * rows : (i + 1) * rows], pieces[i])
        return total

    first_norm = normalized(tokens.astype(F32), gains[0])
    first_low = low(first_norm)
    first_moved = column_blocks(first_low, weight_order)
    rank_query = low(select * against(first_low, query_shrink))
    rank_key = low(select * against(first_low, key_shrink))
    rank_value = low(select * against(first_low, value_shrink))
    kv_projected = slab_product(first_moved, kv_slabs)
    kv_width = key_matrix.shape[1]
    key_projected = kv_projected[:, :kv_width] + product(rank_key, key_widen_maps)
    value_projected = kv_projected[:, kv_width:] + product(rank_value, value_widen_maps)
    key_low = low(key_piece(key_projected))
    value_low = low(value_piece(value_projected))

    def gather_blocks(value, stages):
        slabs = gather_slabs(value.reshape(1, groups, block_len, head_dim), stages)
        return jnp.concatenate(slabs, axis=0)

    key_all = gather_blocks(key_low, key_stages)
    value_all = gather_blocks(value_low, value_stages)
    query_proj = slab_product(first_moved, query_slabs) + product(rank_query, query_expand)
    query_low = low(query_piece(query_proj))
    heads_low, lse = attend(tables, query_low, key_all, value_all, groups, heads_local, head_dim)

    def core_sum(value):
        return own_half(value) + other_core(other_half(value))

    attn_part = jnp.concatenate(
        [slab_against(heads_low, out_slabs), select * against(heads_low, out_shrink)], axis=1
    )
    attn_sum = core_sum(attn_part)
    rank_out = low(attn_sum[:, width:])
    attn_total = column_blocks(attn_sum[:, :width], weight_back) + product(rank_out, out_expand)

    tokens_own = own_half(tokens).astype(F32)
    first_own = normalized(tokens_own, gains[0])
    first_own_low = low(first_own)
    laurel_rank = low(product(first_own_low, laurel_left))
    laurel_back = product(laurel_rank, laurel_right)
    mid_stream = (
        tokens_own + normalized(attn_total, gains[1]) + first_own + normalized(laurel_back, gains[2])
    ) * ROOT_HALF
    second_low = low(normalized(mid_stream, gains[3]))

    def team_gather(value):
        sent = jnp.broadcast_to(value[None], (4,) + value.shape)
        near = lax.all_to_all(sent, "ctx", 0, 0, axis_index_groups=team_groups, tiled=True)
        near = near.reshape(4 * value.shape[0], value.shape[1])
        return near, other_core(near)

    def team_sum(near, far):
        total = low(near + other_core(low(far)).astype(F32))
        total = total.reshape(4, half_rows, total.shape[1])
        parts = lax.all_to_all(total, "ctx", 0, 0, axis_index_groups=team_groups, tiled=True)
        return jnp.sum(parts.astype(F32), axis=0)

    def hidden_columns(value):
        return lax.dynamic_slice_in_dim(value, team_place * hidden_slice, hidden_slice, 1)

    shrink_moved = column_blocks(jnp.concatenate([gate_shrink, up_shrink], axis=0), team_order)
    down_expand_moved = column_blocks(down_expand, team_order)
    gate_expand_slice = hidden_columns(gate_expand)
    up_expand_slice = hidden_columns(up_expand)
    down_shrink_slice = hidden_columns(down_shrink)

    def feed(second_part, select_part):
        ranks = against(second_part, shrink_moved)
        rank_gate = low(select_part * ranks[:, :adapter_width])
        rank_up = low(select_part * ranks[:, adapter_width:])
        gate_proj = piece_product(second_part, gate_pieces) + product(rank_gate, gate_expand_slice)
        up_proj = piece_product(second_part, up_pieces) + product(rank_up, up_expand_slice)
        hidden = low(glu_form(gate_proj, up_proj))
        part = jnp.concatenate(
            [against(hidden, piece) for piece in down_pieces]
            + [select_part * against(hidden, down_shrink_slice)],
            axis=1,
        )
        return rank_gate, rank_up, gate_proj, up_proj, hidden, part

    second_near, second_far = team_gather(column_blocks(second_low, team_order))
    kept_far = feed(second_far, select_far)
    kept_near = feed(second_near, select_near)
    ffn_sum = team_sum(kept_near[-1], kept_far[-1])
    rank_down = low(ffn_sum[:, width:])
    ffn_total = column_blocks(ffn_sum[:, :width], team_back) + product(rank_down, down_expand)
    after_ffn = mid_stream + normalized(ffn_total, gains[4])

    layer_pre = product(low(after_ffn), layer_gate)
    layer_wide = own_half(layer_input).astype(F32)
    gated_low = low(glu_form(layer_pre, layer_wide))
    layer_back = product(gated_low, layer_lift)
    result_own = low(after_ffn + normalized(layer_back, gains[5]))
    upstream = own_half(out_grad).astype(F32)
    grad_layer_back = low(norm_pull(layer_back, gains[5], upstream))
    grad_gated = against(grad_layer_back, layer_lift)
    grad_pre, layer_input_own = jax.vjp(glu_form, layer_pre, layer_wide)[1](grad_gated)
    grad_after = upstream + against(low(grad_pre), layer_gate)
    grad_ffn = low(norm_pull(ffn_total, gains[4], grad_after))
    down_expand_grad = summed(rank_down, grad_ffn)

    def feed_back(grad_part, select_part, kept):
        rank_gate, rank_up, gate_proj, up_proj, hidden, _ = kept
        grad_rank_down = low(select_part * against(grad_part, down_expand_moved))
        grad_hidden = piece_product(grad_part, down_pieces) + product(
            grad_rank_down, down_shrink_slice
        )
        grad_gate, grad_up = jax.vjp(glu_form, gate_proj, up_proj)[1](grad_hidden)
        grad_gate, grad_up = low(grad_gate), low(grad_up)
        part = jnp.concatenate(
            [
                against(grad_gate, gate_piece) + against(grad_up, up_piece)
                for gate_piece, up_piece in zip(gate_pieces, up_pieces)
            ]
            + [
                select_part * against(grad_gate, gate_expand_slice),
                select_part * against(grad_up, up_expand_slice),
            ],
            axis=1,
        )
        return (
            part,
            summed(rank_gate, grad_gate),
            summed(rank_up, grad_up),
            summed(grad_rank_down, hidden),
        )

    grad_near, grad_far = team_gather(column_blocks(grad_ffn, team_order))
    back_far = feed_back(grad_far, select_far, kept_far)
    back_near = feed_back(grad_near, select_near, kept_near)
    gate_expand_grad, up_expand_grad, down_shrink_grad = (
        near + far for near, far in zip(back_near[1:], back_far[1:])
    )
    second_sum = team_sum(back_near[0], back_far[0])
    grad_rank_gate = low(second_sum[:, width : width + adapter_width])
    grad_rank_up = low(second_sum[:, width + adapter_width :])
    grad_second = (
        column_blocks(second_sum[:, :width], team_back)
        + product(grad_rank_gate, gate_shrink)
        + product(grad_rank_up, up_shrink)
    )
    gate_shrink_grad = summed(grad_rank_gate, second_low)
    up_shrink_grad = summed(grad_rank_up, second_low)

    grad_mid = grad_after + norm_pull(mid_stream, gains[3], grad_second)
    grad_scaled = grad_mid * ROOT_HALF
    grad_attn_own = low(norm_pull(attn_total, gains[1], grad_scaled))
    grad_laurel_back = low(norm_pull(laurel_back, gains[2], grad_scaled))
    grad_laurel_rank = low(against(grad_laurel_back, laurel_right))
    grad_first = grad_scaled + against(grad_laurel_rank, laurel_left)
    out_expand_grad = summed(rank_out, grad_attn_own)
    grad_rank_out_own = low(select_own * against(grad_attn_own, out_expand))
    grad_sent = jnp.concatenate(
        [column_blocks(grad_attn_own, weight_order), grad_rank_out_own], axis=1
    )
    grad_joined = both_halves(grad_sent, other_core(grad_sent))
    grad_attn = grad_joined[:, :width]
    grad_rank_out = grad_joined[:, width:]
    out_shrink_grad = summed(grad_rank_out, heads_low)
    grad_heads = low(slab_product(grad_attn, out_slabs) + product(grad_rank_out, out_shrink))

    grad_queries, grad_kv = attend_back(
        tables,
        grad_slot,
        query_low,
        key_all,
        value_all,
        heads_low,
        lse,
        grad_heads,
        groups,
        heads_local,
        head_dim,
    )
    grad_kv = grad_kv.reshape(4, -1, head_dim * 2)
    parts = lax.all_to_all(grad_kv, "ctx", 0, 0, axis_index_groups=plane_groups, tiled=True)
    parts = low(jnp.sum(parts.astype(F32), axis=0)).reshape(count_ctx // 4, local_rows, 2 * head_dim)
    parts = lax.all_to_all(parts, "ctx", 0, 0, axis_index_groups=column_groups, tiled=True)
    grad_kv_own = jnp.sum(parts.astype(F32), axis=0)

    grad_query_proj = low(jax.vjp(query_piece, query_proj)[1](grad_queries)[0])
    grad_key_proj = low(jax.vjp(key_piece, key_projected)[1](grad_kv_own[:, :head_dim])[0])
    grad_value_proj = low(jax.vjp(value_piece, value_projected)[1](grad_kv_own[:, head_dim:])[0])
    query_expand_grad = summed(rank_query, grad_query_proj)
    key_expand_grad = summed(rank_key, grad_key_proj)
    value_expand_grad = summed(rank_value, grad_value_proj)
    grad_kv_proj = jnp.concatenate([grad_key_proj, grad_value_proj], axis=1)
    first_part = jnp.concatenate(
        [
            slab_against(grad_query_proj, query_slabs) + slab_against(grad_kv_proj, kv_slabs),
            select * against(grad_query_proj, query_expand),
            select * against(grad_key_proj, key_widen_maps),
            select * against(grad_value_proj, value_widen_maps),
        ],
        axis=1,
    )
    first_sum = own_half(first_part) + other_core(low(other_half(first_part))).astype(F32)
    grad_rank_query, grad_rank_key, grad_rank_value = (
        low(first_sum[:, width + i * adapter_width : width + (i + 1) * adapter_width])
        for i in range(3)
    )
    grad_first = (
        grad_first
        + column_blocks(first_sum[:, :width], weight_back)
        + product(grad_rank_query, query_shrink)
        + product(grad_rank_key, key_shrink)
        + product(grad_rank_value, value_shrink)
    )
    query_shrink_grad = summed(grad_rank_query, first_own_low)
    key_shrink_grad = summed(grad_rank_key, first_own_low)
    value_shrink_grad = summed(grad_rank_value, first_own_low)
    input_own = grad_scaled + norm_pull(tokens_own, gains[0], grad_first)

    def scatter_split(grads):
        rows = adapter_width // count_ctx
        joined = low(jnp.concatenate(grads, axis=1))
        parts = joined.reshape(count_ctx, rows, joined.shape[1])
        parts = lax.all_to_all(parts, "ctx", 0, 0, tiled=True)
        total = jnp.sum(parts.astype(F32), axis=0)
        cuts, start = [], 0
        for grad in grads:
            cuts.append(total[:, start : start + grad.shape[1]])
            start += grad.shape[1]
        return cuts

    def scatter_team(grads):
        rows = adapter_width // count_ctx
        joined = low(jnp.stack(grads, axis=0)).reshape(len(grads), count_ctx, rows, hidden_slice)
        parts = joined.transpose(1, 0, 2, 3).reshape(count_ctx, len(grads) * rows, hidden_slice)
        parts = lax.all_to_all(parts, "ctx", 0, 0, tiled=True)
        teams = [
            sum(parts[i].astype(F32) for i in range(count_ctx) if (i >> 1) & 3 == t)
            for t in range(4)
        ]
        total = jnp.concatenate(teams, axis=1)
        return [total[i * rows : (i + 1) * rows] for i in range(len(grads))]

    def scatter_shared(grads):
        rows = adapter_width // (2 * count_ctx)
        shaped = jnp.stack(grads, axis=0).reshape(len(grads), count_ctx, 2, rows, width)
        keep = lax.dynamic_index_in_dim(shaped, core, 2, keepdims=False)
        send = lax.dynamic_index_in_dim(shaped, 1 - core, 2, keepdims=False)
        joined = low(keep + other_core(low(send)).astype(F32))
        parts = joined.transpose(1, 0, 2, 3).reshape(count_ctx, len(grads) * rows, width)
        parts = lax.all_to_all(parts, "ctx", 0, 0, tiled=True)
        total = jnp.sum(parts.astype(F32), axis=0)
        return [total[i * rows : (i + 1) * rows] for i in range(len(grads))]

    gate_expand_out, up_expand_out, down_shrink_out = scatter_team(
        [gate_expand_grad, up_expand_grad, down_shrink_grad]
    )
    (out_shrink_out,) = scatter_split([out_shrink_grad])
    gate_shrink_out, up_shrink_out, down_expand_out, out_expand_out = scatter_shared(
        [gate_shrink_grad, up_shrink_grad, down_expand_grad, out_expand_grad]
    )
    query_expand_out, key_expand_out, value_expand_out = scatter_split(
        [query_expand_grad, key_expand_grad, value_expand_grad]
    )
    query_shrink_out, key_shrink_out, value_shrink_out = scatter_shared(
        [query_shrink_grad, key_shrink_grad, value_shrink_grad]
    )

    return (
        both_halves(result_own, other_core(result_own)),
        both_halves(input_own, other_core(input_own)),
        both_halves(layer_input_own, other_core(layer_input_own)),
        query_shrink_out,
        key_shrink_out,
        value_shrink_out,
        gate_shrink_out,
        up_shrink_out,
        out_shrink_out,
        down_shrink_out,
        query_expand_out,
        key_expand_out,
        value_expand_out,
        gate_expand_out,
        up_expand_out,
        out_expand_out,
        down_expand_out,
    )


def solution(mesh):
    in_specs = (
        P("ctx", None),
        P("ctx", None),
        P("ctx", None),
        P(),
        P(),
        P(),
        P(),
        P("ctx", "wt"),
        P("ctx", "wt"),
        P("ctx", "wt"),
        P("ctx", "wt"),
        P("ctx", "wt"),
        P("wt", "ctx"),
        P("wt", "ctx"),
        P(),
        P(),
        P(),
        P(),
        P(),
        P(),
        P(),
        P(),
        P(),
        P(None, "wt"),
        P(None, "wt"),
        P(None, "wt"),
        P(None, "wt"),
        P(None, "wt"),
        P(None, "wt"),
        P(None, "wt"),
        P(),
        P(),
    )
    out_specs = (
        P("ctx", None),
        P("ctx", None),
        P("ctx", None),
        P(("ctx", "wt"), None),
        P(("ctx", "wt"), None),
        P(("ctx", "wt"), None),
        P(("ctx", "wt"), None),
        P(("ctx", "wt"), None),
        P("ctx", "wt"),
        P("ctx", "wt"),
        P("ctx", "wt"),
        P("ctx", "wt"),
        P("ctx", "wt"),
        P("ctx", "wt"),
        P("ctx", "wt"),
        P(("ctx", "wt"), None),
        P(("ctx", "wt"), None),
    )
    return jax.shard_map(local, mesh=mesh, in_specs=in_specs, out_specs=out_specs, check_vma=False)
```

time: 2220 us -> 1100 us (0.50)
  waiting for transfers between devices: 1740 us -> 397 us
  starting transfers between devices: 2.15 us -> 121 us
  local copies, waits for them, and re-layouts: 158 us -> 234 us
  Pallas kernels: 0 us -> 25.4 us
  other arithmetic: 68 us -> 91.1 us
    all_gather x9 -> x0, waiting for transfers between devices: 877 us -> none  [the longest x1 235 us: local(): lax.all_gather(down_weight, 'ctx', axis=1, tiled=True)]
    reduce_scatter x9 -> x0, waiting for transfers between devices: 648 us -> none  [the longest x1 94.1 us: local(): lax.psum_scatter(spread_out(grad_keys), 'ctx', scatter_dimension=0, tiled...]
    ppermute x0 -> x41, waiting for transfers between devices: none -> 252 us  [the longest x29 252 us: flip(): lax.ppermute(value, 'ctx', [(i, i ^ 1 << bit) for i in range(count_ctx)])]
    unnamed x24 -> x0, waiting for transfers between devices: 164 us -> none
    all_to_all x0 -> x14, waiting for transfers between devices: none -> 145 us  [the longest x2 45 us: team_sum(): lax.all_to_all(total, 'ctx', 0, 0, axis_index_groups=team_groups, tiled=T...]
    unnamed x301 -> x631, local copies, waits for them, and re-layouts: 30.8 us -> 166 us
    all_to_all x0 -> x14, starting transfers between devices: none -> 75.5 us  [the longest x2 13.7 us: scatter_shared(): parts = lax.all_to_all(parts, 'ctx', 0, 0, tiled=True)]
    gather x4 -> x0, local copies, waits for them, and re-layouts: 57.8 us -> none  [the longest x2 55.5 us: group_keys(): return shaped[key_device, group_ids[:, None], key_offset]]
  transfers between devices with their start and end apart: 23 -> 55, of which waited for: 22 -> 29; matrix products, arithmetic and copies ran while one was open for 13% -> 35% of each run, Pallas kernels for 0% -> 1%
where the time goes in v1:
time: 1100 us; the launch traced here: 1080 us
  waiting for transfers between devices  397 us (36%)
  local copies, waits for them, and re-layouts  234 us (21%)
  matrix products  207 us (19%)
  starting transfers between devices  121 us (11%)
  other arithmetic  91.1 us (8%)
  Pallas kernels  25.4 us (2%)
    ppermute x29, waiting for transfers between devices, flip(): lax.ppermute(value, 'ctx', [(i, i ^ 1 << bit) for i in range(count_ctx)])  252 us
    unnamed x631, local copies, waits for them, and re-layouts  166 us
    dot_general x51, matrix products, against(): lax.dot_general(left_side, right_side, (((1,), (1,)), ((), ())), preferre...  95.7 us
    dot_general x50, matrix products, product(): return jnp.dot(left_side, right_side, preferred_element_type=F32)  94.8 us
    all_to_all x2, waiting for transfers between devices, team_sum(): lax.all_to_all(total, 'ctx', 0, 0, axis_index_groups=team_groups, tiled=T...  45 us
    ppermute x29, starting transfers between devices, flip(): lax.ppermute(value, 'ctx', [(i, i ^ 1 << bit) for i in range(count_ctx)])  44 us
    all_to_all x1, waiting for transfers between devices, local(): lax.all_to_all(grad_kv, 'ctx', 0, 0, axis_index_groups=plane_groups, tile...  39.3 us
  transfers between devices with their start and end apart: 55, of which 29 were waited for; matrix products, arithmetic and copies ran while one was open for 35% of the time, Pallas kernels for 1%

profile of v1, /device:TPU:16, one launch (start us, length us, event | category | flops | bytes accessed | tf_op | source)
XLA Modules:
  0.0 1082.9 jit_solution(16508233168440039334)
XLA Ops:
  31.0 16.3 %collective-permute-done.5 = bf16[256,512]{1,0:T(8,128)(2,1)} collective-permute-done((bf16[256,512]{1,0:T(8,128)(2,1)}, bf16[256,512]{1,0:T(8,128)(2,1)}, u32[]{:S(2)}, u32[]{:S(2)}) %collective-permute-start.5) | collective-permute-done | bytes 262176 | tf_op jit(solution)/shard_map/ppermute | solution.py:268
  73.6 15.9 %collective-permute-done.17 = bf16[256,1024]{0,1:T(8,128)(2,1)S(1)} collective-permute-done((bf16[256,1024]{0,1:T(8,128)(2,1)S(1)}, bf16[256,1024]{0,1:T(8,128)(2,1)S(1)}, u32[]{:S(2)}, u32[]{:S(2)}) %collective-permute-start.17) | collective-permute-done | bytes 524320 | tf_op jit(solution)/shard_map/ppermute | solution.py:268
  112.6 4.6 collective-permute-done.18
  120.7 4.5 collective-permute-done.9
  135.1 4.8 collective-permute-done.10
  143.5 56.6 %collective-permute-done.14 = bf16[4,1,256,256]{3,2,1,0:T(8,128)(2,1)S(1)} collective-permute-done((bf16[4,1,256,256]{3,2,1,0:T(8,128)(2,1)S(1)}, bf16[4,1,256,256]{3,2,1,0:T(8,128)(2,1)S(1)}, u32[]{:S(2)}, u32[]{:S(2)}) %collective-permute-start.14) | collective-permute-done | bytes 524320 | tf_op jit(solution)/shard_map/ppermute | solution.py:268
  226.4 7.3 shard_map.437
  277.9 9.6 all-to-all-done.1
  300.5 5.1 all-to-all-done.2
  351.1 71.4 %collective-permute-done.21 = bf16[512,1024]{1,0:T(8,128)(2,1)} collective-permute-done((bf16[512,1024]{1,0:T(8,128)(2,1)}, bf16[512,1024]{1,0:T(8,128)(2,1)}, u32[]{:S(2)}, u32[]{:S(2)}) %collective-permute-start.21) | collective-permute-done | bytes 1048608 | tf_op jit(solution)/shard_map/ppermute | solution.py:268
  426.4 18.5 %collective-permute-done.24 = bf16[512,1024]{1,0:T(8,128)(2,1)} collective-permute-done((bf16[512,1024]{1,0:T(8,128)(2,1)}, bf16[512,1024]{1,0:T(8,128)(2,1)}, u32[]{:S(2)}, u32[]{:S(2)}) %collective-permute-start.24) | collective-permute-done | bytes 1048608 | tf_op jit(solution)/shard_map/ppermute | solution.py:268
  456.8 8.7 collective-permute-done.27
  490.4 26.4 %collective-permute-done.26 = bf16[512,1024]{1,0:T(8,128)(2,1)S(1)} collective-permute-done((bf16[512,1024]{1,0:T(8,128)(2,1)}, bf16[512,1024]{1,0:T(8,128)(2,1)S(1)}, u32[]{:S(2)}, u32[]{:S(2)}) %collective-permute-start.26) | collective-permute-done | bytes 1048608 | tf_op jit(solution)/shard_map/ppermute | solution.py:268
  530.1 4.6 collective-permute-done.29
  557.6 5.1 all-to-all-start.4
  562.7 28.8 %all-to-all-done.4 = bf16[4,128,2176]{1,2,0:T(8,128)(2,1)} async-done(((bf16[4,128,2176]{1,2,0:T(8,128)(2,1)}), bf16[4,128,2176]{1,2,0:T(8,128)(2,1)}, u32[]{:S(2)}, u32[]{:S(2)}) %all-to-all-start.4) | async-done | bytes 2228256 | tf_op jit(solution)/shard_map/all_to_all | solution.py:490
  635.7 4.7 all-to-all-start.5
  746.5 6.6 all-to-all-start.12
  757.9 5.0 copy_bitcast_fusion
  762.9 8.9 all-to-all-done.12
  787.4 16.2 %all-to-all-done.6 = bf16[4,128,2304]{1,2,0:T(8,128)(2,1)} async-done(((bf16[4,128,2304]{1,2,0:T(8,128)(2,1)}), bf16[4,128,2304]{1,2,0:T(8,128)(2,1)}, u32[]{:S(2)}, u32[]{:S(2)}) %all-to-all-start.6) | async-done | bytes 2359328 | tf_op jit(solution)/shard_map/all_to_all | solution.py:490
  852.6 18.0 %shard_map.438 = (f32[256,1024]{1,0:T(8,128)S(1)}, bf16[16,1,256,512]{3,2,1,0:T(8,128)(2,1)}) custom-call(s32[1]{0:T(128)} %bitcast.1.refs_0_, s32[1,9]{1,0:T(1,128)S(1)} %get-tuple-element.142.refs_1_, s32[1,9]{1,0:T(1,128)S(1)} %get-tuple-element.143.refs_2_, s32[1,9]{1,0:T(1,128)S(1)} %get-tuple-element.141.refs_3_, bf16[256,1024]{1,0:T(8,128)(2,1)S(1)} %bitcast.296, ...), custom_call_target="tpu_custom_call" | custom-call | flops 6039797760 | bytes 12582912 | tf_op jit(solution)/shard_map/pallas_call | solution.py:190
  870.7 5.0 all-to-all-start.7
  884.7 39.3 %all-to-all-done.7 = bf16[4,1024,512]{2,1,0:T(8,128)(2,1)} async-done(((bf16[4,1024,512]{2,1,0:T(8,128)(2,1)}), bf16[4,1024,512]{2,1,0:T(8,128)(2,1)}, u32[]{:S(2)}, u32[]{:S(2)}) %all-to-all-start.7) | async-done | bytes 4194336 | tf_op jit(solution)/shard_map/all_to_all | solution.py:611
  928.2 4.9 all-to-all-start.8
  944.6 11.1 %all-to-all-done.8 = bf16[4,256,512]{2,1,0:T(8,128)(2,1)} async-done(((bf16[4,256,512]{2,1,0:T(8,128)(2,1)}), bf16[4,256,512]{2,1,0:T(8,128)(2,1)}, u32[]{:S(2)}, u32[]{:S(2)}) %all-to-all-start.8) | async-done | bytes 1048608 | tf_op jit(solution)/shard_map/all_to_all | solution.py:613
  955.6 7.8 all-to-all-start.11
  1003.9 7.1 all-to-all-start.10
  1034.4 5.9 all-to-all-start.13
  1045.4 5.1 all-to-all-done.13
  1050.5 6.6 all-to-all-start.9
  1064.0 16.4 %all-to-all-done.9 = bf16[16,12,2048]{2,1,0:T(8,128)(2,1)} async-done(((bf16[16,12,2048]{2,1,0:T(8,128)(2,1)}), bf16[16,12,2048]{2,1,0:T(8,128)(2,1)}, u32[]{:S(2)}, u32[]{:S(2)}) %all-to-all-start.9) | async-done | bytes 786464 | tf_op jit(solution)/shard_map/all_to_all | solution.py:680
  (1001 shorter events, 619.1 us)
Async XLA Ops:
  4.1 62.7 %collective-permute-start.16 = (bf16[128,1024]{0,1:T(8,128)(2,1)}, bf16[128,1024]{0,1:T(8,128)(2,1)}, u32[]{:S(2)}, u32[]{:S(2)}) collective-permute-start(bf16[128,1024]{0,1:T(8,128)(2,1)} %bitcast.319), channel_id=1, source_target_pairs={{0,8},{2,10},{4,12},{6,14},{8,0},{10,2},{12,4},{14,6},{16,24},{18,... | collective-permute-start | bytes 786440 | tf_op jit(solution)/shard_map/ppermute | solution.py:268
  28.4 30.0 %collective-permute-start.1 = (bf16[256,1024]{1,0:T(8,128)(2,1)}, bf16[256,1024]{1,0:T(8,128)(2,1)}, u32[]{:S(2)}, u32[]{:S(2)}) collective-permute-start(bf16[256,1024]{1,0:T(8,128)(2,1)} %pad_maximum_fusion.8), channel_id=1, source_target_pairs={{0,16},{2,18},{4,20},{6,22},{8,24},{10,26},{12,28},{14,30},{16,0},... | collective-permute-start | bytes 1572872 | tf_op jit(solution)/shard_map/ppermute | solution.py:268
  59.7 34.5 %collective-permute-start.2 = (bf16[512,1024]{1,0:T(8,128)(2,1)S(1)}, bf16[512,1024]{1,0:T(8,128)(2,1)S(1)}, u32[]{:S(2)}, u32[]{:S(2)}) collective-permute-start(bf16[512,1024]{1,0:T(8,128)(2,1)S(1)} %pad_maximum_fusion.3), channel_id=1, source_target_pairs={{0,2},{2,0},{4,6},{6,4},{8,10},{10,8},{12,14},{14,12},{16,18},{18,... | collective-permute-start | bytes 3145736 | tf_op jit(solution)/shard_map/ppermute | solution.py:268
  65.2 30.6 %collective-permute-start.7 = (bf16[1024,512]{1,0:T(8,128)(2,1)S(1)}, bf16[1024,512]{1,0:T(8,128)(2,1)S(1)}, u32[]{:S(2)}, u32[]{:S(2)}) collective-permute-start(bf16[1024,512]{1,0:T(8,128)(2,1)S(1)} %pad_maximum_fusion.4), channel_id=1, source_target_pairs={{0,4},{2,6},{4,0},{6,2},{8,12},{10,14},{12,8},{14,10},{16,20},{18,... | collective-permute-start | bytes 3145736 | tf_op jit(solution)/shard_map/ppermute | solution.py:268
  95.2 108.5 %collective-permute-start.3 = (bf16[1024,1024]{1,0:T(8,128)(2,1)}, bf16[1024,1024]{1,0:T(8,128)(2,1)}, u32[]{:S(2)}, u32[]{:S(2)}) collective-permute-start(bf16[1024,1024]{1,0:T(8,128)(2,1)} %constant_dynamic-update-slice_fusion.8), channel_id=1, source_target_pairs={{0,4},{2,6},{4,0},{6,2},{8,12},{10,14},{12,8},{14,10},{16,20},{18,... | collective-permute-start | bytes 6291464 | tf_op jit(solution)/shard_map/ppermute | solution.py:268
  120.1 116.4 %collective-permute-start.19 = (bf16[1024,1024]{0,1:T(8,128)(2,1)}, bf16[1024,1024]{0,1:T(8,128)(2,1)}, u32[]{:S(2)}, u32[]{:S(2)}) collective-permute-start(bf16[1024,1024]{0,1:T(8,128)(2,1)} %pad_maximum_fusion.2), channel_id=1, source_target_pairs={{0,4},{2,6},{4,0},{6,2},{8,12},{10,14},{12,8},{14,10},{16,20},{18,... | collective-permute-start | bytes 6291464 | tf_op jit(solution)/shard_map/ppermute | solution.py:268
  131.6 68.5 %collective-permute-start.14 = (bf16[4,1,256,256]{3,2,1,0:T(8,128)(2,1)S(1)}, bf16[4,1,256,256]{3,2,1,0:T(8,128)(2,1)S(1)}, u32[]{:S(2)}, u32[]{:S(2)}) collective-permute-start(bf16[4,1,256,256]{3,2,1,0:T(8,128)(2,1)S(1)} %pad_maximum_fusion.11), channel_id=1, source_target_pairs={{0,4},{2,6},{4,0},{6,2},{8,12},{10,14},{12,8},{14,10},{16,20},{18,... | collective-permute-start | bytes 1572872 | tf_op jit(solution)/shard_map/ppermute | solution.py:268
  142.0 79.4 %collective-permute-start.11 = (bf16[8,1,256,256]{3,2,1,0:T(8,128)(2,1)}, bf16[8,1,256,256]{3,2,1,0:T(8,128)(2,1)}, u32[]{:S(2)}, u32[]{:S(2)}) collective-permute-start(bf16[8,1,256,256]{3,2,1,0:T(8,128)(2,1)} %pad_maximum_fusion.5), channel_id=1, source_target_pairs={{0,4},{2,6},{4,0},{6,2},{8,12},{10,14},{12,8},{14,10},{16,20},{18,... | collective-permute-start | bytes 3145736 | tf_op jit(solution)/shard_map/ppermute | solution.py:268
  241.5 27.0 %all-to-all-start.3 = ((bf16[4,128,1024]{1,2,0:T(8,128)(2,1)}), bf16[4,128,1024]{1,2,0:T(8,128)(2,1)}, u32[]{:S(2)}, u32[]{:S(2)}) async-start(bf16[4,128,1024]{1,2,0:T(8,128)(2,1)} %bitcast.326), calls=%async_computation.3 | async-start | bytes 2097152 | tf_op jit(solution)/shard_map/all_to_all | solution.py:322
  308.3 34.6 %all-to-all-start = ((bf16[4,128,2048]{2,1,0:T(8,128)(2,1)}), bf16[4,128,2048]{2,1,0:T(8,128)(2,1)}, u32[]{:S(2)}, u32[]{:S(2)}) async-start(bf16[4,128,2048]{2,1,0:T(8,128)(2,1)} %broadcast_in_dim.77), calls=%async_computation | async-start | bytes 4194304 | tf_op jit(solution)/shard_map/all_to_all | solution.py:483
  328.8 93.6 %collective-permute-start.21 = (bf16[512,1024]{1,0:T(8,128)(2,1)}, bf16[512,1024]{1,0:T(8,128)(2,1)}, u32[]{:S(2)}, u32[]{:S(2)}) collective-permute-start(bf16[512,1024]{1,0:T(8,128)(2,1)} %bitcast.303), channel_id=1, source_target_pairs={{0,16},{2,18},{4,20},{6,22},{8,24},{10,26},{12,28},{14,30},{16,0},... | collective-permute-start | bytes 3145736 | tf_op jit(solution)/shard_map/ppermute | solution.py:268
  334.7 116.7 %collective-permute-start.25 = (bf16[512,1024]{1,0:T(8,128)(2,1)}, bf16[512,1024]{1,0:T(8,128)(2,1)}, u32[]{:S(2)}, u32[]{:S(2)}) collective-permute-start(bf16[512,1024]{1,0:T(8,128)(2,1)} %bitcast.297), channel_id=1, source_target_pairs={{0,2},{2,0},{4,6},{6,4},{8,10},{10,8},{12,14},{14,12},{16,18},{18,... | collective-permute-start | bytes 3145736 | tf_op jit(solution)/shard_map/ppermute | solution.py:268
  337.2 107.7 %collective-permute-start.24 = (bf16[512,1024]{1,0:T(8,128)(2,1)}, bf16[512,1024]{1,0:T(8,128)(2,1)}, u32[]{:S(2)}, u32[]{:S(2)}) collective-permute-start(bf16[512,1024]{1,0:T(8,128)(2,1)} %bitcast.298), channel_id=1, source_target_pairs={{0,16},{2,18},{4,20},{6,22},{8,24},{10,26},{12,28},{14,30},{16,0},... | collective-permute-start | bytes 3145736 | tf_op jit(solution)/shard_map/ppermute | solution.py:268
  337.2 117.6 %collective-permute-start.22 = (bf16[512,1024]{1,0:T(8,128)(2,1)}, bf16[512,1024]{1,0:T(8,128)(2,1)}, u32[]{:S(2)}, u32[]{:S(2)}) collective-permute-start(bf16[512,1024]{1,0:T(8,128)(2,1)} %bitcast.304), channel_id=1, source_target_pairs={{0,2},{2,0},{4,6},{6,4},{8,10},{10,8},{12,14},{14,12},{16,18},{18,... | collective-permute-start | bytes 3145736 | tf_op jit(solution)/shard_map/ppermute | solution.py:268
  340.0 125.4 %collective-permute-start.27 = (bf16[512,1024]{1,0:T(8,128)(2,1)}, bf16[512,1024]{1,0:T(8,128)(2,1)}, u32[]{:S(2)}, u32[]{:S(2)}) collective-permute-start(bf16[512,1024]{1,0:T(8,128)(2,1)} %bitcast.24), channel_id=1, source_target_pairs={{0,16},{2,18},{4,20},{6,22},{8,24},{10,26},{12,28},{14,30},{16,0},... | collective-permute-start | bytes 3145736 | tf_op jit(solution)/shard_map/ppermute | solution.py:268
  422.5 53.0 %collective-permute-start.30 = (bf16[512,2048]{1,0:T(8,128)(2,1)}, bf16[512,2048]{1,0:T(8,128)(2,1)S(1)}, u32[]{:S(2)}, u32[]{:S(2)}) collective-permute-start(bf16[512,2048]{1,0:T(8,128)(2,1)} %bitcast.14), channel_id=1, source_target_pairs={{0,1},{1,0},{2,3},{3,2},{4,5},{5,4},{6,7},{7,6},{8,9},{9,8},{10,11... | collective-permute-start | bytes 6291464 | tf_op jit(solution)/shard_map/ppermute | solution.py:271
  444.9 26.8 %collective-permute-start.23 = (bf16[512,1024]{1,0:T(8,128)(2,1)}, bf16[512,1024]{1,0:T(8,128)(2,1)S(1)}, u32[]{:S(2)}, u32[]{:S(2)}) collective-permute-start(bf16[512,1024]{1,0:T(8,128)(2,1)} %collective-permute-done.21), channel_id=1, source_target_pairs={{0,2},{2,0},{4,6},{6,4},{8,10},{10,8},{12,14},{14,12},{16,18},{18,... | collective-permute-start | bytes 3145736 | tf_op jit(solution)/shard_map/ppermute | solution.py:268
  451.4 75.8 %collective-permute-start.28 = (bf16[512,1024]{1,0:T(8,128)(2,1)}, bf16[512,1024]{1,0:T(8,128)(2,1)}, u32[]{:S(2)}, u32[]{:S(2)}) collective-permute-start(bf16[512,1024]{1,0:T(8,128)(2,1)} %bitcast.24), channel_id=1, source_target_pairs={{0,2},{2,0},{4,6},{6,4},{8,10},{10,8},{12,14},{14,12},{16,18},{18,... | collective-permute-start | bytes 3145736 | tf_op jit(solution)/shard_map/ppermute | solution.py:268
  454.8 61.9 %collective-permute-start.26 = (bf16[512,1024]{1,0:T(8,128)(2,1)}, bf16[512,1024]{1,0:T(8,128)(2,1)S(1)}, u32[]{:S(2)}, u32[]{:S(2)}) collective-permute-start(bf16[512,1024]{1,0:T(8,128)(2,1)} %collective-permute-done.24), channel_id=1, source_target_pairs={{0,2},{2,0},{4,6},{6,4},{8,10},{10,8},{12,14},{14,12},{16,18},{18,... | collective-permute-start | bytes 3145736 | tf_op jit(solution)/shard_map/ppermute | solution.py:268
  465.5 69.2 %collective-permute-start.29 = (bf16[512,1024]{1,0:T(8,128)(2,1)}, bf16[512,1024]{1,0:T(8,128)(2,1)}, u32[]{:S(2)}, u32[]{:S(2)}) collective-permute-start(bf16[512,1024]{1,0:T(8,128)(2,1)} %collective-permute-done.27), channel_id=1, source_target_pairs={{0,2},{2,0},{4,6},{6,4},{8,10},{10,8},{12,14},{14,12},{16,18},{18,... | collective-permute-start | bytes 3145736 | tf_op jit(solution)/shard_map/ppermute | solution.py:268
  557.6 33.9 %all-to-all-start.4 = ((bf16[4,128,2176]{1,2,0:T(8,128)(2,1)}), bf16[4,128,2176]{1,2,0:T(8,128)(2,1)}, u32[]{:S(2)}, u32[]{:S(2)}) async-start(bf16[4,128,2176]{1,2,0:T(8,128)(2,1)} %copy_bitcast_fusion.1), calls=%async_computation.4 | async-start | bytes 4456448 | tf_op jit(solution)/shard_map/all_to_all | solution.py:490
  635.7 30.0 %all-to-all-start.5 = ((bf16[4,128,2048]{2,1,0:T(8,128)(2,1)}), bf16[4,128,2048]{2,1,0:T(8,128)(2,1)}, u32[]{:S(2)}, u32[]{:S(2)}) async-start(bf16[4,128,2048]{2,1,0:T(8,128)(2,1)} %broadcast_in_dim.80), calls=%async_computation.5 | async-start | bytes 4194304 | tf_op jit(solution)/shard_map/all_to_all | solution.py:483
  667.8 26.4 %collective-permute-start.33 = (bf16[512,2048]{1,0:T(8,128)(2,1)}, bf16[512,2048]{1,0:T(8,128)(2,1)S(1)}, u32[]{:S(2)}, u32[]{:S(2)}) collective-permute-start(bf16[512,2048]{1,0:T(8,128)(2,1)} %bitcast.27), channel_id=1, source_target_pairs={{0,1},{1,0},{2,3},{3,2},{4,5},{5,4},{6,7},{7,6},{8,9},{9,8},{10,11... | collective-permute-start | bytes 6291464 | tf_op jit(solution)/shard_map/ppermute | solution.py:271
  729.4 28.4 %collective-permute-start.34 = (bf16[512,2304]{0,1:T(8,128)(2,1)}, bf16[512,2304]{0,1:T(8,128)(2,1)}, u32[]{:S(2)}, u32[]{:S(2)}) collective-permute-start(bf16[512,2304]{0,1:T(8,128)(2,1)} %constant_dynamic-update-slice_fusion.134), channel_id=1, source_target_pairs={{0,1},{1,0},{2,3},{3,2},{4,5},{5,4},{6,7},{7,6},{8,9},{9,8},{10,11... | collective-permute-start | bytes 7077896 | tf_op jit(solution)/shard_map/ppermute | solution.py:271
  771.8 31.9 %all-to-all-start.6 = ((bf16[4,128,2304]{1,2,0:T(8,128)(2,1)}), bf16[4,128,2304]{1,2,0:T(8,128)(2,1)}, u32[]{:S(2)}, u32[]{:S(2)}) async-start(bf16[4,128,2304]{1,2,0:T(8,128)(2,1)} %copy_bitcast_fusion), calls=%async_computation.6 | async-start | bytes 4718592 | tf_op jit(solution)/shard_map/all_to_all | solution.py:490
  870.7 53.4 %all-to-all-start.7 = ((bf16[4,1024,512]{2,1,0:T(8,128)(2,1)}), bf16[4,1024,512]{2,1,0:T(8,128)(2,1)}, u32[]{:S(2)}, u32[]{:S(2)}) async-start(bf16[4,1024,512]{2,1,0:T(8,128)(2,1)} %bitcast.314), calls=%async_computation.7 | async-start | bytes 8388608 | tf_op jit(solution)/shard_map/all_to_all | solution.py:611
  880.1 99.0 %collective-permute-start.40 = (bf16[4,16,4,2048]{3,1,2,0:T(8,128)(2,1)}, bf16[4,16,4,2048]{3,1,2,0:T(8,128)(2,1)}, u32[]{:S(2)}, u32[]{:S(2)}) collective-permute-start(bf16[4,16,4,2048]{3,1,2,0:T(8,128)(2,1)} %fusion.78), channel_id=1, source_target_pairs={{0,1},{1,0},{2,3},{3,2},{4,5},{5,4},{6,7},{7,6},{8,9},{9,8},{10,11... | collective-permute-start | bytes 3145736 | tf_op jit(solution)/shard_map/ppermute | solution.py:271
  928.2 27.4 %all-to-all-start.8 = ((bf16[4,256,512]{2,1,0:T(8,128)(2,1)}), bf16[4,256,512]{2,1,0:T(8,128)(2,1)}, u32[]{:S(2)}, u32[]{:S(2)}) async-start(bf16[4,256,512]{2,1,0:T(8,128)(2,1)} %bitcast.317), calls=%async_computation.8 | async-start | bytes 2097152 | tf_op jit(solution)/shard_map/all_to_all | solution.py:613
  955.6 48.2 %all-to-all-start.11 = ((bf16[16,8,1024]{2,1,0:T(8,128)(2,1)}), bf16[16,8,1024]{2,1,0:T(8,128)(2,1)}, u32[]{:S(2)}, u32[]{:S(2)}) async-start(bf16[16,8,1024]{2,1,0:T(8,128)(2,1)} %fusion.48), calls=%async_computation.11 | async-start | bytes 524288 | tf_op jit(solution)/shard_map/all_to_all | solution.py:653
  1003.9 30.5 %all-to-all-start.10 = ((bf16[16,16,2048]{2,1,0:T(8,128)(2,1)}), bf16[16,16,2048]{2,1,0:T(8,128)(2,1)}, u32[]{:S(2)}, u32[]{:S(2)}) async-start(bf16[16,16,2048]{2,1,0:T(8,128)(2,1)} %copy.299), calls=%async_computation.10 | async-start | bytes 2097152 | tf_op jit(solution)/shard_map/all_to_all | solution.py:680
  1012.4 29.8 %collective-permute-start.39 = (bf16[3,16,4,2048]{3,1,2,0:T(8,128)(2,1)}, bf16[3,16,4,2048]{3,1,2,0:T(8,128)(2,1)}, u32[]{:S(2)}, u32[]{:S(2)}) collective-permute-start(bf16[3,16,4,2048]{3,1,2,0:T(8,128)(2,1)} %fusion.80), channel_id=1, source_target_pairs={{0,1},{1,0},{2,3},{3,2},{4,5},{5,4},{6,7},{7,6},{8,9},{9,8},{10,11... | collective-permute-start | bytes 2359304 | tf_op jit(solution)/shard_map/ppermute | solution.py:271
  1050.5 29.9 %all-to-all-start.9 = ((bf16[16,12,2048]{2,1,0:T(8,128)(2,1)}), bf16[16,12,2048]{2,1,0:T(8,128)(2,1)}, u32[]{:S(2)}, u32[]{:S(2)}) async-start(bf16[16,12,2048]{2,1,0:T(8,128)(2,1)} %copy.294), calls=%async_computation.9 | async-start | bytes 2097152 | tf_op jit(solution)/shard_map/all_to_all | solution.py:680
  (240 other events, 2808.6 us)

commit v2 on v1

v2 whole, which is shorter than its diff:
```python
import jax
import jax.numpy as jnp
from jax import lax
from jax.experimental import pallas as pl
from jax.experimental.pallas import tpu as pltpu
from jax.sharding import PartitionSpec as P

QUERY_HEADS = 8
KEY_VALUE_HEADS = 2
ADAPTER_COUNT = 8
ADAPTER_RANK = 16
PROMPT = 2048
CONT = 256

EPS = 1e-06
THETA = 1000000.0
ROOT_HALF = 0.5**0.5
F32 = jnp.float32
BF16 = jnp.bfloat16
SWAP = [(0, 1), (1, 0)]


def normalized(inputs, norm_gain):
    return inputs * lax.rsqrt(jnp.mean(inputs * inputs, axis=-1, keepdims=True) + EPS) * norm_gain


def rotary_applied(inputs, cosine, sine_term):
    half_width = inputs.shape[-1] // 2
    first_half = inputs[..., :half_width]
    second_half = inputs[..., half_width:]
    return jnp.concatenate(
        [
            first_half * cosine - second_half * sine_term,
            second_half * cosine + first_half * sine_term,
        ],
        axis=-1,
    )


def product(left_side, right_side):
    return jnp.dot(left_side, right_side, preferred_element_type=F32)


def against(left_side, right_side):
    return lax.dot_general(
        left_side, right_side, (((1,), (1,)), ((), ())), preferred_element_type=F32
    )


def summed(left_side, right_side):
    return lax.dot_general(
        left_side, right_side, (((0,), (0,)), ((), ())), preferred_element_type=F32
    )


def low(value):
    return value.astype(BF16)


def attend_kernel(count_ref, kslot_ref, vslot_ref, q_ref, k_ref, v_ref, o_ref, lse_ref, acc, tot, *, heads, dim):
    group = pl.program_id(0)
    count = count_ref[group]
    rows = q_ref.shape[0]
    fold = tot.shape[-1]
    acc[...] = jnp.zeros_like(acc)
    tot[...] = jnp.zeros_like(tot)

    def step(index, masked):
        keys = k_ref[kslot_ref[group, index], 0]
        values = v_ref[vslot_ref[group, index], 0]
        for head in range(heads):
            lanes = slice(head * dim, (head + 1) * dim)
            scores = against(q_ref[:, lanes], keys)
            weights = jnp.exp(scores)
            if masked:
                row = lax.broadcasted_iota(jnp.int32, scores.shape, 0)
                col = lax.broadcasted_iota(jnp.int32, scores.shape, 1)
                weights = jnp.where(col <= row, weights, 0.0)
            part = weights[:, :fold]
            for start in range(fold, rows, fold):
                part = part + weights[:, start : start + fold]
            tot[head] += part
            acc[:, lanes] += product(low(weights), values)

    def body(index, carry):
        step(index, False)
        return carry

    lax.fori_loop(0, count - 1, body, 0)
    step(count - 1, True)
    lane = lax.broadcasted_iota(jnp.int32, lse_ref.shape, 1)
    lse = jnp.zeros(lse_ref.shape, F32)
    for head in range(heads):
        lanes = slice(head * dim, (head + 1) * dim)
        total = jnp.sum(tot[head], axis=-1, keepdims=True)
        o_ref[:, lanes] = low(acc[:, lanes] / total)
        lse = jnp.where(lane == head, jnp.log(total), lse)
    lse_ref[...] = lse


def attend_back_kernel(
    count_ref, kslot_ref, vslot_ref, q_ref, k_ref, v_ref, o_ref, lse_ref, g_ref, dq_ref, dk_near, dk_far, dv_near, dv_far, delta, *, heads, dim
):
    group = pl.program_id(0)
    count = count_ref[group]
    dq_ref[...] = jnp.zeros_like(dq_ref)
    for out_ref in (dk_near, dk_far, dv_near, dv_far):
        out_ref[...] = jnp.zeros_like(out_ref)
    half = dk_near.shape[0]

    def put(near_ref, far_ref, slot, value):
        @pl.when(slot < half)
        def _():
            near_ref[slot, 0] = low(value)

        @pl.when(slot >= half)
        def _():
            far_ref[slot - half, 0] = low(value)

    for head in range(heads):
        lanes = slice(head * dim, (head + 1) * dim)
        delta[head] = jnp.sum(
            o_ref[:, lanes].astype(F32) * g_ref[:, lanes].astype(F32), axis=-1, keepdims=True
        )

    def step(index, masked):
        keys = k_ref[kslot_ref[group, index], 0]
        values = v_ref[vslot_ref[group, index], 0]
        dk = jnp.zeros(keys.shape, F32)
        dv = jnp.zeros(values.shape, F32)
        for head in range(heads):
            lanes = slice(head * dim, (head + 1) * dim)
            queries = q_ref[:, lanes]
            upstream = g_ref[:, lanes]
            scores = against(queries, keys)
            weights = jnp.exp(scores - lse_ref[:, head : head + 1])
            if masked:
                row = lax.broadcasted_iota(jnp.int32, scores.shape, 0)
                col = lax.broadcasted_iota(jnp.int32, scores.shape, 1)
                weights = jnp.where(col <= row, weights, 0.0)
            grad_weights = against(upstream, values)
            grad_scores = low(weights * (grad_weights - delta[head]))
            dq_ref[:, lanes] += product(grad_scores, keys)
            dk += summed(grad_scores, queries)
            dv += summed(low(weights), upstream)
        put(dk_near, dk_far, kslot_ref[group, index], dk)
        put(dv_near, dv_far, vslot_ref[group, index], dv)

    def body(index, carry):
        step(index, False)
        return carry

    lax.fori_loop(0, count - 1, body, 0)
    step(count - 1, True)


def attend(tables, queries, key_all, value_all, groups, heads, dim):
    count, kslot, vslot = tables
    slots, _, block, _ = key_all.shape
    rows = queries.shape[0]
    fold = min(128, block)
    whole = pl.BlockSpec((slots, 1, block, dim), lambda g, *_: (0, g, 0, 0))
    mine = pl.BlockSpec((block, heads * dim), lambda g, *_: (g, 0))
    return pl.pallas_call(
        lambda *refs: attend_kernel(*refs, heads=heads, dim=dim),
        grid_spec=pltpu.PrefetchScalarGridSpec(
            num_scalar_prefetch=3,
            grid=(groups,),
            in_specs=[mine, whole, whole],
            out_specs=[mine, pl.BlockSpec((block, 128), lambda g, *_: (g, 0))],
            scratch_shapes=[
                pltpu.VMEM((block, heads * dim), F32),
                pltpu.VMEM((heads, block, fold), F32),
            ],
        ),
        out_shape=[
            jax.ShapeDtypeStruct((rows, heads * dim), BF16),
            jax.ShapeDtypeStruct((rows, 128), F32),
        ],
        compiler_params=pltpu.CompilerParams(vmem_limit_bytes=40 * 2**20),
        cost_estimate=pl.CostEstimate(
            flops=4 * rows * heads * dim * 2304, bytes_accessed=6 * 2**20, transcendentals=rows * heads * 2304
        ),
    )(count, kslot, vslot, queries, key_all, value_all)


def attend_back(tables, queries, key_all, value_all, heads_low, lse, grads, groups, heads, dim):
    count, kslot, vslot = tables
    slots, _, block, _ = key_all.shape
    rows = queries.shape[0]
    whole = pl.BlockSpec((slots, 1, block, dim), lambda g, *_: (0, g, 0, 0))
    part = pl.BlockSpec((slots // 2, 1, block, dim), lambda g, *_: (0, g, 0, 0))
    mine = pl.BlockSpec((block, heads * dim), lambda g, *_: (g, 0))
    return pl.pallas_call(
        lambda *refs: attend_back_kernel(*refs, heads=heads, dim=dim),
        grid_spec=pltpu.PrefetchScalarGridSpec(
            num_scalar_prefetch=3,
            grid=(groups,),
            in_specs=[mine, whole, whole, mine, pl.BlockSpec((block, 128), lambda g, *_: (g, 0)), mine],
            out_specs=[mine] + [part] * 4,
            scratch_shapes=[pltpu.VMEM((heads, block, 1), F32)],
        ),
        out_shape=[
            jax.ShapeDtypeStruct((rows, heads * dim), F32),
        ]
        + [jax.ShapeDtypeStruct((slots // 2, groups, block, dim), BF16)] * 4,
        compiler_params=pltpu.CompilerParams(vmem_limit_bytes=48 * 2**20),
        cost_estimate=pl.CostEstimate(
            flops=10 * rows * heads * dim * 2304, bytes_accessed=12 * 2**20, transcendentals=rows * heads * 2304
        ),
    )(count, kslot, vslot, queries, key_all, value_all, heads_low, lse, grads)


def gelu_parts(gate):
    slope = 0.7978845608028654
    square = gate * gate
    bend = jnp.tanh(slope * gate * (1.0 + 0.044715 * square))
    half = 0.5 * (1.0 + bend)
    grad = half + 0.5 * gate * (1.0 - bend * bend) * slope * (1.0 + 0.134145 * square)
    return gate * half, grad


def rms_scale(value):
    return lax.rsqrt(jnp.mean(value * value, axis=-1, keepdims=True) + EPS)


def rms_pull(value, scale, weighted):
    return scale * weighted - value * (
        scale * scale * scale * jnp.mean(value * weighted, axis=-1, keepdims=True)
    )


def move_columns(out_ref, in_ref, table_ref, count, block):
    for j in range(count):
        start = pl.multiple_of(table_ref[j] * block, block)
        out_ref[:, j * block : (j + 1) * block] = in_ref[:, pl.ds(start, block)].astype(
            out_ref.dtype
        )


def whole_call(kernel, inputs, outputs, scratch=(), tables=(), specs=None, flops=10**9):
    specs = specs or {}

    def full(array):
        return pl.BlockSpec(array.shape, lambda *_: (0,) * len(array.shape))

    in_specs = [specs.get(i, full(array)) for i, array in enumerate(inputs)]
    size = sum(a.size * a.dtype.itemsize for a in inputs)
    return pl.pallas_call(
        kernel,
        grid_spec=pltpu.PrefetchScalarGridSpec(
            num_scalar_prefetch=len(tables),
            grid=(1,),
            in_specs=in_specs,
            out_specs=[full(array) for array in outputs],
            scratch_shapes=list(scratch),
        ),
        out_shape=list(outputs),
        compiler_params=pltpu.CompilerParams(vmem_limit_bytes=56 * 2**20),
        cost_estimate=pl.CostEstimate(flops=flops, bytes_accessed=size, transcendentals=0),
    )(*tables, *inputs)


def first_kernel(order_ref, tokens_ref, gains_ref, select_ref, shrink_ref, moved_ref, low_ref, rank_ref, *, count, block, aligned):
    tokens = tokens_ref[...].astype(F32)
    first = low(tokens * rms_scale(tokens) * gains_ref[0:1, :])
    low_ref[...] = first
    ranks = against(first, shrink_ref[...])
    select = select_ref[...]
    width = select.shape[1]
    for i in range(3):
        rank_ref[:, i * width : (i + 1) * width] = low(select * ranks[:, i * width : (i + 1) * width])
    if aligned:
        move_columns(moved_ref, low_ref, order_ref, count, block)
    else:
        moved_ref[...] = first


def middle_kernel(
    half_ref, back_ref, own_ref, other_ref, tokens_ref, gains_ref, expand_ref, left_ref, right_ref,
    total_ref, laurel_ref, mid_ref, second_ref, rank_ref, work, *, count, block, aligned
):
    width = total_ref.shape[1]
    summed_all = own_ref[...] + other_ref[...].astype(F32)
    rank = low(summed_all[:, width:])
    rank_ref[...] = rank
    if aligned:
        work[...] = summed_all[:, :width]
        move_columns(total_ref, work, back_ref, count, block)
        attn = total_ref[...] + product(rank, expand_ref[...])
    else:
        attn = summed_all[:, :width] + product(rank, expand_ref[...])
    total_ref[...] = attn
    tokens = tokens_ref[...].astype(F32)
    first = tokens * rms_scale(tokens) * gains_ref[0:1, :]
    laurel = product(low(product(low(first), left_ref[...])), right_ref[...])
    laurel_ref[...] = laurel
    mid = (
        tokens
        + attn * rms_scale(attn) * gains_ref[1:2, :]
        + first
        + laurel * rms_scale(laurel) * gains_ref[2:3, :]
    ) * ROOT_HALF
    mid_ref[...] = mid
    second_ref[...] = low(mid * rms_scale(mid) * gains_ref[3:4, :])


def keep_rows(out_ref, work_ref, value, pick_ref):
    if out_ref.shape[0] == value.shape[0]:
        out_ref[...] = value.astype(out_ref.dtype)
    else:
        work_ref[...] = value
        rows = out_ref.shape[0]
        start = pl.multiple_of(pick_ref[0] * rows, rows)
        out_ref[...] = work_ref[pl.ds(start, rows), :].astype(out_ref.dtype)


def layer_kernel(
    half_ref, pick_ref, near_ref, y_ref, z_ref, yz_ref, mid_ref, gains_ref, expand_ref, gate_ref, lift_ref, layer_ref, up_ref,
    result_ref, layer_grad_ref, after_ref, grad_ref, expand_grad_ref, kept
):
    width = mid_ref.shape[1]
    joined = near_ref[...].astype(F32) + y_ref[...] + z_ref[...] + yz_ref[...]
    rank = low(joined[:, width:])
    total = joined[:, :width] + product(rank, expand_ref[...])
    scale = rms_scale(total)
    gain = gains_ref[4:5, :]
    after = mid_ref[...] + total * scale * gain
    layer_pre = product(low(after), gate_ref[...])
    layer_in = layer_ref[...].astype(F32)
    act, slope = gelu_parts(layer_pre)
    back = product(low(act * layer_in), lift_ref[...])
    back_scale = rms_scale(back)
    last_gain = gains_ref[5:6, :]
    result_ref[...] = low(after + back * back_scale * last_gain)
    upstream = up_ref[...].astype(F32)
    grad_back = low(rms_pull(back, back_scale, upstream * last_gain))
    grad_gated = against(grad_back, lift_ref[...])
    layer_grad_ref[...] = grad_gated * act
    grad_pre = low(grad_gated * layer_in * slope)
    grad_after = upstream + against(grad_pre, gate_ref[...])
    after_ref[...] = grad_after
    grad_ffn = low(rms_pull(total, scale, grad_after * gain))
    grad_ref[...] = grad_ffn
    keep_rows(expand_grad_ref, kept, summed(rank, grad_ffn), pick_ref)


def turn_kernel(
    order_ref, pick_ref, near_ref, y_ref, z_ref, yz_ref, mid_ref, after_ref, total_ref, laurel_ref, second_ref, gains_ref, gate_ref, up_ref,
    right_ref, left_ref, expand_ref, rank_ref, select_ref,
    sent_ref, scaled_ref, first_ref, grads_ref, work, kept, *, count, block, aligned
):
    width = mid_ref.shape[1]
    ranks = select_ref.shape[1]
    joined = near_ref[...].astype(F32) + y_ref[...] + z_ref[...] + yz_ref[...]
    rank_gate = low(joined[:, width : width + ranks])
    rank_up = low(joined[:, width + ranks :])
    grad_second = joined[:, :width]
    grad_second = grad_second + product(rank_gate, gate_ref[...]) + product(rank_up, up_ref[...])
    keep_rows(grads_ref.at[0], kept, summed(rank_gate, second_ref[...]), pick_ref)
    keep_rows(grads_ref.at[1], kept, summed(rank_up, second_ref[...]), pick_ref)
    mid = mid_ref[...]
    grad_mid = after_ref[...] + rms_pull(mid, rms_scale(mid), grad_second * gains_ref[3:4, :])
    scaled = grad_mid * ROOT_HALF
    scaled_ref[...] = scaled
    attn = total_ref[...]
    grad_attn = rms_pull(attn, rms_scale(attn), scaled * gains_ref[1:2, :])
    laurel = laurel_ref[...]
    grad_laurel = low(rms_pull(laurel, rms_scale(laurel), scaled * gains_ref[2:3, :]))
    grad_rank = low(against(grad_laurel, right_ref[...]))
    first_ref[...] = scaled + against(grad_rank, left_ref[...])
    attn_low = low(grad_attn)
    keep_rows(grads_ref.at[2], kept, summed(rank_ref[...], attn_low), pick_ref)
    sent_ref[:, width:] = low(select_ref[...] * against(attn_low, expand_ref[...]))
    if aligned:
        work[...] = grad_attn
        for j in range(count):
            start = pl.multiple_of(order_ref[j] * block, block)
            sent_ref[:, j * block : (j + 1) * block] = low(work[:, pl.ds(start, block)])
    else:
        sent_ref[:, :width] = attn_low


def last_kernel(
    half_ref, back_ref, pick_ref, own_ref, other_ref, tokens_ref, gains_ref, scaled_ref, first_ref, shrink_ref,
    input_ref, grads_ref, work, place, kept, *, count, block, aligned
):
    width = scaled_ref.shape[1]
    joined = own_ref[...] + other_ref[...].astype(F32)
    ranks = low(joined[:, width:])
    each = ranks.shape[1] // 3
    work[...] = joined[:, :width]
    if aligned:
        move_columns(place, work, back_ref, count, block)
        grad_first = place[...]
    else:
        grad_first = work[...]
    grad_first = grad_first + first_ref[...] + product(ranks, shrink_ref[...])
    tokens = tokens_ref[...].astype(F32)
    scale = rms_scale(tokens)
    gain = gains_ref[0:1, :]
    input_ref[...] = scaled_ref[...] + rms_pull(tokens, scale, grad_first * gain)
    first = low(tokens * scale * gain)
    for i in range(3):
        keep_rows(
            grads_ref.at[i], kept, summed(ranks[:, i * each : (i + 1) * each], first), pick_ref
        )


def gather_parts(out_ref, parts, table_ref, count, width):
    height = parts[0].shape[0]
    block = width // count
    for i, part in enumerate(parts):
        rows = slice(i * height, (i + 1) * height)
        if block % 128 == 0:
            for j in range(count):
                start = pl.multiple_of(table_ref[j] * block, block)
                out_ref[rows, j * block : (j + 1) * block] = part[:, pl.ds(start, block)]
        else:
            out_ref[rows, :] = part[...]


def ranks_of(out_ref, parts, select_ref, maps_ref):
    height = parts[0].shape[0]
    ranks = select_ref.shape[1]
    for i, part in enumerate(parts):
        rows = slice(i * height, (i + 1) * height)
        found = against(part[...], maps_ref[...])
        for start in range(0, out_ref.shape[1], ranks):
            out_ref[rows, start : start + ranks] = low(
                select_ref[rows, :] * found[:, start : start + ranks]
            )


def bring(pieces, space, sems):
    rows = pieces[0].shape[0]
    copies = [
        pltpu.make_async_copy(piece, space.at[pl.ds(i * rows, rows), :], sems.at[i])
        for i, piece in enumerate(pieces)
    ]
    for copy in copies:
        copy.start()
    return copies


def put_columns(out_ref, value, start, table_ref, block):
    size = value.shape[1]
    if block % 128:
        out_ref[:, pl.ds(start, size)] = value.astype(out_ref.dtype)
        return
    for i in range(size // block):
        place = pl.multiple_of(table_ref[start // block + i] * block, block)
        out_ref[:, pl.ds(place, block)] = value[:, i * block : (i + 1) * block].astype(out_ref.dtype)


def feed_kernel(order_ref, *refs, pieces, width, count):
    parts, (select_ref, shrink_ref, gexp_ref, uexp_ref, dshr_ref), refs = refs[:4], refs[4:9], refs[9:]
    gates, ups, downs = refs[:pieces], refs[pieces : 2 * pieces], refs[2 * pieces : 3 * pieces]
    rank_ref, act_ref, slope_ref, hid_ref, part_ref, x_ref, gate_w, up_w, down_w, sems = refs[3 * pieces :]
    arriving = bring(gates, gate_w, sems.at[0]) + bring(ups, up_w, sems.at[1])
    arriving_down = bring(downs, down_w, sems.at[2])
    ranks = select_ref.shape[1]
    hidden_width = gate_w.shape[1]
    chunk = min(256, hidden_width)
    gather_parts(x_ref, parts, order_ref, count, width)
    ranks_of(rank_ref, parts, select_ref, shrink_ref)
    for copy in arriving:
        copy.wait()

    @pl.loop(0, hidden_width // chunk)
    def _(i):
        lanes = pl.ds(pl.multiple_of(i * chunk, chunk), chunk)
        gate = product(x_ref[...], gate_w[:, lanes]) + product(rank_ref[:, :ranks], gexp_ref[:, lanes])
        up = product(x_ref[...], up_w[:, lanes]) + product(rank_ref[:, ranks:], uexp_ref[:, lanes])
        act, slope = gelu_parts(gate)
        act_ref[:, lanes] = low(act)
        slope_ref[:, lanes] = low(slope * up)
        hid_ref[:, lanes] = low(act * up)

    for copy in arriving_down:
        copy.wait()
    step = 256

    @pl.loop(0, width // step)
    def _(i):
        start = pl.multiple_of(i * step, step)
        put_columns(
            part_ref, against(hid_ref[...], down_w[pl.ds(start, step), :]), start, order_ref, width // count
        )

    part_ref[:, width:] = (select_ref[...] * against(hid_ref[...], dshr_ref[...])).astype(part_ref.dtype)


def feed_call(kernel, order, parts, inputs, weights, outputs, scratch, flops):
    def full(array):
        return pl.BlockSpec(array.shape, lambda *_: (0,) * len(array.shape))

    pieces = [piece for matrix in weights for piece in matrix]
    matrix = pltpu.VMEM((len(weights[0]) * weights[0][0].shape[0], weights[0][0].shape[1]), BF16)
    width = parts[0].shape[1]
    return pl.pallas_call(
        lambda *refs: kernel(*refs, pieces=len(weights[0]), width=width, count=order.shape[0]),
        grid_spec=pltpu.PrefetchScalarGridSpec(
            num_scalar_prefetch=1,
            grid=(1,),
            in_specs=[full(array) for array in (*parts, *inputs)]
            + [pl.BlockSpec(memory_space=pl.ANY)] * len(pieces),
            out_specs=[full(array) for array in outputs],
            scratch_shapes=list(scratch)
            + [matrix, matrix, matrix, pltpu.SemaphoreType.DMA((3, len(weights[0])))],
        ),
        out_shape=list(outputs),
        compiler_params=pltpu.CompilerParams(vmem_limit_bytes=58 * 2**20),
        cost_estimate=pl.CostEstimate(flops=flops, bytes_accessed=20 * 2**20, transcendentals=0),
    )(order, *parts, *inputs, *pieces)


def feed(order, parts, select, shrink, gexp, uexp, dshr, gates, ups, downs, out_dtype):
    rows, width = 4 * parts[0].shape[0], parts[0].shape[1]
    hidden, ranks = gexp.shape[1], select.shape[1]
    low_hidden = jax.ShapeDtypeStruct((rows, hidden), BF16)
    return feed_call(
        feed_kernel,
        order,
        parts,
        (select, shrink, gexp, uexp, dshr),
        (gates, ups, downs),
        (
            jax.ShapeDtypeStruct((rows, 2 * ranks), BF16),
            low_hidden,
            low_hidden,
            low_hidden,
            jax.ShapeDtypeStruct((rows, width + ranks), out_dtype),
        ),
        (pltpu.VMEM((rows, width), BF16),),
        6 * rows * width * hidden,
    )


def feed_back_kernel(order_ref, *refs, pieces, width, count):
    parts, refs = refs[:4], refs[4:]
    (
        select_ref,
        dexp_ref,
        rank_ref,
        start_ref,
        act_ref,
        slope_ref,
        hid_ref,
        gexp_ref,
        uexp_ref,
        dshr_ref,
    ), refs = refs[:10], refs[10:]
    gates, ups, downs = refs[:pieces], refs[pieces : 2 * pieces], refs[2 * pieces : 3 * pieces]
    part_ref, grads_ref, g_ref, down_rank, gate_grad, up_grad, gate_w, up_w, down_w, sems = refs[3 * pieces :]
    arriving = bring(downs, down_w, sems.at[2])
    arriving_next = bring(gates, gate_w, sems.at[0]) + bring(ups, up_w, sems.at[1])
    ranks = select_ref.shape[1]
    hidden_width = gate_w.shape[1]
    chunk = min(256, hidden_width)
    gather_parts(g_ref, parts, order_ref, count, width)
    ranks_of(down_rank, parts, select_ref, dexp_ref)
    for copy in arriving:
        copy.wait()

    @pl.loop(0, hidden_width // chunk)
    def _(i):
        lanes = pl.ds(pl.multiple_of(i * chunk, chunk), chunk)
        grad_hidden = product(g_ref[...], down_w[:, lanes]) + product(down_rank[...], dshr_ref[:, lanes])
        grad_gate = low(grad_hidden * slope_ref[:, lanes].astype(F32))
        grad_up = low(grad_hidden * act_ref[:, lanes].astype(F32))
        gate_grad[:, lanes] = grad_gate
        up_grad[:, lanes] = grad_up
        grads_ref[0, :, lanes] = start_ref[0, :, lanes] + summed(rank_ref[:, :ranks], grad_gate)
        grads_ref[1, :, lanes] = start_ref[1, :, lanes] + summed(rank_ref[:, ranks:], grad_up)
        grads_ref[2, :, lanes] = start_ref[2, :, lanes] + summed(down_rank[...], hid_ref[:, lanes])

    for copy in arriving_next:
        copy.wait()
    step = 256

    @pl.loop(0, width // step)
    def _(i):
        start = pl.multiple_of(i * step, step)
        found = against(gate_grad[...], gate_w[pl.ds(start, step), :]) + against(
            up_grad[...], up_w[pl.ds(start, step), :]
        )
        put_columns(part_ref, found, start, order_ref, width // count)

    select = select_ref[...]
    part_ref[:, width : width + ranks] = (select * against(gate_grad[...], gexp_ref[...])).astype(part_ref.dtype)
    part_ref[:, width + ranks :] = (select * against(up_grad[...], uexp_ref[...])).astype(part_ref.dtype)


def feed_back(order, parts, select, dexp, start, kept, gexp, uexp, dshr, gates, ups, downs, out_dtype):
    rows, width = 4 * parts[0].shape[0], parts[0].shape[1]
    hidden, ranks = gexp.shape[1], select.shape[1]
    low_hidden = pltpu.VMEM((rows, hidden), BF16)
    return feed_call(
        feed_back_kernel,
        order,
        parts,
        (select, dexp, kept[0], start, *kept[1:], gexp, uexp, dshr),
        (gates, ups, downs),
        (
            jax.ShapeDtypeStruct((rows, width + 2 * ranks), out_dtype),
            jax.ShapeDtypeStruct((3, ranks, hidden), F32),
        ),
        (pltpu.VMEM((rows, width), BF16), pltpu.VMEM((rows, ranks), BF16), low_hidden, low_hidden),
        6 * rows * width * hidden,
    )


def local(
    tokens,
    layer_input,
    out_grad,
    block_device,
    adapter_pick,
    norm_gains,
    head_norm_gains,
    query_weight,
    key_matrix,
    value_matrix,
    gate_weight,
    up_weight,
    out_weight,
    down_weight,
    laurel_left,
    laurel_right,
    layer_gate,
    layer_lift,
    query_shrink,
    key_shrink,
    value_shrink,
    gate_shrink,
    up_shrink,
    out_shrink,
    down_shrink,
    query_expand,
    key_widen_maps,
    value_widen_maps,
    gate_expand,
    up_expand,
    out_expand,
    down_expand,
):
    count_ctx = lax.axis_size("ctx")
    bit_count = count_ctx.bit_length() - 1
    groups = block_device.shape[0]
    local_rows, width = tokens.shape
    block_len = local_rows // groups
    half_rows = local_rows // 2
    head_dim = head_norm_gains.shape[1]
    heads_local = query_weight.shape[1] // head_dim
    adapter_width = ADAPTER_COUNT * ADAPTER_RANK
    model_block = width // count_ctx
    hidden_slice = gate_weight.shape[1] // 4
    me = lax.axis_index("ctx")
    core = lax.axis_index("wt")

    spread_bits = list(range(3, bit_count)) + [0]
    team_place = (me >> 1) & 3

    def flip(value, bit):
        return lax.ppermute(value, "ctx", [(i, i ^ (1 << bit)) for i in range(count_ctx)])

    def other_core(value):
        return lax.ppermute(value, "wt", SWAP)

    def own_half(value):
        return lax.dynamic_slice_in_dim(value, core * half_rows, half_rows, 0)

    def other_half(value):
        return lax.dynamic_slice_in_dim(value, (1 - core) * half_rows, half_rows, 0)

    def both_halves(own, other):
        return jnp.where(
            core == 0, jnp.concatenate([own, other], axis=0), jnp.concatenate([other, own], axis=0)
        )

    def column_blocks(value, places):
        return jnp.concatenate(
            [
                lax.dynamic_slice_in_dim(value, place * model_block, model_block, 1)
                for place in places
            ],
            axis=1,
        )

    rest = count_ctx // 4
    rest_bits = list(range(2, bit_count))

    def rest_place(apart):
        return sum(((apart >> bit) & 1) << i for i, bit in enumerate(rest_bits))

    weight_order = [
        me
        ^ (
            (j // (2 * rest)) * 2
            + (j // rest) % 2
            + sum(((j >> i) & 1) << bit for i, bit in enumerate(rest_bits))
        )
        for j in range(count_ctx)
    ]
    weight_back = [
        (((d ^ me) >> 1) & 1) * 2 * rest + ((d ^ me) & 1) * rest + rest_place(d ^ me)
        for d in range(count_ctx)
    ]
    piece_masks = [0]
    for bit in spread_bits:
        piece_masks = piece_masks + [mask | (1 << bit) for mask in piece_masks]
    team_order = [me ^ mask ^ (2 * t) for mask in piece_masks for t in range(4)]
    team_back = [
        4 * sum((((b ^ me) >> bit) & 1) << i for i, bit in enumerate(spread_bits))
        + (((b ^ me) >> 1) & 3)
        for b in range(count_ctx)
    ]

    def to_member(value, member):
        if member == 0:
            return value
        return lax.ppermute(value, "ctx", [(d, d ^ (2 * member)) for d in range(count_ctx)])

    def team_split(shard):
        parts = [
            to_member(
                lax.dynamic_slice_in_dim(
                    shard, (team_place ^ member) * hidden_slice, hidden_slice, 1
                ),
                member,
            )
            for member in range(4)
        ]
        return joined(parts[0], parts[1]), joined(parts[2], parts[3])

    def joined(own, arrived):
        return jnp.concatenate([own, arrived], axis=0)

    prompt_blocks = PROMPT // block_len
    cont_blocks = CONT // block_len
    device_ids = jnp.arange(count_ctx, dtype=jnp.int32)
    block_of = jnp.sum(
        jnp.where(block_device[None] == device_ids[:, None, None], device_ids[None, None, :], 0),
        axis=2,
    )
    cont_of = (block_of - prompt_blocks) // cont_blocks
    pick_of = jnp.sum(
        jnp.where(
            cont_of[:, :, None] == jnp.arange(adapter_pick.shape[1], dtype=jnp.int32),
            adapter_pick[None],
            0,
        ),
        axis=2,
    )
    pick_of = jnp.where(block_of < prompt_blocks, -1, pick_of)
    compact = groups == 1 and count_ctx * 8 == adapter_width
    own_pick = jnp.maximum(jnp.sum(jnp.where(device_ids[:, None] == me, pick_of, 0), axis=0), 0)
    own_pick = own_pick[:1].astype(jnp.int32)
    grad_rows = ADAPTER_RANK if compact else adapter_width
    grad_type = BF16 if compact else F32

    def picks_at(device):
        return jnp.sum(jnp.where(device_ids[:, None] == device, pick_of, 0), axis=0)

    def select_rows(picks):
        rows = jnp.repeat(picks, block_len)
        return (
            jnp.arange(adapter_width, dtype=jnp.int32)[None, :] // ADAPTER_RANK == rows[:, None]
        ).astype(F32)

    select = select_rows(picks_at(me))
    select_own = own_half(select)
    team_select = [select_rows(picks_at(me ^ (2 * t))) for t in range(4)]
    select_near = jnp.concatenate([own_half(part) for part in team_select], axis=0)
    select_far = jnp.concatenate([other_half(part) for part in team_select], axis=0)

    my_block = jnp.sum(jnp.where(device_ids[:, None] == me, block_of, 0), axis=0)
    positions = (
        my_block[:, None] * block_len + jnp.arange(block_len, dtype=jnp.int32)[None, :]
    ).reshape(-1)
    seq_pos = jnp.where(positions < PROMPT, positions, PROMPT + (positions - PROMPT) % CONT)
    frequency = THETA ** (-2.0 * jnp.arange(head_dim // 2, dtype=F32) / head_dim)
    rotary_angles = seq_pos.astype(F32)[:, None] * frequency[None, :]
    cosine = jnp.cos(rotary_angles)[:, None, :]
    sine_term = jnp.sin(rotary_angles)[:, None, :]
    cont_start = prompt_blocks + (my_block - prompt_blocks) // cont_blocks * cont_blocks
    is_prompt = my_block < prompt_blocks
    visible_count = jnp.where(
        is_prompt, my_block + 1, prompt_blocks + my_block - cont_start + 1
    ).astype(jnp.int32)
    entries = jnp.arange(prompt_blocks + cont_blocks, dtype=jnp.int32)
    visible_block = jnp.where(
        is_prompt[:, None] | (entries < prompt_blocks)[None, :],
        entries[None, :],
        cont_start[:, None] + entries[None, :] - prompt_blocks,
    )
    visible_device = jnp.sum(
        jnp.where(
            visible_block[:, :, None] == device_ids[None, None, :], block_device[:, None, :], 0
        ),
        axis=2,
    )
    apart = visible_device ^ me
    key_slot = (((apart >> 1) & 1) * 2 + (apart & 1)) * rest + rest_place(apart)
    value_slot = ((apart & 1) * 2 + ((apart >> 1) & 1)) * rest + rest_place(apart)
    tables = (visible_count, key_slot.astype(jnp.int32), value_slot.astype(jnp.int32))

    gains = norm_gains.astype(F32)
    query_gain = head_norm_gains[0].astype(F32)
    key_gain = head_norm_gains[1].astype(F32)

    def query_piece(projected):
        return (
            rotary_applied(
                normalized(projected.reshape(local_rows, -1, head_dim), query_gain),
                cosine,
                sine_term,
            )
            * head_dim ** (-0.5)
        ).reshape(local_rows, -1)

    def key_piece(projected):
        return rotary_applied(
            normalized(projected.reshape(local_rows, -1, head_dim), key_gain), cosine, sine_term
        ).reshape(local_rows, -1)

    def value_piece(projected):
        return normalized(projected.reshape(local_rows, -1, head_dim), 1.0).reshape(local_rows, -1)

    def slab_product(value, slabs):
        middle = value.shape[1] // 2
        return product(value[:, :middle], slabs[0]) + product(value[:, middle:], slabs[1])

    def slab_against(value, slabs):
        return jnp.concatenate([against(value, slabs[0]), against(value, slabs[1])], axis=1)

    half = jnp.reshape(core, (1,)).astype(jnp.int32)
    aligned = model_block % 128 == 0
    style = dict(count=count_ctx, block=model_block, aligned=aligned)
    weight_order_table = jnp.stack(weight_order).astype(jnp.int32)
    weight_back_table = jnp.stack(weight_back).astype(jnp.int32)
    team_order_table = jnp.stack(team_order).astype(jnp.int32)
    half_spec = pl.BlockSpec((half_rows, width), lambda i, half, *_: (half[0], 0))
    wide_f32 = jax.ShapeDtypeStruct((half_rows, width), F32)
    wide_low = jax.ShapeDtypeStruct((half_rows, width), BF16)
    work_space = pltpu.VMEM((half_rows, width), F32)
    kept_space = pltpu.VMEM((adapter_width, width), F32)

    def moved(value, places):
        return value if aligned else column_blocks(value, places)

    def moved_back(value, places):
        if aligned:
            return value
        flat = value.reshape(-1, value.shape[-1])
        flat = jnp.concatenate([column_blocks(flat[:, :width], places), flat[:, width:]], axis=1)
        return flat.reshape(value.shape)

    first_shrink = jnp.concatenate([query_shrink, key_shrink, value_shrink], axis=0)
    first_moved, first_low, rank_first = whole_call(
        lambda *refs: first_kernel(*refs, **style),
        (tokens, gains, select, first_shrink),
        (
            jax.ShapeDtypeStruct(tokens.shape, BF16),
            jax.ShapeDtypeStruct(tokens.shape, BF16),
            jax.ShapeDtypeStruct((local_rows, 3 * adapter_width), BF16),
        ),
        tables=(weight_order_table,),
    )
    first_moved = moved(first_moved, weight_order)
    rank_query = rank_first[:, :adapter_width]
    rank_key = rank_first[:, adapter_width : 2 * adapter_width]
    rank_value = rank_first[:, 2 * adapter_width :]

    far_bits, near_bit = spread_bits[:-1], spread_bits[-1]
    x_bit, y_bit = 0, 1
    first_bit = rest_bits[0]
    sent_before = {}

    def queued(line, value, move, depth=2):
        earlier = sent_before.setdefault(line, [])
        if len(earlier) >= depth:
            value = lax.optimization_barrier((value, earlier[-depth]))[0]
        result = move(value)
        earlier.append(result)
        return result

    def over_x(value):
        return queued("x", value, lambda v: flip(v, x_bit))

    def over_y(value):
        return queued("y", value, lambda v: flip(v, y_bit))

    def over_rest(value, bits):
        for bit in bits:
            value = joined(value, queued("z", value, lambda v, bit=bit: flip(v, bit)))
        return value

    def spread_far(piece):
        pieces = [piece]
        for bit in far_bits:
            pieces = pieces + [queued("z", other, lambda v, bit=bit: flip(v, bit)) for other in pieces]
        return pieces[1:]

    def near(pieces):
        return [over_x(piece) for piece in pieces]

    step = lax.optimization_barrier
    kv_weight = jnp.concatenate([key_matrix, value_matrix], axis=1)
    out_rows, down_rows = out_weight.T, down_weight.T
    kv_part = joined(kv_weight, flip(kv_weight, first_bit))
    query_part = joined(query_weight, flip(query_weight, first_bit))
    out_part = joined(out_rows, flip(out_rows, first_bit))
    kv_part = over_rest(kv_part, rest_bits[1:])
    gate_a, gate_b = team_split(gate_weight)
    query_part = over_rest(query_part, rest_bits[1:])
    kv_slab = joined(kv_part, over_x(kv_part))
    kv_slab, gate_a, gate_b, up_weight, down_rows, out_part = step(
        (kv_slab, gate_a, gate_b, up_weight, down_rows, out_part)
    )
    kv_slabs = kv_slab, over_y(kv_slab)
    up_a, up_b = team_split(up_weight)
    query_slab = joined(query_part, over_x(query_part))
    gate_far_a = spread_far(gate_a)
    gate_near_a = near([gate_a])
    query_y_a = over_y(query_slab[: width // 4])
    kv_slabs, query_slab, gate_far_a, up_a, up_b = step((kv_slabs, query_slab, gate_far_a, up_a, up_b))

    kv_projected = slab_product(first_moved, kv_slabs)
    kv_width = key_matrix.shape[1]
    key_projected = kv_projected[:, :kv_width] + product(rank_key, key_widen_maps)
    value_projected = kv_projected[:, kv_width:] + product(rank_value, value_widen_maps)
    key_low = low(key_piece(key_projected)).reshape(1, groups, block_len, head_dim)
    value_low = low(value_piece(value_projected)).reshape(1, groups, block_len, head_dim)
    kv_part = jnp.stack([key_low, value_low], axis=1)
    gate_far_b = spread_far(gate_b)
    down_a, down_b = team_split(down_rows)
    kv_part, gate_far_b, gate_near_a, query_y_a, down_a, down_b, out_part = step(
        (kv_part, gate_far_b, gate_near_a, query_y_a, down_a, down_b, out_part)
    )
    for bit in rest_bits:
        kv_part = joined(kv_part, flip(kv_part, bit))
    out_part = over_rest(out_part, rest_bits[1:])
    query_y_b = over_y(query_slab[width // 4 :])
    gate_near_b = near([gate_b])
    gate_far_near_a = near(gate_far_a)
    kv_part, out_part, gate_near_b, gate_far_near_a, query_y_b = step(
        (kv_part, out_part, gate_near_b, gate_far_near_a, query_y_b)
    )
    key_part, value_part = kv_part[:, 0], kv_part[:, 1]
    key_x, value_y = flip(key_part, x_bit), flip(value_part, y_bit)
    up_far_a = spread_far(up_a)
    key_x, value_y, up_far_a = step((key_x, value_y, up_far_a))
    key_part = joined(key_part, key_x)
    value_part = joined(value_part, value_y)
    key_all = joined(key_part, flip(key_part, y_bit))
    value_all = joined(value_part, flip(value_part, x_bit))
    query_slabs = query_slab, joined(query_y_a, query_y_b)
    query_proj = slab_product(first_moved, query_slabs) + product(rank_query, query_expand)
    query_low = low(query_piece(query_proj))
    up_far_b = spread_far(up_b)
    out_slab = joined(out_part, over_x(out_part))
    key_all, value_all, query_low, up_far_b, out_slab = step(
        (key_all, value_all, query_low, up_far_b, out_slab)
    )
    out_slabs = out_slab, over_y(out_slab)
    down_far_a = spread_far(down_a)
    gate_far_near_b = near(gate_far_b)
    up_near_a = near([up_a])
    up_near_b = near([up_b])
    heads_low, lse = attend(tables, query_low, key_all, value_all, groups, heads_local, head_dim)

    heads_low, out_slabs, down_far_a, gate_far_near_b, up_near_a, up_near_b = step(
        (heads_low, out_slabs, down_far_a, gate_far_near_b, up_near_a, up_near_b)
    )
    down_far_b = spread_far(down_b)
    up_far_near_a = near(up_far_a)
    down_near_a, down_near_b = near([down_a]), near([down_b])
    attn_part = jnp.concatenate(
        [slab_against(heads_low, out_slabs), select * against(heads_low, out_shrink)], axis=1
    )
    attn_total, laurel_back, mid_stream, second_low, rank_out = whole_call(
        lambda *refs: middle_kernel(*refs, **style),
        (
            moved_back(own_half(attn_part), weight_back),
            moved_back(other_core(other_half(attn_part)), weight_back),
            tokens,
            gains,
            out_expand,
            laurel_left,
            laurel_right,
        ),
        (
            wide_f32,
            wide_f32,
            wide_f32,
            wide_low,
            jax.ShapeDtypeStruct((half_rows, adapter_width), BF16),
        ),
        scratch=(work_space,),
        tables=(half, weight_back_table),
        specs={2: half_spec},
    )

    second_low, down_far_b, up_far_near_a, down_near_a, down_near_b = step(
        (second_low, down_far_b, up_far_near_a, down_near_a, down_near_b)
    )
    up_far_near_b = near(up_far_b)
    down_far_near_a, down_far_near_b = near(down_far_a), near(down_far_b)

    def in_order(own, far, near_own, near_far):
        first, second = ([o] + f + n + nf for o, f, n, nf in zip(own, far, near_own, near_far))
        return [piece for pair in zip(first, second) for piece in pair]

    gate_pieces = in_order(
        (gate_a, gate_b),
        (gate_far_a, gate_far_b),
        (gate_near_a, gate_near_b),
        (gate_far_near_a, gate_far_near_b),
    )
    up_pieces = in_order(
        (up_a, up_b), (up_far_a, up_far_b), (up_near_a, up_near_b), (up_far_near_a, up_far_near_b)
    )
    down_pieces = in_order(
        (down_a, down_b),
        (down_far_a, down_far_b),
        (down_near_a, down_near_b),
        (down_far_near_a, down_far_near_b),
    )

    def team_gather(value):
        near_parts = [to_member(value, member) for member in range(4)]
        return near_parts, [other_core(part) for part in near_parts]

    def team_sum(near_part, far_part):
        arrived = other_core(far_part).astype(F32)
        parts = []
        for member in (3, 1, 2, 0):
            rows = slice(member * half_rows, (member + 1) * half_rows)
            parts.append(to_member(low(near_part[rows] + arrived[rows]), member))
        return parts

    def hidden_columns(value):
        return lax.dynamic_slice_in_dim(value, team_place * hidden_slice, hidden_slice, 1)

    feed_maps = moved(jnp.concatenate([gate_shrink, up_shrink], axis=0), team_order)
    down_map = moved(down_expand, team_order)
    slices = tuple(hidden_columns(value) for value in (gate_expand, up_expand, down_shrink))
    pieces = (gate_pieces, up_pieces, down_pieces)

    second_near, second_far = team_gather(moved(second_low, team_order))
    *kept_far, part_far = feed(
        team_order_table, second_far, select_far, feed_maps, *slices, *pieces, BF16
    )
    *kept_near, part_near = feed(
        team_order_table, second_near, select_near, feed_maps, *slices, *pieces, F32
    )
    ffn_parts = team_sum(part_near, part_far)

    result_own, layer_input_own, grad_after, grad_ffn, down_expand_grad = whole_call(
        layer_kernel,
        (
            *(moved_back(part, team_back) for part in ffn_parts),
            mid_stream,
            gains,
            down_expand,
            layer_gate,
            layer_lift,
            layer_input,
            out_grad,
        ),
        (
            wide_low,
            jax.ShapeDtypeStruct((half_rows, layer_input.shape[1]), F32),
            wide_f32,
            wide_low,
            jax.ShapeDtypeStruct((grad_rows, width), grad_type),
        ),
        scratch=(kept_space,),
        tables=(half, own_pick),
        specs={
            9: pl.BlockSpec((half_rows, layer_input.shape[1]), lambda i, half, *_: (half[0], 0)),
            10: half_spec,
        },
    )

    grad_near, grad_far = team_gather(moved(grad_ffn, team_order))
    nothing = jnp.zeros((3, adapter_width, hidden_slice), F32)
    back_far, team_grads = feed_back(
        team_order_table, grad_far, select_far, down_map, nothing, kept_far, *slices, *pieces, BF16
    )
    back_near, team_grads = feed_back(
        team_order_table, grad_near, select_near, down_map, team_grads, kept_near, *slices, *pieces, F32
    )
    second_parts = team_sum(back_near, back_far)
    grad_sent, grad_scaled, grad_first, own_grads = whole_call(
        lambda *refs: turn_kernel(*refs, **style),
        (
            *(moved_back(part, team_back) for part in second_parts),
            mid_stream,
            grad_after,
            attn_total,
            laurel_back,
            second_low,
            gains,
            gate_shrink,
            up_shrink,
            laurel_right,
            laurel_left,
            out_expand,
            rank_out,
            select_own,
        ),
        (
            jax.ShapeDtypeStruct((half_rows, width + adapter_width), BF16),
            wide_f32,
            wide_f32,
            jax.ShapeDtypeStruct((3, grad_rows, width), grad_type),
        ),
        scratch=(work_space, kept_space),
        tables=(weight_order_table, own_pick),
    )
    if not aligned:
        grad_sent = jnp.concatenate(
            [column_blocks(grad_sent[:, :width], weight_order), grad_sent[:, width:]], axis=1
        )
    grad_joined = both_halves(grad_sent, other_core(grad_sent))
    grad_attn = grad_joined[:, :width]
    grad_rank_out = grad_joined[:, width:]
    out_shrink_grad = summed(grad_rank_out, heads_low)
    grad_heads = low(slab_product(grad_attn, out_slabs) + product(grad_rank_out, out_shrink))

    grad_queries, keys_near, keys_far, values_near, values_far = attend_back(
        tables, query_low, key_all, value_all, heads_low, lse, grad_heads, groups, heads_local, head_dim
    )

    keys_come, values_come = flip(keys_far, y_bit), flip(values_far, x_bit)
    keep = keys_near.shape[0] // 2

    def sum_of(own, arrived, rows):
        return low(own[rows].astype(F32) + arrived[rows])

    keys_far = flip(sum_of(keys_near, keys_come, slice(keep, None)), x_bit)
    values_far = flip(sum_of(values_near, values_come, slice(keep, None)), y_bit)
    near_rows = slice(None, keep)
    grad_keys = low(keys_near[near_rows].astype(F32) + keys_come[near_rows] + keys_far)
    grad_values = low(values_near[near_rows].astype(F32) + values_come[near_rows] + values_far)

    def collect(value):
        total = value[0].astype(F32)
        for i in range(1, rest):
            mask = sum(((i >> j) & 1) << bit for j, bit in enumerate(rest_bits))
            total = total + lax.ppermute(
                value[i], "ctx", [(d, d ^ mask) for d in range(count_ctx)]
            )
        return total.reshape(local_rows, -1)

    grad_kv_own = jnp.concatenate([collect(grad_keys), collect(grad_values)], axis=1)

    grad_query_proj = low(jax.vjp(query_piece, query_proj)[1](grad_queries)[0])
    grad_key_proj = low(jax.vjp(key_piece, key_projected)[1](grad_kv_own[:, :head_dim])[0])
    grad_value_proj = low(jax.vjp(value_piece, value_projected)[1](grad_kv_own[:, head_dim:])[0])
    query_expand_grad = summed(rank_query, grad_query_proj)
    key_expand_grad = summed(rank_key, grad_key_proj)
    value_expand_grad = summed(rank_value, grad_value_proj)
    grad_kv_proj = jnp.concatenate([grad_key_proj, grad_value_proj], axis=1)
    first_part = jnp.concatenate(
        [
            slab_against(grad_query_proj, query_slabs) + slab_against(grad_kv_proj, kv_slabs),
            select * against(grad_query_proj, query_expand),
            select * against(grad_key_proj, key_widen_maps),
            select * against(grad_value_proj, value_widen_maps),
        ],
        axis=1,
    )
    input_own, first_grads = whole_call(
        lambda *refs: last_kernel(*refs, **style),
        (
            moved_back(own_half(first_part), weight_back),
            moved_back(other_core(low(other_half(first_part))), weight_back),
            tokens,
            gains,
            grad_scaled,
            grad_first,
            first_shrink,
        ),
        (wide_f32, jax.ShapeDtypeStruct((3, grad_rows, width), grad_type)),
        scratch=(work_space, work_space, kept_space),
        tables=(half, weight_back_table, own_pick),
        specs={2: half_spec},
    )

    def scatter_split(grads):
        rows = adapter_width // count_ctx
        joined = low(jnp.concatenate(grads, axis=1))
        parts = joined.reshape(count_ctx, rows, joined.shape[1])
        parts = lax.all_to_all(parts, "ctx", 0, 0, tiled=True)
        total = jnp.sum(parts.astype(F32), axis=0)
        cuts, start = [], 0
        for grad in grads:
            cuts.append(total[:, start : start + grad.shape[1]])
            start += grad.shape[1]
        return cuts

    def scatter_team(grads):
        rows = adapter_width // count_ctx
        joined = low(grads).reshape(3, count_ctx, rows, hidden_slice)
        parts = joined.transpose(1, 0, 2, 3).reshape(count_ctx, 3 * rows, hidden_slice)
        parts = lax.all_to_all(parts, "ctx", 0, 0, tiled=True)
        teams = [
            sum(parts[i].astype(F32) for i in range(count_ctx) if (i >> 1) & 3 == t)
            for t in range(4)
        ]
        total = jnp.concatenate(teams, axis=1)
        return [total[i * rows : (i + 1) * rows] for i in range(3)]

    def scatter_shared(grads):
        rows = adapter_width // (2 * count_ctx)
        shaped = grads.reshape(grads.shape[0], count_ctx, 2, rows, width)
        keep = lax.dynamic_index_in_dim(shaped, core, 2, keepdims=False)
        send = lax.dynamic_index_in_dim(shaped, 1 - core, 2, keepdims=False)
        joined = low(keep + other_core(low(send)).astype(F32))
        parts = joined.transpose(1, 0, 2, 3).reshape(count_ctx, grads.shape[0] * rows, width)
        parts = lax.all_to_all(parts, "ctx", 0, 0, tiled=True)
        total = jnp.sum(parts.astype(F32), axis=0)
        return [total[i * rows : (i + 1) * rows] for i in range(grads.shape[0])]

    def one_adapter(grad):
        return low(lax.dynamic_slice_in_dim(grad, own_pick[0] * ADAPTER_RANK, ADAPTER_RANK, 0))

    def core_rows(grads):
        shaped = grads.reshape(grads.shape[0], 2, 2, 4, width)
        keep = lax.dynamic_index_in_dim(shaped, core, 2, keepdims=False).astype(F32)
        send = lax.dynamic_index_in_dim(shaped, 1 - core, 2, keepdims=False)
        return low(keep + other_core(send)).transpose(1, 0, 2, 3).reshape(2, -1, width)

    def deliver(load):
        loads = [load] + [
            lax.ppermute(load, "ctx", [(d, d ^ (4 * r)) for d in range(count_ctx)])
            for r in range(1, count_ctx // 4)
        ]
        picks = [
            jnp.sum(jnp.where(device_ids == (me ^ (4 * r)), pick_of[:, 0], 0))
            for r in range(count_ctx // 4)
        ]
        total = 0.0
        for m in (3, 1, 2, 0):
            place = (me & 3) ^ m
            wanted = (me >> 2) * 2 + (place >> 1)
            sent = sum(
                jnp.where(
                    pick == wanted,
                    lax.dynamic_index_in_dim(each, place & 1, 0, keepdims=False).astype(F32),
                    0.0,
                )
                for pick, each in zip(picks, loads)
            )
            if m:
                sent = lax.ppermute(low(sent), "ctx", [(d, d ^ m) for d in range(count_ctx)])
            total = total + sent.astype(F32)
        return total

    gate_expand_out, up_expand_out, down_shrink_out = scatter_team(team_grads)
    if compact:
        shared = core_rows(jnp.concatenate([own_grads, down_expand_grad[None]], axis=0))
        split = one_adapter(out_shrink_grad).reshape(2, 8, -1)
        split = jnp.pad(split, ((0, 0), (0, 0), (0, width - split.shape[2])))
        found = deliver(jnp.concatenate([shared, split], axis=1))
        gate_shrink_out, up_shrink_out, out_expand_out, down_expand_out = (
            found[4 * i : 4 * i + 4] for i in range(4)
        )
        out_shrink_out = found[16:, : out_shrink_grad.shape[1]]
        expands = [one_adapter(g) for g in (query_expand_grad, key_expand_grad, value_expand_grad)]
        sizes = [g.shape[1] for g in expands]
        split = jnp.concatenate(expands, axis=1).reshape(2, 8, -1)
        split = jnp.pad(split, ((0, 0), (0, 0), (0, width - split.shape[2])))
        found = deliver(jnp.concatenate([core_rows(first_grads), split], axis=1))
        query_shrink_out, key_shrink_out, value_shrink_out = (
            found[4 * i : 4 * i + 4] for i in range(3)
        )
        query_expand_out = found[12:, : sizes[0]]
        key_expand_out = found[12:, sizes[0] : sizes[0] + sizes[1]]
        value_expand_out = found[12:, sizes[0] + sizes[1] : sum(sizes)]
    else:
        (out_shrink_out,) = scatter_split([out_shrink_grad])
        gate_shrink_out, up_shrink_out, out_expand_out, down_expand_out = scatter_shared(
            jnp.concatenate([own_grads, down_expand_grad[None]], axis=0)
        )
        query_expand_out, key_expand_out, value_expand_out = scatter_split(
            [query_expand_grad, key_expand_grad, value_expand_grad]
        )
        query_shrink_out, key_shrink_out, value_shrink_out = scatter_shared(first_grads)

    return (
        both_halves(result_own, other_core(result_own)),
        both_halves(input_own, other_core(input_own)),
        both_halves(layer_input_own, other_core(layer_input_own)),
        query_shrink_out,
        key_shrink_out,
        value_shrink_out,
        gate_shrink_out,
        up_shrink_out,
        out_shrink_out,
        down_shrink_out,
        query_expand_out,
        key_expand_out,
        value_expand_out,
        gate_expand_out,
        up_expand_out,
        out_expand_out,
        down_expand_out,
    )


def solution(mesh):
    in_specs = (
        P("ctx", None),
        P("ctx", None),
        P("ctx", None),
        P(),
        P(),
        P(),
        P(),
        P("ctx", "wt"),
        P("ctx", "wt"),
        P("ctx", "wt"),
        P("ctx", "wt"),
        P("ctx", "wt"),
        P("wt", "ctx"),
        P("wt", "ctx"),
        P(),
        P(),
        P(),
        P(),
        P(),
        P(),
        P(),
        P(),
        P(),
        P(None, "wt"),
        P(None, "wt"),
        P(None, "wt"),
        P(None, "wt"),
        P(None, "wt"),
        P(None, "wt"),
        P(None, "wt"),
        P(),
        P(),
    )
    out_specs = (
        P("ctx", None),
        P("ctx", None),
        P("ctx", None),
        P(("ctx", "wt"), None),
        P(("ctx", "wt"), None),
        P(("ctx", "wt"), None),
        P(("ctx", "wt"), None),
        P(("ctx", "wt"), None),
        P("ctx", "wt"),
        P("ctx", "wt"),
        P("ctx", "wt"),
        P("ctx", "wt"),
        P("ctx", "wt"),
        P("ctx", "wt"),
        P("ctx", "wt"),
        P(("ctx", "wt"), None),
        P(("ctx", "wt"), None),
    )
    return jax.shard_map(local, mesh=mesh, in_specs=in_specs, out_specs=out_specs, check_vma=False)
```

time: 1100 us -> 784 us (0.71)
  matrix products: 207 us -> 20.7 us
  local copies, waits for them, and re-layouts: 234 us -> 49.8 us
  Pallas kernels: 25.4 us -> 133 us
  waiting for transfers between devices: 397 us -> 373 us
  other arithmetic: 91.1 us -> 72.8 us
  starting transfers between devices: 121 us -> 109 us
    unnamed x631 -> x246, local copies, waits for them, and re-layouts: 166 us -> 18.3 us
    ppermute x0 -> x39, waiting for transfers between devices: none -> 143 us  [the longest x21 109 us: to_member(): lax.ppermute(value, 'ctx', [(d, d ^ 2 * member) for d in range(count_ctx)])]
    all_to_all x13 -> x0, waiting for transfers between devices: 137 us -> none  [the longest x2 45 us: team_sum(): lax.all_to_all(total, 'ctx', 0, 0, axis_index_groups=team_groups, tiled=T...]
    pallas_call x0 -> x9, Pallas kernels: none -> 112 us  [the longest x4 81.2 us: feed_call(): pl.pallas_call(lambda *refs: kernel(*refs, pieces=len(weights[0]), width=...]
    dot_general x51 -> x10, matrix products: 95.7 us -> 9.28 us  [against(): lax.dot_general(left_side, right_side, (((1,), (1,)), ((), ())), preferre...]
    dot_general x50 -> x10, matrix products: 94.8 us -> 10.5 us  [product(): return jnp.dot(left_side, right_side, preferred_element_type=F32)]
    all_to_all x13 -> x0, starting transfers between devices: 68.9 us -> none  [the longest x2 13.7 us: scatter_shared(): parts = lax.all_to_all(parts, 'ctx', 0, 0, tiled=True)]
    ppermute x0 -> x39, starting transfers between devices: none -> 51.3 us  [the longest x21 29.4 us: to_member(): lax.ppermute(value, 'ctx', [(d, d ^ 2 * member) for d in range(count_ctx)])]
  transfers between devices with their start and end apart: 55 -> 99, of which waited for: 29 -> 48; matrix products, arithmetic and copies ran while one was open for 35% -> 14% of each run, Pallas kernels for 1% -> 9%
where the time goes in v2:
time: 784 us; the launch traced here: 773 us
  waiting for transfers between devices  373 us (48%)
  Pallas kernels  133 us (17%)
  starting transfers between devices  109 us (14%)
  other arithmetic  72.8 us (9%)
  local copies, waits for them, and re-layouts  49.8 us (6%)
  matrix products  20.7 us (3%)
  between operations  15.1 us (2%)
    ppermute x41, waiting for transfers between devices, flip(): lax.ppermute(value, 'ctx', [(i, i ^ 1 << bit) for i in range(count_ctx)])  225 us
    ppermute x21, waiting for transfers between devices, to_member(): lax.ppermute(value, 'ctx', [(d, d ^ 2 * member) for d in range(count_ctx)])  109 us
    pallas_call x4, Pallas kernels, feed_call(): pl.pallas_call(lambda *refs: kernel(*refs, pieces=len(weights[0]), width=...  81.2 us
    ppermute x41, starting transfers between devices, flip(): lax.ppermute(value, 'ctx', [(i, i ^ 1 << bit) for i in range(count_ctx)])  50.3 us
    pallas_call x5, Pallas kernels, whole_call(): pl.pallas_call(kernel, grid_spec=pltpu.PrefetchScalarGridSpec(num_scalar_...  30.7 us
    ppermute x21, starting transfers between devices, to_member(): lax.ppermute(value, 'ctx', [(d, d ^ 2 * member) for d in range(count_ctx)])  29.4 us
    concatenate x20, other arithmetic, joined(): return jnp.concatenate([own, arrived], axis=0)  27.9 us
    unnamed x246, local copies, waits for them, and re-layouts  18.3 us
  transfers between devices with their start and end apart: 99, of which 48 were waited for; matrix products, arithmetic and copies ran while one was open for 14% of the time, Pallas kernels for 9%

profile of v2, /device:TPU:16, one launch (start us, length us, event | category | flops | bytes accessed | tf_op | source)
XLA Modules:
  0.0 773.1 jit_solution(13931122519621610136)
XLA Ops:
  24.1 11.7 %collective-permute-done.8 = bf16[128,1024]{1,0:T(8,128)(2,1)S(1)} collective-permute-done((bf16[128,1024]{1,0:T(8,128)(2,1)S(1)}, bf16[128,1024]{1,0:T(8,128)(2,1)S(1)}, u32[]{:S(2)}, u32[]{:S(2)}) %collective-permute-start.8) | collective-permute-done | bytes 262176 | tf_op jit(solution)/shard_map/ppermute | solution.py:666
  46.6 13.3 %collective-permute-done.9 = bf16[256,1024]{1,0:T(8,128)(2,1)S(1)} collective-permute-done((bf16[256,1024]{1,0:T(8,128)(2,1)S(1)}, bf16[256,1024]{1,0:T(8,128)(2,1)S(1)}, u32[]{:S(2)}, u32[]{:S(2)}) %collective-permute-start.9) | collective-permute-done | bytes 524320 | tf_op jit(solution)/shard_map/ppermute | solution.py:666
  89.2 20.8 %collective-permute-done.12 = bf16[128,1024]{1,0:T(8,128)(2,1)} collective-permute-done((bf16[128,1024]{1,0:T(8,128)(2,1)}, bf16[128,1024]{1,0:T(8,128)(2,1)}, u32[]{:S(2)}, u32[]{:S(2)}) %collective-permute-start.12) | collective-permute-done | bytes 262176 | tf_op jit(solution)/shard_map/ppermute | solution.py:723
  122.5 23.8 %collective-permute-done.11.refs_12_.refs_17_ = bf16[256,1024]{1,0:T(8,128)(2,1)S(1)} collective-permute-done((bf16[256,1024]{1,0:T(8,128)(2,1)S(1)}, bf16[256,1024]{1,0:T(8,128)(2,1)S(1)}, u32[]{:S(2)}, u32[]{:S(2)}) %collective-permute-start.11) | collective-permute-done | bytes 524320 | tf_op jit(solution)/shard_map/ppermute | solution.py:666
  162.3 7.4 collective-permute-done.21
  175.4 21.7 %collective-permute-done.23 = bf16[256,1024]{0,1:T(8,128)(2,1)S(1)} collective-permute-done((bf16[256,1024]{0,1:T(8,128)(2,1)S(1)}, bf16[256,1024]{0,1:T(8,128)(2,1)S(1)}, u32[]{:S(2)}, u32[]{:S(2)}) %collective-permute-start.23) | collective-permute-done | bytes 524320 | tf_op jit(solution)/shard_map/ppermute | solution.py:666
  201.5 18.0 %collective-permute-done.22 = bf16[2,2,1,256,256]{4,3,0,2,1:T(8,128)(2,1)S(1)} collective-permute-done((bf16[2,2,1,256,256]{4,3,0,2,1:T(8,128)(2,1)S(1)}, bf16[2,2,1,256,256]{4,3,0,2,1:T(8,128)(2,1)S(1)}, u32[]{:S(2)}, u32[]{:S(2)}) %collective-permute-start.22) | collective-permute-done | bytes 524320 | tf_op jit(solution)/shard_map/ppermute | solution.py:666
  233.0 9.1 %collective-permute-done.29.refs_20_.refs_25_ = bf16[256,1024]{1,0:T(8,128)(2,1)} collective-permute-done((bf16[256,1024]{1,0:T(8,128)(2,1)}, bf16[256,1024]{1,0:T(8,128)(2,1)}, u32[]{:S(2)}, u32[]{:S(2)}) %collective-permute-start.29) | collective-permute-done | bytes 524320 | tf_op jit(solution)/shard_map/ppermute | solution.py:666
  242.1 15.0 %collective-permute-done.27 = bf16[4,1,256,256]{3,2,0,1:T(8,128)(2,1)} collective-permute-done((bf16[4,1,256,256]{3,2,0,1:T(8,128)(2,1)S(1)}, bf16[4,1,256,256]{3,2,0,1:T(8,128)(2,1)}, u32[]{:S(2)}, u32[]{:S(2)}) %collective-permute-start.27) | collective-permute-done | bytes 524320 | tf_op jit(solution)/shard_map/ppermute | solution.py:666
  268.8 12.3 %collective-permute-done.31 = bf16[8,1,256,256]{3,2,1,0:T(8,128)(2,1)} collective-permute-done((bf16[8,1,256,256]{3,2,1,0:T(8,128)(2,1)}, bf16[8,1,256,256]{3,2,1,0:T(8,128)(2,1)}, u32[]{:S(2)}, u32[]{:S(2)}) %collective-permute-start.31) | collective-permute-done | bytes 1048608 | tf_op jit(solution)/shard_map/ppermute | solution.py:666
  291.8 8.0 %collective-permute-done.36.refs_17_.refs_22_ = bf16[256,1024]{1,0:T(8,128)(2,1)S(1)} collective-permute-done((bf16[256,1024]{1,0:T(8,128)(2,1)S(1)}, bf16[256,1024]{1,0:T(8,128)(2,1)S(1)}, u32[]{:S(2)}, u32[]{:S(2)}) %collective-permute-start.36) | collective-permute-done | bytes 524320 | tf_op jit(solution)/shard_map/ppermute | solution.py:666
  319.6 10.8 %collective-permute-done.34 = bf16[1024,1024]{0,1:T(8,128)(2,1)} collective-permute-done((bf16[1024,1024]{0,1:T(8,128)(2,1)}, bf16[1024,1024]{0,1:T(8,128)(2,1)}, u32[]{:S(2)}, u32[]{:S(2)}) %collective-permute-start.34) | collective-permute-done | bytes 2097184 | tf_op jit(solution)/shard_map/ppermute | solution.py:666
  339.2 13.0 %collective-permute-done.41.refs_24_.refs_29_ = bf16[256,1024]{1,0:T(8,128)(2,1)} collective-permute-done((bf16[256,1024]{1,0:T(8,128)(2,1)}, bf16[256,1024]{1,0:T(8,128)(2,1)}, u32[]{:S(2)}, u32[]{:S(2)}) %collective-permute-start.41) | collective-permute-done | bytes 524320 | tf_op jit(solution)/shard_map/ppermute | solution.py:666
  355.4 8.0 %collective-permute-done.42.refs_30_.refs_35_ = bf16[256,1024]{1,0:T(8,128)(2,1)} collective-permute-done((bf16[256,1024]{1,0:T(8,128)(2,1)S(1)}, bf16[256,1024]{1,0:T(8,128)(2,1)}, u32[]{:S(2)}, u32[]{:S(2)}) %collective-permute-start.42) | collective-permute-done | bytes 524320 | tf_op jit(solution)/shard_map/ppermute | solution.py:666
  364.2 10.5 %collective-permute-done.43.refs_31_.refs_36_ = bf16[256,1024]{1,0:T(8,128)(2,1)} collective-permute-done((bf16[256,1024]{1,0:T(8,128)(2,1)}, bf16[256,1024]{1,0:T(8,128)(2,1)}, u32[]{:S(2)}, u32[]{:S(2)}) %collective-permute-start.43) | collective-permute-done | bytes 524320 | tf_op jit(solution)/shard_map/ppermute | solution.py:666
  388.3 8.4 %collective-permute-done.48.refs_32_.refs_37_ = bf16[256,1024]{1,0:T(8,128)(2,1)S(1)} collective-permute-done((bf16[256,1024]{1,0:T(8,128)(2,1)}, bf16[256,1024]{1,0:T(8,128)(2,1)S(1)}, u32[]{:S(2)}, u32[]{:S(2)}) %collective-permute-start.48) | collective-permute-done | bytes 524320 | tf_op jit(solution)/shard_map/ppermute | solution.py:666
  397.9 8.7 %collective-permute-done.46.refs_4_ = bf16[128,2048]{1,0:T(8,128)(2,1)} collective-permute-done((bf16[128,2048]{1,0:T(8,128)(2,1)}, bf16[128,2048]{1,0:T(8,128)(2,1)}, u32[]{:S(2)}, u32[]{:S(2)}) %collective-permute-start.46) | collective-permute-done | bytes 524320 | tf_op jit(solution)/shard_map/ppermute | solution.py:723
  411.4 19.8 %shard_map.441 = (bf16[512,256]{1,0:T(8,128)(2,1)}, bf16[512,1024]{1,0:T(8,128)(2,1)}, bf16[512,1024]{1,0:T(8,128)(2,1)}, bf16[512,1024]{1,0:T(8,128)(2,1)}, bf16[512,2176]{1,0:T(8,128)(2,1)}) custom-call(s32[16]{0:T(128)} %stack.158.refs_0_, bf16[128,2048]{1,0:T(8,128)(2,1)} %collective-permute-done.50.refs_1_, ...), custom_call_target="tpu_custom_call" | custom-call | flops 6442450944 | bytes 20971520 | tf_op jit(solution)/shard_map/pallas_call | solution.py:501
  431.2 20.2 %shard_map.440 = (bf16[512,256]{1,0:T(8,128)(2,1)}, bf16[512,1024]{1,0:T(8,128)(2,1)}, bf16[512,1024]{1,0:T(8,128)(2,1)}, bf16[512,1024]{1,0:T(8,128)(2,1)}, f32[512,2176]{1,0:T(8,128)}) custom-call(s32[16]{0:T(128)} %stack.158.refs_0_, bf16[128,2048]{1,0:T(8,128)(2,1)} %get-tuple-element.176.refs_1_.refs_10_, ...), custom_call_target="tpu_custom_call" | custom-call | flops 6442450944 | bytes 20971520 | tf_op jit(solution)/shard_map/pallas_call | solution.py:501
  459.3 12.5 %collective-permute-done.55.near_ref = bf16[128,2176]{1,0:T(8,128)(2,1)S(1)} collective-permute-done((bf16[128,2176]{1,0:T(8,128)(2,1)}, bf16[128,2176]{1,0:T(8,128)(2,1)S(1)}, u32[]{:S(2)}, u32[]{:S(2)}) %collective-permute-start.55) | collective-permute-done | bytes 557088 | tf_op jit(solution)/shard_map/ppermute | solution.py:723
  471.9 11.4 %collective-permute-done.56.y_ref = bf16[128,2176]{1,0:T(8,128)(2,1)S(1)} collective-permute-done((bf16[128,2176]{1,0:T(8,128)(2,1)}, bf16[128,2176]{1,0:T(8,128)(2,1)S(1)}, u32[]{:S(2)}, u32[]{:S(2)}) %collective-permute-start.56) | collective-permute-done | bytes 557088 | tf_op jit(solution)/shard_map/ppermute | solution.py:723
  494.3 10.6 %collective-permute-done.59.refs_2_ = bf16[128,2048]{1,0:T(8,128)(2,1)S(1)} collective-permute-done((bf16[128,2048]{1,0:T(8,128)(2,1)}, bf16[128,2048]{1,0:T(8,128)(2,1)S(1)}, u32[]{:S(2)}, u32[]{:S(2)}) %collective-permute-start.59) | collective-permute-done | bytes 524320 | tf_op jit(solution)/shard_map/ppermute | solution.py:723
  506.9 10.4 %collective-permute-done.61.refs_4_ = bf16[128,2048]{1,0:T(8,128)(2,1)S(1)} collective-permute-done((bf16[128,2048]{1,0:T(8,128)(2,1)}, bf16[128,2048]{1,0:T(8,128)(2,1)S(1)}, u32[]{:S(2)}, u32[]{:S(2)}) %collective-permute-start.61) | collective-permute-done | bytes 524320 | tf_op jit(solution)/shard_map/ppermute | solution.py:723
  520.6 20.4 %shard_map.443 = (bf16[512,2304]{1,0:T(8,128)(2,1)}, f32[3,128,1024]{2,1,0:T(8,128)}) custom-call(s32[16]{0:T(128)} %stack.158.refs_0_, bf16[128,2048]{1,0:T(8,128)(2,1)} %copy-done.110, bf16[128,2048]{1,0:T(8,128)(2,1)} %copy-done.111, bf16[128,2048]{1,0:T(8,128)(2,1)} %copy-done.112, bf16[128,2048]{1,0:T(8,128)(2,1)} %copy-done.113, ...), custom_call_target="tpu_custom_call" | custom-call | flops 6442450944 | bytes 20971520 | tf_op jit(solution)/shard_map/pallas_call | solution.py:501
  541.6 20.8 %shard_map.444 = (f32[512,2304]{1,0:T(8,128)}, f32[3,128,1024]{2,1,0:T(8,128)}) custom-call(s32[16]{0:T(128)} %stack.158.refs_0_, bf16[128,2048]{1,0:T(8,128)(2,1)} %get-tuple-element.197.refs_1_, bf16[128,2048]{1,0:T(8,128)(2,1)} %copy-done.107, bf16[128,2048]{1,0:T(8,128)(2,1)} %copy-done.108, bf16[128,2048]{1,0:T(8,128)(2,1)} %copy-done.109, ...), custom_call_target="tpu_custom_call" | custom-call | flops 6442450944 | bytes 20971520 | tf_op jit(solution)/shard_map/pallas_call | solution.py:501
  591.0 13.6 %collective-permute-done.67.refs_2_ = bf16[128,2304]{1,0:T(8,128)(2,1)S(1)} collective-permute-done((bf16[128,2304]{1,0:T(8,128)(2,1)}, bf16[128,2304]{1,0:T(8,128)(2,1)S(1)}, u32[]{:S(2)}, u32[]{:S(2)}) %collective-permute-start.67) | collective-permute-done | bytes 589856 | tf_op jit(solution)/shard_map/ppermute | solution.py:723
  604.7 12.3 %collective-permute-done.68.refs_3_ = bf16[128,2304]{1,0:T(8,128)(2,1)} collective-permute-done((bf16[128,2304]{1,0:T(8,128)(2,1)}, bf16[128,2304]{1,0:T(8,128)(2,1)}, u32[]{:S(2)}, u32[]{:S(2)}) %collective-permute-start.68) | collective-permute-done | bytes 589856 | tf_op jit(solution)/shard_map/ppermute | solution.py:723
  617.0 7.9 %shard_map.445 = (bf16[128,2176]{1,0:T(8,128)(2,1)}, f32[128,2048]{1,0:T(8,128)}, f32[128,2048]{1,0:T(8,128)}, bf16[3,16,2048]{2,1,0:T(8,128)(2,1)}) custom-call(s32[16]{0:T(128)} %stack.185.refs_0_, s32[1]{0:T(128)} %bitcast.3.pick_ref.refs_1_.refs_2_, bf16[128,2304]{1,0:T(8,128)(2,1)} %copy-done.47, bf16[128,2304]{1,0:T(8,128)(2,1)} %collective-permute-done.68.refs_3_, ...), custom_call_target="tpu_custom_call" | custom-call | flops 1000000000 | bytes 9322496 | tf_op jit(solution)/shard_map/pallas_call | solution.py:249
  639.8 15.2 %shard_map.446 = (f32[256,1024]{1,0:T(8,128)S(1)}, bf16[8,1,256,256]{3,2,1,0:T(8,128)(2,1)S(1)}, bf16[8,1,256,256]{3,2,1,0:T(8,128)(2,1)}, bf16[8,1,256,256]{3,2,1,0:T(8,128)(2,1)S(1)}, bf16[8,1,256,256]{3,2,1,0:T(8,128)(2,1)}) custom-call(s32[1]{0:T(128)} %bitcast.36.refs_0_, s32[1,9]{1,0:T(1,128)S(1)} %get-tuple-element.300.refs_1_, ...), custom_call_target="tpu_custom_call" | custom-call | flops 6039797760 | bytes 12582912 | tf_op jit(solution)/shard_map/pallas_call | solution.py:194
  691.8 7.6 collective-permute-done.72
  709.8 11.4 %collective-permute-done.75 = bf16[1,256,256]{2,1,0:T(8,128)(2,1)S(1)} collective-permute-done((bf16[1,256,256]{2,1,0:T(8,128)(2,1)S(1)}, bf16[1,256,256]{2,1,0:T(8,128)(2,1)S(1)}, u32[]{:S(2)}, u32[]{:S(2)}) %collective-permute-start.75) | collective-permute-done | bytes 131104 | tf_op jit(solution)/shard_map/ppermute | solution.py:1154
  748.6 7.9 %collective-permute-done.86 = bf16[2,20,2048]{2,1,0:T(8,128)(2,1)S(1)} collective-permute-done((bf16[2,20,2048]{2,1,0:T(8,128)(2,1)S(1)}, bf16[2,20,2048]{2,1,0:T(8,128)(2,1)S(1)}, u32[]{:S(2)}, u32[]{:S(2)}) %collective-permute-start.86) | collective-permute-done | bytes 163872 | tf_op jit(solution)/shard_map/ppermute | solution.py:1240
  (592 shorter events, 335.4 us)
Async XLA Ops:
  3.1 40.8 %collective-permute-start.4 = (bf16[128,1024]{1,0:T(8,128)(2,1)}, bf16[128,1024]{1,0:T(8,128)(2,1)}, u32[]{:S(2)}, u32[]{:S(2)}) collective-permute-start(bf16[128,1024]{1,0:T(8,128)(2,1)} %get-tuple-element.257), channel_id=1, source_target_pairs={{0,8},{2,10},{4,12},{6,14},{8,0},{10,2},{12,4},{14,6},{16,24},{18,... | collective-permute-start | bytes 786440 | tf_op jit(solution)/shard_map/ppermute | solution.py:723
  4.7 39.2 %collective-permute-start.5 = (bf16[128,1024]{1,0:T(8,128)(2,1)}, bf16[128,1024]{1,0:T(8,128)(2,1)}, u32[]{:S(2)}, u32[]{:S(2)}) collective-permute-start(bf16[128,1024]{1,0:T(8,128)(2,1)} %get-tuple-element.260), channel_id=1, source_target_pairs={{0,12},{2,14},{4,8},{6,10},{8,4},{10,6},{12,0},{14,2},{16,28},{18,... | collective-permute-start | bytes 786440 | tf_op jit(solution)/shard_map/ppermute | solution.py:723
  7.8 31.9 %collective-permute-start.6 = (bf16[128,1024]{0,1:T(8,128)(2,1)}, bf16[128,1024]{0,1:T(8,128)(2,1)}, u32[]{:S(2)}, u32[]{:S(2)}) collective-permute-start(bf16[128,1024]{0,1:T(8,128)(2,1)} %bitcast.50), channel_id=1, source_target_pairs={{0,8},{2,10},{4,12},{6,14},{8,0},{10,2},{12,4},{14,6},{16,24},{18,... | collective-permute-start | bytes 786440 | tf_op jit(solution)/shard_map/ppermute | solution.py:666
  8.2 27.5 %collective-permute-start.8 = (bf16[128,1024]{1,0:T(8,128)(2,1)S(1)}, bf16[128,1024]{1,0:T(8,128)(2,1)S(1)}, u32[]{:S(2)}, u32[]{:S(2)}) collective-permute-start(bf16[128,1024]{1,0:T(8,128)(2,1)S(1)} %copy-done.19), channel_id=1, source_target_pairs={{0,8},{2,10},{4,12},{6,14},{8,0},{10,2},{12,4},{14,6},{16,24},{18,... | collective-permute-start | bytes 786440 | tf_op jit(solution)/shard_map/ppermute | solution.py:666
  60.8 58.3 %collective-permute-start.10 = (bf16[512,1024]{1,0:T(8,128)(2,1)}, bf16[512,1024]{1,0:T(8,128)(2,1)}, u32[]{:S(2)}, u32[]{:S(2)}) collective-permute-start(bf16[512,1024]{1,0:T(8,128)(2,1)} %constant_dynamic-update-slice_fusion.5), channel_id=1, source_target_pairs={{0,2},{2,0},{4,6},{6,4},{8,10},{10,8},{12,14},{14,12},{16,18},{18,... | collective-permute-start | bytes 3145736 | tf_op jit(solution)/shard_map/ppermute | solution.py:666
  68.5 77.8 %collective-permute-start.7 = (bf16[1024,512]{1,0:T(8,128)(2,1)S(1)}, bf16[1024,512]{1,0:T(8,128)(2,1)}, u32[]{:S(2)}, u32[]{:S(2)}) collective-permute-start(bf16[1024,512]{1,0:T(8,128)(2,1)S(1)} %pad_maximum_fusion.6), channel_id=1, source_target_pairs={{0,4},{2,6},{4,0},{6,2},{8,12},{10,14},{12,8},{14,10},{16,20},{18,... | collective-permute-start | bytes 3145736 | tf_op jit(solution)/shard_map/ppermute | solution.py:666
  69.5 40.5 %collective-permute-start.12 = (bf16[128,1024]{1,0:T(8,128)(2,1)}, bf16[128,1024]{1,0:T(8,128)(2,1)}, u32[]{:S(2)}, u32[]{:S(2)}) collective-permute-start(bf16[128,1024]{1,0:T(8,128)(2,1)} %get-tuple-element.255), channel_id=1, source_target_pairs={{0,4},{2,6},{4,0},{6,2},{8,12},{10,14},{12,8},{14,10},{16,20},{18,... | collective-permute-start | bytes 786440 | tf_op jit(solution)/shard_map/ppermute | solution.py:723
  75.8 37.1 %collective-permute-start.19 = (bf16[128,1024]{1,0:T(8,128)(2,1)}, bf16[128,1024]{1,0:T(8,128)(2,1)S(1)}, u32[]{:S(2)}, u32[]{:S(2)}) collective-permute-start(bf16[128,1024]{1,0:T(8,128)(2,1)} %get-tuple-element.249), channel_id=1, source_target_pairs={{0,8},{2,10},{4,12},{6,14},{8,0},{10,2},{12,4},{14,6},{16,24},{18,... | collective-permute-start | bytes 786440 | tf_op jit(solution)/shard_map/ppermute | solution.py:723
  81.3 33.9 %collective-permute-start.20 = (bf16[128,1024]{1,0:T(8,128)(2,1)}, bf16[128,1024]{1,0:T(8,128)(2,1)S(1)}, u32[]{:S(2)}, u32[]{:S(2)}) collective-permute-start(bf16[128,1024]{1,0:T(8,128)(2,1)} %get-tuple-element.250), channel_id=1, source_target_pairs={{0,12},{2,14},{4,8},{6,10},{8,4},{10,6},{12,0},{14,2},{16,28},{18,... | collective-permute-start | bytes 786440 | tf_op jit(solution)/shard_map/ppermute | solution.py:723
  112.9 33.5 %collective-permute-start.11 = (bf16[256,1024]{1,0:T(8,128)(2,1)S(1)}, bf16[256,1024]{1,0:T(8,128)(2,1)S(1)}, u32[]{:S(2)}, u32[]{:S(2)}) collective-permute-start(bf16[256,1024]{1,0:T(8,128)(2,1)S(1)} %copy-done.56), channel_id=1, source_target_pairs={{0,16},{2,18},{4,20},{6,22},{8,24},{10,26},{12,28},{14,30},{16,0},... | collective-permute-start | bytes 1572872 | tf_op jit(solution)/shard_map/ppermute | solution.py:666
  115.2 41.3 %collective-permute-start.17 = (bf16[512,1024]{1,0:T(8,128)(2,1)}, bf16[512,1024]{1,0:T(8,128)(2,1)S(1)}, u32[]{:S(2)}, u32[]{:S(2)}) collective-permute-start(bf16[512,1024]{1,0:T(8,128)(2,1)} %constant_dynamic-update-slice_fusion.5), channel_id=1, source_target_pairs={{0,4},{2,6},{4,0},{6,2},{8,12},{10,14},{12,8},{14,10},{16,20},{18,... | collective-permute-start | bytes 3145736 | tf_op jit(solution)/shard_map/ppermute | solution.py:666
  117.7 33.7 %collective-permute-start.16 = (bf16[256,1024]{1,0:T(8,128)(2,1)S(1)}, bf16[256,1024]{1,0:T(8,128)(2,1)S(1)}, u32[]{:S(2)}, u32[]{:S(2)}) collective-permute-start(bf16[256,1024]{1,0:T(8,128)(2,1)S(1)} %copy-done.56), channel_id=1, source_target_pairs={{0,2},{2,0},{4,6},{6,4},{8,10},{10,8},{12,14},{14,12},{16,18},{18,... | collective-permute-start | bytes 1572872 | tf_op jit(solution)/shard_map/ppermute | solution.py:666
  119.1 37.4 %collective-permute-start.15 = (bf16[256,1024]{1,0:T(8,128)(2,1)S(1)}, bf16[256,1024]{1,0:T(8,128)(2,1)S(1)}, u32[]{:S(2)}, u32[]{:S(2)}) collective-permute-start(bf16[256,1024]{1,0:T(8,128)(2,1)S(1)} %copy-done.55), channel_id=1, source_target_pairs={{0,16},{2,18},{4,20},{6,22},{8,24},{10,26},{12,28},{14,30},{16,0},... | collective-permute-start | bytes 1572872 | tf_op jit(solution)/shard_map/ppermute | solution.py:666
  161.2 61.9 %collective-permute-start.26 = (bf16[512,1024]{1,0:T(8,128)(2,1)S(1)}, bf16[512,1024]{1,0:T(8,128)(2,1)S(1)}, u32[]{:S(2)}, u32[]{:S(2)}) collective-permute-start(bf16[512,1024]{1,0:T(8,128)(2,1)S(1)} %slice.257), channel_id=1, source_target_pairs={{0,4},{2,6},{4,0},{6,2},{8,12},{10,14},{12,8},{14,10},{16,20},{18,... | collective-permute-start | bytes 3145736 | tf_op jit(solution)/shard_map/ppermute | solution.py:666
  162.3 34.8 %collective-permute-start.23 = (bf16[256,1024]{0,1:T(8,128)(2,1)S(1)}, bf16[256,1024]{0,1:T(8,128)(2,1)S(1)}, u32[]{:S(2)}, u32[]{:S(2)}) collective-permute-start(bf16[256,1024]{0,1:T(8,128)(2,1)S(1)} %copy-done.24), channel_id=1, source_target_pairs={{0,16},{2,18},{4,20},{6,22},{8,24},{10,26},{12,28},{14,30},{16,0},... | collective-permute-start | bytes 1572872 | tf_op jit(solution)/shard_map/ppermute | solution.py:666
  169.7 49.9 %collective-permute-start.22 = (bf16[2,2,1,256,256]{4,3,0,2,1:T(8,128)(2,1)S(1)}, bf16[2,2,1,256,256]{4,3,0,2,1:T(8,128)(2,1)S(1)}, u32[]{:S(2)}, u32[]{:S(2)}) collective-permute-start(bf16[2,2,1,256,256]{4,3,0,2,1:T(8,128)(2,1)S(1)} %pad_maximum_fusion.20), channel_id=1, source_target_pairs={{0,16},{2,18},{4,20},{6,22},{8,24},{10,26},{12,28},{14,30},{16,0},... | collective-permute-start | bytes 1572872 | tf_op jit(solution)/shard_map/ppermute | solution.py:666
  172.1 51.0 %collective-permute-start.24 = (bf16[256,1024]{1,0:T(8,128)(2,1)S(1)}, bf16[256,1024]{1,0:T(8,128)(2,1)S(1)}, u32[]{:S(2)}, u32[]{:S(2)}) collective-permute-start(bf16[256,1024]{1,0:T(8,128)(2,1)S(1)} %copy-done.55), channel_id=1, source_target_pairs={{0,2},{2,0},{4,6},{6,4},{8,10},{10,8},{12,14},{14,12},{16,18},{18,... | collective-permute-start | bytes 1572872 | tf_op jit(solution)/shard_map/ppermute | solution.py:666
  172.7 50.4 %collective-permute-start.25 = (bf16[256,1024]{1,0:T(8,128)(2,1)S(1)}, bf16[256,1024]{1,0:T(8,128)(2,1)S(1)}, u32[]{:S(2)}, u32[]{:S(2)}) collective-permute-start(bf16[256,1024]{1,0:T(8,128)(2,1)S(1)} %collective-permute-done.11.refs_12_.refs_17_), channel_id=1, source_target_pairs={{0,2},{2,0},{4,6},{6,4},{8,10},{10,8},{12,14},{14,12},{16,18},{18,... | collective-permute-start | bytes 1572872 | tf_op jit(solution)/shard_map/ppermute | solution.py:666
  197.1 45.0 %collective-permute-start.29 = (bf16[256,1024]{1,0:T(8,128)(2,1)}, bf16[256,1024]{1,0:T(8,128)(2,1)}, u32[]{:S(2)}, u32[]{:S(2)}) collective-permute-start(bf16[256,1024]{1,0:T(8,128)(2,1)} %pad_maximum_fusion.16.refs_18_.refs_23_), channel_id=1, source_target_pairs={{0,16},{2,18},{4,20},{6,22},{8,24},{10,26},{12,28},{14,30},{16,0},... | collective-permute-start | bytes 1572872 | tf_op jit(solution)/shard_map/ppermute | solution.py:666
  219.6 67.4 %collective-permute-start.32 = (bf16[256,1024]{1,0:T(8,128)(2,1)}, bf16[256,1024]{1,0:T(8,128)(2,1)}, u32[]{:S(2)}, u32[]{:S(2)}) collective-permute-start(bf16[256,1024]{1,0:T(8,128)(2,1)} %pad_maximum_fusion.17.refs_19_.refs_24_), channel_id=1, source_target_pairs={{0,16},{2,18},{4,20},{6,22},{8,24},{10,26},{12,28},{14,30},{16,0},... | collective-permute-start | bytes 1572872 | tf_op jit(solution)/shard_map/ppermute | solution.py:666
  223.1 42.6 %collective-permute-start.33 = (bf16[512,1024]{0,1:T(8,128)(2,1)}, bf16[512,1024]{0,1:T(8,128)(2,1)}, u32[]{:S(2)}, u32[]{:S(2)}) collective-permute-start(bf16[512,1024]{0,1:T(8,128)(2,1)} %pad_maximum_fusion.8), channel_id=1, source_target_pairs={{0,2},{2,0},{4,6},{6,4},{8,10},{10,8},{12,14},{14,12},{16,18},{18,... | collective-permute-start | bytes 3145736 | tf_op jit(solution)/shard_map/ppermute | solution.py:666
  225.1 32.1 %collective-permute-start.27 = (bf16[4,1,256,256]{3,2,0,1:T(8,128)(2,1)S(1)}, bf16[4,1,256,256]{3,2,0,1:T(8,128)(2,1)}, u32[]{:S(2)}, u32[]{:S(2)}) collective-permute-start(bf16[4,1,256,256]{3,2,0,1:T(8,128)(2,1)S(1)} %get-tuple-element.248), channel_id=1, source_target_pairs={{0,2},{2,0},{4,6},{6,4},{8,10},{10,8},{12,14},{14,12},{16,18},{18,... | collective-permute-start | bytes 1572872 | tf_op jit(solution)/shard_map/ppermute | solution.py:666
  226.6 30.6 %collective-permute-start.28 = (bf16[4,1,256,256]{3,2,1,0:T(8,128)(2,1)S(1)}, bf16[4,1,256,256]{3,2,1,0:T(8,128)(2,1)}, u32[]{:S(2)}, u32[]{:S(2)}) collective-permute-start(bf16[4,1,256,256]{3,2,1,0:T(8,128)(2,1)S(1)} %get-tuple-element.247), channel_id=1, source_target_pairs={{0,4},{2,6},{4,0},{6,2},{8,12},{10,14},{12,8},{14,10},{16,20},{18,... | collective-permute-start | bytes 1572872 | tf_op jit(solution)/shard_map/ppermute | solution.py:666
  287.0 43.4 %collective-permute-start.34 = (bf16[1024,1024]{0,1:T(8,128)(2,1)}, bf16[1024,1024]{0,1:T(8,128)(2,1)}, u32[]{:S(2)}, u32[]{:S(2)}) collective-permute-start(bf16[1024,1024]{0,1:T(8,128)(2,1)} %pad_maximum_fusion.5), channel_id=1, source_target_pairs={{0,4},{2,6},{4,0},{6,2},{8,12},{10,14},{12,8},{14,10},{16,20},{18,... | collective-permute-start | bytes 6291464 | tf_op jit(solution)/shard_map/ppermute | solution.py:666
  337.2 38.2 %collective-permute-start.39 = (f32[128,2176]{1,0:T(8,128)}, f32[128,2176]{1,0:T(8,128)}, u32[]{:S(2)}, u32[]{:S(2)}) collective-permute-start(f32[128,2176]{1,0:T(8,128)} %get-tuple-element.241), channel_id=1, source_target_pairs={{0,1},{1,0},{2,3},{3,2},{4,5},{5,4},{6,7},{7,6},{8,9},{9,8},{10,11... | collective-permute-start | bytes 3342344 | tf_op jit(solution)/shard_map/ppermute | solution.py:669
  352.9 28.0 %collective-permute-start.40 = (bf16[256,1024]{1,0:T(8,128)(2,1)}, bf16[256,1024]{1,0:T(8,128)(2,1)}, u32[]{:S(2)}, u32[]{:S(2)}) collective-permute-start(bf16[256,1024]{1,0:T(8,128)(2,1)} %pad_maximum_fusion.19.refs_27_.refs_32_), channel_id=1, source_target_pairs={{0,16},{2,18},{4,20},{6,22},{8,24},{10,26},{12,28},{14,30},{16,0},... | collective-permute-start | bytes 1572872 | tf_op jit(solution)/shard_map/ppermute | solution.py:666
  541.1 41.7 %collective-permute-start.66 = (bf16[512,2304]{1,0:T(8,128)(2,1)}, bf16[512,2304]{1,0:T(8,128)(2,1)}, u32[]{:S(2)}, u32[]{:S(2)}) collective-permute-start(bf16[512,2304]{1,0:T(8,128)(2,1)} %get-tuple-element.208), channel_id=1, source_target_pairs={{0,1},{1,0},{2,3},{3,2},{4,5},{5,4},{6,7},{7,6},{8,9},{9,8},{10,11... | collective-permute-start | bytes 7077896 | tf_op jit(solution)/shard_map/ppermute | solution.py:669
  541.3 40.2 %collective-permute-start.58 = (bf16[128,2048]{1,0:T(8,128)(2,1)S(1)}, bf16[128,2048]{1,0:T(8,128)(2,1)S(1)}, u32[]{:S(2)}, u32[]{:S(2)}) collective-permute-start(bf16[128,2048]{1,0:T(8,128)(2,1)S(1)} %copy-done.51), channel_id=1, source_target_pairs={{0,1},{1,0},{2,3},{3,2},{4,5},{5,4},{6,7},{7,6},{8,9},{9,8},{10,11... | collective-permute-start | bytes 1572872 | tf_op jit(solution)/shard_map/ppermute | solution.py:669
  631.3 43.6 %collective-permute-start.92 = (bf16[2,24,2048]{2,1,0:T(8,128)(2,1)}, bf16[2,24,2048]{2,1,0:T(8,128)(2,1)}, u32[]{:S(2)}, u32[]{:S(2)}) collective-permute-start(bf16[2,24,2048]{2,1,0:T(8,128)(2,1)} %fusion.33), channel_id=1, source_target_pairs={{0,8},{2,10},{4,12},{6,14},{8,0},{10,2},{12,4},{14,6},{16,24},{18,... | collective-permute-start | bytes 589832 | tf_op jit(solution)/shard_map/ppermute | solution.py:1240
  632.7 42.1 %collective-permute-start.93 = (bf16[2,24,2048]{2,1,0:T(8,128)(2,1)}, bf16[2,24,2048]{2,1,0:T(8,128)(2,1)}, u32[]{:S(2)}, u32[]{:S(2)}) collective-permute-start(bf16[2,24,2048]{2,1,0:T(8,128)(2,1)} %fusion.33), channel_id=1, source_target_pairs={{0,16},{2,18},{4,20},{6,22},{8,24},{10,26},{12,28},{14,30},{16,0},... | collective-permute-start | bytes 589832 | tf_op jit(solution)/shard_map/ppermute | solution.py:1240
  633.3 41.6 %collective-permute-start.94 = (bf16[2,24,2048]{2,1,0:T(8,128)(2,1)}, bf16[2,24,2048]{2,1,0:T(8,128)(2,1)}, u32[]{:S(2)}, u32[]{:S(2)}) collective-permute-start(bf16[2,24,2048]{2,1,0:T(8,128)(2,1)} %fusion.33), channel_id=1, source_target_pairs={{0,24},{2,26},{4,28},{6,30},{8,16},{10,18},{12,20},{14,22},{16,8},... | collective-permute-start | bytes 589832 | tf_op jit(solution)/shard_map/ppermute | solution.py:1240
  655.0 29.6 %collective-permute-start.71 = (bf16[8,1,256,256]{3,2,1,0:T(8,128)(2,1)}, bf16[8,1,256,256]{3,2,1,0:T(8,128)(2,1)}, u32[]{:S(2)}, u32[]{:S(2)}) collective-permute-start(bf16[8,1,256,256]{3,2,1,0:T(8,128)(2,1)} %get-tuple-element.216), channel_id=1, source_target_pairs={{0,4},{2,6},{4,0},{6,2},{8,12},{10,14},{12,8},{14,10},{16,20},{18,... | collective-permute-start | bytes 3145736 | tf_op jit(solution)/shard_map/ppermute | solution.py:666
  (184 other events, 3489.5 us)

commit v3 on v2

--- a/solution.py
+++ b/solution.py
@@ -57,7 +57,7 @@
     return value.astype(BF16)
 
 
-def attend_kernel(count_ref, kslot_ref, vslot_ref, q_ref, k_ref, v_ref, o_ref, lse_ref, acc, tot, *, heads, dim):
+def attend_kernel(count_ref, slot_ref, kslot_ref, vslot_ref, q_ref, kv_ref, o_ref, lse_ref, acc, tot, *, heads, dim):
     group = pl.program_id(0)
     count = count_ref[group]
     rows = q_ref.shape[0]
@@ -66,8 +66,8 @@
     tot[...] = jnp.zeros_like(tot)
 
     def step(index, masked):
-        keys = k_ref[kslot_ref[group, index], 0]
-        values = v_ref[vslot_ref[group, index], 0]
+        keys = kv_ref[slot_ref[group, index], 0, :, :dim]
+        values = kv_ref[slot_ref[group, index], 0, :, dim:]
         for head in range(heads):
             lanes = slice(head * dim, (head + 1) * dim)
             scores = against(q_ref[:, lanes], keys)
@@ -99,7 +99,7 @@
 
 
 def attend_back_kernel(
-    count_ref, kslot_ref, vslot_ref, q_ref, k_ref, v_ref, o_ref, lse_ref, g_ref, dq_ref, dk_near, dk_far, dv_near, dv_far, delta, *, heads, dim
+    count_ref, slot_ref, kslot_ref, vslot_ref, q_ref, kv_ref, o_ref, lse_ref, g_ref, dq_ref, dk_near, dk_far, dv_near, dv_far, delta, *, heads, dim
 ):
     group = pl.program_id(0)
     count = count_ref[group]
@@ -124,8 +124,8 @@
         )
 
     def step(index, masked):
-        keys = k_ref[kslot_ref[group, index], 0]
-        values = v_ref[vslot_ref[group, index], 0]
+        keys = kv_ref[slot_ref[group, index], 0, :, :dim]
+        values = kv_ref[slot_ref[group, index], 0, :, dim:]
         dk = jnp.zeros(keys.shape, F32)
         dv = jnp.zeros(values.shape, F32)
         for head in range(heads):
@@ -154,19 +154,18 @@
     step(count - 1, True)
 
 
-def attend(tables, queries, key_all, value_all, groups, heads, dim):
-    count, kslot, vslot = tables
-    slots, _, block, _ = key_all.shape
+def attend(tables, queries, kv_all, groups, heads, dim):
+    slots, _, block, _ = kv_all.shape
     rows = queries.shape[0]
     fold = min(128, block)
-    whole = pl.BlockSpec((slots, 1, block, dim), lambda g, *_: (0, g, 0, 0))
+    whole = pl.BlockSpec((slots, 1, block, 2 * dim), lambda g, *_: (0, g, 0, 0))
     mine = pl.BlockSpec((block, heads * dim), lambda g, *_: (g, 0))
     return pl.pallas_call(
         lambda *refs: attend_kernel(*refs, heads=heads, dim=dim),
         grid_spec=pltpu.PrefetchScalarGridSpec(
-            num_scalar_prefetch=3,
+            num_scalar_prefetch=4,
             grid=(groups,),
-            in_specs=[mine, whole, whole],
+            in_specs=[mine, whole],
             out_specs=[mine, pl.BlockSpec((block, 128), lambda g, *_: (g, 0))],
             scratch_shapes=[
                 pltpu.VMEM((block, heads * dim), F32),
@@ -181,22 +180,21 @@
         cost_estimate=pl.CostEstimate(
             flops=4 * rows * heads * dim * 2304, bytes_accessed=6 * 2**20, transcendentals=rows * heads * 2304
         ),
-    )(count, kslot, vslot, queries, key_all, value_all)
-
-
-def attend_back(tables, queries, key_all, value_all, heads_low, lse, grads, groups, heads, dim):
-    count, kslot, vslot = tables
-    slots, _, block, _ = key_all.shape
+    )(*tables, queries, kv_all)
+
+
+def attend_back(tables, queries, kv_all, heads_low, lse, grads, groups, heads, dim):
+    slots, _, block, _ = kv_all.shape
     rows = queries.shape[0]
-    whole = pl.BlockSpec((slots, 1, block, dim), lambda g, *_: (0, g, 0, 0))
+    whole = pl.BlockSpec((slots, 1, block, 2 * dim), lambda g, *_: (0, g, 0, 0))
     part = pl.BlockSpec((slots // 2, 1, block, dim), lambda g, *_: (0, g, 0, 0))
     mine = pl.BlockSpec((block, heads * dim), lambda g, *_: (g, 0))
     return pl.pallas_call(
         lambda *refs: attend_back_kernel(*refs, heads=heads, dim=dim),
         grid_spec=pltpu.PrefetchScalarGridSpec(
-            num_scalar_prefetch=3,
+            num_scalar_prefetch=4,
             grid=(groups,),
-            in_specs=[mine, whole, whole, mine, pl.BlockSpec((block, 128), lambda g, *_: (g, 0)), mine],
+            in_specs=[mine, whole, mine, pl.BlockSpec((block, 128), lambda g, *_: (g, 0)), mine],
             out_specs=[mine] + [part] * 4,
             scratch_shapes=[pltpu.VMEM((heads, block, 1), F32)],
         ),
@@ -208,7 +206,7 @@
         cost_estimate=pl.CostEstimate(
             flops=10 * rows * heads * dim * 2304, bytes_accessed=12 * 2**20, transcendentals=rows * heads * 2304
         ),
-    )(count, kslot, vslot, queries, key_all, value_all, heads_low, lse, grads)
+    )(*tables, queries, kv_all, heads_low, lse, grads)
 
 
 def gelu_parts(gate):
@@ -261,7 +259,7 @@
     )(*tables, *inputs)
 
 
-def first_kernel(order_ref, tokens_ref, gains_ref, select_ref, shrink_ref, moved_ref, low_ref, rank_ref, *, count, block, aligned):
+def first_kernel(tokens_ref, gains_ref, select_ref, shrink_ref, low_ref, rank_ref):
     tokens = tokens_ref[...].astype(F32)
     first = low(tokens * rms_scale(tokens) * gains_ref[0:1, :])
     low_ref[...] = first
@@ -270,10 +268,6 @@
     width = select.shape[1]
     for i in range(3):
         rank_ref[:, i * width : (i + 1) * width] = low(select * ranks[:, i * width : (i + 1) * width])
-    if aligned:
-        move_columns(moved_ref, low_ref, order_ref, count, block)
-    else:
-        moved_ref[...] = first
 
 
 def middle_kernel(
@@ -382,19 +376,14 @@
 
 
 def last_kernel(
-    half_ref, back_ref, pick_ref, own_ref, other_ref, tokens_ref, gains_ref, scaled_ref, first_ref, shrink_ref,
-    input_ref, grads_ref, work, place, kept, *, count, block, aligned
+    half_ref, pick_ref, own_ref, other_ref, tokens_ref, gains_ref, scaled_ref, first_ref, shrink_ref,
+    input_ref, grads_ref, kept
 ):
     width = scaled_ref.shape[1]
     joined = own_ref[...] + other_ref[...].astype(F32)
     ranks = low(joined[:, width:])
     each = ranks.shape[1] // 3
-    work[...] = joined[:, :width]
-    if aligned:
-        move_columns(place, work, back_ref, count, block)
-        grad_first = place[...]
-    else:
-        grad_first = work[...]
+    grad_first = joined[:, :width]
     grad_first = grad_first + first_ref[...] + product(ranks, shrink_ref[...])
     tokens = tokens_ref[...].astype(F32)
     scale = rms_scale(tokens)
@@ -461,7 +450,7 @@
     arriving_down = bring(downs, down_w, sems.at[2])
     ranks = select_ref.shape[1]
     hidden_width = gate_w.shape[1]
-    chunk = min(256, hidden_width)
+    chunk = min(1024, hidden_width)
     gather_parts(x_ref, parts, order_ref, count, width)
     ranks_of(rank_ref, parts, select_ref, shrink_ref)
     for copy in arriving:
@@ -479,7 +468,7 @@
 
     for copy in arriving_down:
         copy.wait()
-    step = 256
+    step = 1024
 
     @pl.loop(0, width // step)
     def _(i):
@@ -557,7 +546,7 @@
     arriving_next = bring(gates, gate_w, sems.at[0]) + bring(ups, up_w, sems.at[1])
     ranks = select_ref.shape[1]
     hidden_width = gate_w.shape[1]
-    chunk = min(256, hidden_width)
+    chunk = min(1024, hidden_width)
     gather_parts(g_ref, parts, order_ref, count, width)
     ranks_of(down_rank, parts, select_ref, dexp_ref)
     for copy in arriving:
@@ -577,7 +566,7 @@
 
     for copy in arriving_next:
         copy.wait()
-    step = 256
+    step = 1024
 
     @pl.loop(0, width // step)
     def _(i):
@@ -804,7 +793,9 @@
     apart = visible_device ^ me
     key_slot = (((apart >> 1) & 1) * 2 + (apart & 1)) * rest + rest_place(apart)
     value_slot = ((apart & 1) * 2 + ((apart >> 1) & 1)) * rest + rest_place(apart)
-    tables = (visible_count, key_slot.astype(jnp.int32), value_slot.astype(jnp.int32))
+    tables = tuple(
+        table.astype(jnp.int32) for table in (visible_count, visible_device, key_slot, value_slot)
+    )
 
     gains = norm_gains.astype(F32)
     query_gain = head_norm_gains[0].astype(F32)
@@ -858,17 +849,14 @@
         return flat.reshape(value.shape)
 
     first_shrink = jnp.concatenate([query_shrink, key_shrink, value_shrink], axis=0)
-    first_moved, first_low, rank_first = whole_call(
-        lambda *refs: first_kernel(*refs, **style),
+    first_low, rank_first = whole_call(
+        first_kernel,
         (tokens, gains, select, first_shrink),
         (
             jax.ShapeDtypeStruct(tokens.shape, BF16),
-            jax.ShapeDtypeStruct(tokens.shape, BF16),
             jax.ShapeDtypeStruct((local_rows, 3 * adapter_width), BF16),
         ),
-        tables=(weight_order_table,),
-    )
-    first_moved = moved(first_moved, weight_order)
+    )
     rank_query = rank_first[:, :adapter_width]
     rank_key = rank_first[:, adapter_width : 2 * adapter_width]
     rank_value = rank_first[:, 2 * adapter_width :]
@@ -907,76 +895,54 @@
         return [over_x(piece) for piece in pieces]
 
     step = lax.optimization_barrier
-    kv_weight = jnp.concatenate([key_matrix, value_matrix], axis=1)
-    out_rows, down_rows = out_weight.T, down_weight.T
-    kv_part = joined(kv_weight, flip(kv_weight, first_bit))
-    query_part = joined(query_weight, flip(query_weight, first_bit))
-    out_part = joined(out_rows, flip(out_rows, first_bit))
-    kv_part = over_rest(kv_part, rest_bits[1:])
+    head_maps = lax.all_gather(
+        jnp.concatenate([query_weight, key_matrix, value_matrix], axis=1), "ctx", axis=0, tiled=True
+    )
+    out_rows = out_weight.T
     gate_a, gate_b = team_split(gate_weight)
-    query_part = over_rest(query_part, rest_bits[1:])
-    kv_slab = joined(kv_part, over_x(kv_part))
-    kv_slab, gate_a, gate_b, up_weight, down_rows, out_part = step(
-        (kv_slab, gate_a, gate_b, up_weight, down_rows, out_part)
-    )
-    kv_slabs = kv_slab, over_y(kv_slab)
     up_a, up_b = team_split(up_weight)
-    query_slab = joined(query_part, over_x(query_part))
     gate_far_a = spread_far(gate_a)
-    gate_near_a = near([gate_a])
-    query_y_a = over_y(query_slab[: width // 4])
-    kv_slabs, query_slab, gate_far_a, up_a, up_b = step((kv_slabs, query_slab, gate_far_a, up_a, up_b))
-
-    kv_projected = slab_product(first_moved, kv_slabs)
-    kv_width = key_matrix.shape[1]
+    gate_far_b = spread_far(gate_b)
+    gate_near_a, gate_near_b = near([gate_a]), near([gate_b])
+    up_far_a = spread_far(up_a)
+    up_near_a, up_near_b = near([up_a]), near([up_b])
+    gate_far_near_a = near(gate_far_a)
+    head_maps, gate_far_a, gate_far_b, gate_near_a, gate_near_b, up_far_a, up_near_a, up_near_b, gate_far_near_a = step(
+        (head_maps, gate_far_a, gate_far_b, gate_near_a, gate_near_b, up_far_a, up_near_a, up_near_b, gate_far_near_a)
+    )
+    query_width, kv_width = query_weight.shape[1], key_matrix.shape[1]
+    query_maps, kv_maps = head_maps[:, :query_width], head_maps[:, query_width:]
+    kv_projected = product(first_low, kv_maps)
     key_projected = kv_projected[:, :kv_width] + product(rank_key, key_widen_maps)
     value_projected = kv_projected[:, kv_width:] + product(rank_value, value_widen_maps)
-    key_low = low(key_piece(key_projected)).reshape(1, groups, block_len, head_dim)
-    value_low = low(value_piece(value_projected)).reshape(1, groups, block_len, head_dim)
-    kv_part = jnp.stack([key_low, value_low], axis=1)
-    gate_far_b = spread_far(gate_b)
-    down_a, down_b = team_split(down_rows)
-    kv_part, gate_far_b, gate_near_a, query_y_a, down_a, down_b, out_part = step(
-        (kv_part, gate_far_b, gate_near_a, query_y_a, down_a, down_b, out_part)
-    )
-    for bit in rest_bits:
-        kv_part = joined(kv_part, flip(kv_part, bit))
+    kv_low = jnp.concatenate([low(key_piece(key_projected)), low(value_piece(value_projected))], axis=1)
+    kv_all = lax.all_gather(kv_low, "ctx", axis=0, tiled=True).reshape(
+        count_ctx, groups, block_len, 2 * head_dim
+    )
+    query_proj = product(first_low, query_maps) + product(rank_query, query_expand)
+    query_low = low(query_piece(query_proj))
+    down_a, down_b = team_split(down_weight.T)
+    up_far_b = spread_far(up_b)
+    out_part = joined(out_rows, flip(out_rows, first_bit))
     out_part = over_rest(out_part, rest_bits[1:])
-    query_y_b = over_y(query_slab[width // 4 :])
-    gate_near_b = near([gate_b])
-    gate_far_near_a = near(gate_far_a)
-    kv_part, out_part, gate_near_b, gate_far_near_a, query_y_b = step(
-        (kv_part, out_part, gate_near_b, gate_far_near_a, query_y_b)
-    )
-    key_part, value_part = kv_part[:, 0], kv_part[:, 1]
-    key_x, value_y = flip(key_part, x_bit), flip(value_part, y_bit)
-    up_far_a = spread_far(up_a)
-    key_x, value_y, up_far_a = step((key_x, value_y, up_far_a))
-    key_part = joined(key_part, key_x)
-    value_part = joined(value_part, value_y)
-    key_all = joined(key_part, flip(key_part, y_bit))
-    value_all = joined(value_part, flip(value_part, x_bit))
-    query_slabs = query_slab, joined(query_y_a, query_y_b)
-    query_proj = slab_product(first_moved, query_slabs) + product(rank_query, query_expand)
-    query_low = low(query_piece(query_proj))
-    up_far_b = spread_far(up_b)
     out_slab = joined(out_part, over_x(out_part))
-    key_all, value_all, query_low, up_far_b, out_slab = step(
-        (key_all, value_all, query_low, up_far_b, out_slab)
-    )
     out_slabs = out_slab, over_y(out_slab)
-    down_far_a = spread_far(down_a)
     gate_far_near_b = near(gate_far_b)
-    up_near_a = near([up_a])
-    up_near_b = near([up_b])
-    heads_low, lse = attend(tables, query_low, key_all, value_all, groups, heads_local, head_dim)
-
-    heads_low, out_slabs, down_far_a, gate_far_near_b, up_near_a, up_near_b = step(
-        (heads_low, out_slabs, down_far_a, gate_far_near_b, up_near_a, up_near_b)
-    )
-    down_far_b = spread_far(down_b)
     up_far_near_a = near(up_far_a)
+    down_far_a, down_far_b = spread_far(down_a), spread_far(down_b)
     down_near_a, down_near_b = near([down_a]), near([down_b])
+    up_far_near_b = near(up_far_b)
+    kv_all, down_far_a, up_far_near_a, up_far_b, out_slab, gate_far_near_b, down_near_a = step(
+        (kv_all, down_far_a, up_far_near_a, up_far_b, out_slab, gate_far_near_b, down_near_a)
+    )
+    out_slabs = out_slab, out_slabs[1]
+    down_far_near_a = near(down_far_a)
+    heads_low, lse = attend(tables, query_low, kv_all, groups, heads_local, head_dim)
+
+    heads_low, out_slabs, down_far_b, up_far_near_b, down_near_b = step(
+        (heads_low, out_slabs, down_far_b, up_far_near_b, down_near_b)
+    )
+    down_far_near_b = near(down_far_b)
     attn_part = jnp.concatenate(
         [slab_against(heads_low, out_slabs), select * against(heads_low, out_shrink)], axis=1
     )
@@ -1003,12 +969,6 @@
         specs={2: half_spec},
     )
 
-    second_low, down_far_b, up_far_near_a, down_near_a, down_near_b = step(
-        (second_low, down_far_b, up_far_near_a, down_near_a, down_near_b)
-    )
-    up_far_near_b = near(up_far_b)
-    down_far_near_a, down_far_near_b = near(down_far_a), near(down_far_b)
-
     def in_order(own, far, near_own, near_far):
         first, second = ([o] + f + n + nf for o, f, n, nf in zip(own, far, near_own, near_far))
         return [piece for pair in zip(first, second) for piece in pair]
@@ -1038,7 +998,7 @@
         parts = []
         for member in (3, 1, 2, 0):
             rows = slice(member * half_rows, (member + 1) * half_rows)
-            parts.append(to_member(low(near_part[rows] + arrived[rows]), member))
+            parts.append(to_member(low(near_part[rows].astype(F32) + arrived[rows]), member))
         return parts
 
     def hidden_columns(value):
@@ -1054,7 +1014,7 @@
         team_order_table, second_far, select_far, feed_maps, *slices, *pieces, BF16
     )
     *kept_near, part_near = feed(
-        team_order_table, second_near, select_near, feed_maps, *slices, *pieces, F32
+        team_order_table, second_near, select_near, feed_maps, *slices, *pieces, BF16
     )
     ffn_parts = team_sum(part_near, part_far)
 
@@ -1091,9 +1051,10 @@
         team_order_table, grad_far, select_far, down_map, nothing, kept_far, *slices, *pieces, BF16
     )
     back_near, team_grads = feed_back(
-        team_order_table, grad_near, select_near, down_map, team_grads, kept_near, *slices, *pieces, F32
+        team_order_table, grad_near, select_near, down_map, team_grads, kept_near, *slices, *pieces, BF16
     )
     second_parts = team_sum(back_near, back_far)
+    second_parts, team_grads = step((second_parts, team_grads))
     grad_sent, grad_scaled, grad_first, own_grads = whole_call(
         lambda *refs: turn_kernel(*refs, **style),
         (
@@ -1132,7 +1093,7 @@
     grad_heads = low(slab_product(grad_attn, out_slabs) + product(grad_rank_out, out_shrink))
 
     grad_queries, keys_near, keys_far, values_near, values_far = attend_back(
-        tables, query_low, key_all, value_all, heads_low, lse, grad_heads, groups, heads_local, head_dim
+        tables, query_low, kv_all, heads_low, lse, grad_heads, groups, heads_local, head_dim
     )
 
     keys_come, values_come = flip(keys_far, y_bit), flip(values_far, x_bit)
@@ -1167,7 +1128,7 @@
     grad_kv_proj = jnp.concatenate([grad_key_proj, grad_value_proj], axis=1)
     first_part = jnp.concatenate(
         [
-            slab_against(grad_query_proj, query_slabs) + slab_against(grad_kv_proj, kv_slabs),
+            against(grad_query_proj, query_maps) + against(grad_kv_proj, kv_maps),
             select * against(grad_query_proj, query_expand),
             select * against(grad_key_proj, key_widen_maps),
             select * against(grad_value_proj, value_widen_maps),
@@ -1175,10 +1136,10 @@
         axis=1,
     )
     input_own, first_grads = whole_call(
-        lambda *refs: last_kernel(*refs, **style),
+        last_kernel,
         (
-            moved_back(own_half(first_part), weight_back),
-            moved_back(other_core(low(other_half(first_part))), weight_back),
+            own_half(first_part),
+            other_core(low(other_half(first_part))),
             tokens,
             gains,
             grad_scaled,
@@ -1186,8 +1147,8 @@
             first_shrink,
         ),
         (wide_f32, jax.ShapeDtypeStruct((3, grad_rows, width), grad_type)),
-        scratch=(work_space, work_space, kept_space),
-        tables=(half, weight_back_table, own_pick),
+        scratch=(kept_space,),
+        tables=(half, own_pick),
         specs={2: half_spec},
     )
 

time: 784 us -> 710 us (0.906)
  waiting for transfers between devices: 373 us -> 323 us
  other arithmetic: 72.8 us -> 47.2 us
  between operations: 15.1 us -> 28.1 us
  Pallas kernels: 133 us -> 123 us
    ppermute x41 -> x26, waiting for transfers between devices: 225 us -> 191 us  [flip(): lax.ppermute(value, 'ctx', [(i, i ^ 1 << bit) for i in range(count_ctx)])]
    concatenate x20 -> x6, other arithmetic: 27.9 us -> 3.63 us  [joined(): return jnp.concatenate([own, arrived], axis=0)]
    ppermute x21, waiting for transfers between devices: 109 us -> 84.8 us  [to_member(): lax.ppermute(value, 'ctx', [(d, d ^ 2 * member) for d in range(count_ctx)])]
    pallas_call x4, Pallas kernels: 81.2 us -> 68.9 us  [feed_call(): pl.pallas_call(lambda *refs: kernel(*refs, pieces=len(weights[0]), width=...]
    ppermute x41 -> x26, starting transfers between devices: 50.3 us -> 46.7 us  [flip(): lax.ppermute(value, 'ctx', [(i, i ^ 1 << bit) for i in range(count_ctx)])]
    unnamed x246 -> x194, local copies, waits for them, and re-layouts: 18.3 us -> 17.8 us
  transfers between devices with their start and end apart: 99 -> 86, of which waited for: 48 -> 45; matrix products, arithmetic and copies ran while one was open for 14% -> 12% of each run, Pallas kernels for 9% -> 10%
where the time goes in v3:
time: 710 us; the launch traced here: 701 us
  waiting for transfers between devices  323 us (45%)
  Pallas kernels  123 us (17%)
  starting transfers between devices  105 us (15%)
  local copies, waits for them, and re-layouts  47.5 us (7%)
  other arithmetic  47.2 us (7%)
  between operations  28.1 us (4%)
  matrix products  26.6 us (4%)
    ppermute x26, waiting for transfers between devices, flip(): lax.ppermute(value, 'ctx', [(i, i ^ 1 << bit) for i in range(count_ctx)])  191 us
    ppermute x21, waiting for transfers between devices, to_member(): lax.ppermute(value, 'ctx', [(d, d ^ 2 * member) for d in range(count_ctx)])  84.8 us
    pallas_call x4, Pallas kernels, feed_call(): pl.pallas_call(lambda *refs: kernel(*refs, pieces=len(weights[0]), width=...  68.9 us
    ppermute x26, starting transfers between devices, flip(): lax.ppermute(value, 'ctx', [(i, i ^ 1 << bit) for i in range(count_ctx)])  46.7 us
    ppermute x21, starting transfers between devices, to_member(): lax.ppermute(value, 'ctx', [(d, d ^ 2 * member) for d in range(count_ctx)])  28.8 us
    pallas_call x5, Pallas kernels, whole_call(): pl.pallas_call(kernel, grid_spec=pltpu.PrefetchScalarGridSpec(num_scalar_...  28.4 us
    pallas_call x1, Pallas kernels, attend_back(): pl.pallas_call(lambda *refs: attend_back_kernel(*refs, heads=heads, dim=d...  17.9 us
    unnamed x194, local copies, waits for them, and re-layouts  17.8 us
  transfers between devices with their start and end apart: 86, of which 45 were waited for; matrix products, arithmetic and copies ran while one was open for 12% of the time, Pallas kernels for 10%

profile of v3, /device:TPU:16, one launch (start us, length us, event | category | flops | bytes accessed | tf_op | source)
XLA Modules:
  0.0 700.6 jit_solution(8197280175807202088)
XLA Ops:
  26.8 5.7 collective-permute-done.3
  32.5 9.2 %collective-permute-start.1 = (bf16[256,1024]{1,0:T(8,128)(2,1)S(1)}, bf16[256,1024]{1,0:T(8,128)(2,1)}, u32[]{:S(2)}, u32[]{:S(2)}) collective-permute-start(bf16[256,1024]{1,0:T(8,128)(2,1)S(1)} %pad_maximum_fusion.4.refs_10_.refs_15_), channel_id=1, source_target_pairs={{0,16},{2,18},{4,20},{6,22},{8,24},{10,26},{12,28},{14,30},{16,0},... | collective-permute-start | bytes 1572872 | tf_op jit(solution)/shard_map/ppermute | solution.py:655
  54.4 43.1 %collective-permute-done.1.refs_12_.refs_17_ = bf16[256,1024]{1,0:T(8,128)(2,1)} collective-permute-done((bf16[256,1024]{1,0:T(8,128)(2,1)S(1)}, bf16[256,1024]{1,0:T(8,128)(2,1)}, u32[]{:S(2)}, u32[]{:S(2)}) %collective-permute-start.1) | collective-permute-done | bytes 524320 | tf_op jit(solution)/shard_map/ppermute | solution.py:655
  107.3 15.4 %collective-permute-done.4.refs_13_.refs_18_ = bf16[256,1024]{1,0:T(8,128)(2,1)} collective-permute-done((bf16[256,1024]{1,0:T(8,128)(2,1)}, bf16[256,1024]{1,0:T(8,128)(2,1)}, u32[]{:S(2)}, u32[]{:S(2)}) %collective-permute-start.4) | collective-permute-done | bytes 524320 | tf_op jit(solution)/shard_map/ppermute | solution.py:655
  122.7 30.1 %collective-permute-done.8.refs_20_.refs_25_ = bf16[256,1024]{1,0:T(8,128)(2,1)} collective-permute-done((bf16[256,1024]{1,0:T(8,128)(2,1)S(1)}, bf16[256,1024]{1,0:T(8,128)(2,1)}, u32[]{:S(2)}, u32[]{:S(2)}) %collective-permute-start.8) | collective-permute-done | bytes 524320 | tf_op jit(solution)/shard_map/ppermute | solution.py:655
  165.8 6.5 collective-permute-done.17
  184.6 17.3 %collective-permute-done.18 = bf16[256,1024]{0,1:T(8,128)(2,1)S(1)} collective-permute-done((bf16[256,1024]{0,1:T(8,128)(2,1)}, bf16[256,1024]{0,1:T(8,128)(2,1)S(1)}, u32[]{:S(2)}, u32[]{:S(2)}) %collective-permute-start.18) | collective-permute-done | bytes 524320 | tf_op jit(solution)/shard_map/ppermute | solution.py:655
  211.5 22.9 %collective-permute-done.19 = bf16[512,1024]{0,1:T(8,128)(2,1)S(1)} collective-permute-done((bf16[512,1024]{0,1:T(8,128)(2,1)S(1)}, bf16[512,1024]{0,1:T(8,128)(2,1)S(1)}, u32[]{:S(2)}, u32[]{:S(2)}) %collective-permute-start.19) | collective-permute-done | bytes 1048608 | tf_op jit(solution)/shard_map/ppermute | solution.py:655
  252.2 13.0 %collective-permute-done.21.refs_17_.refs_22_ = bf16[256,1024]{1,0:T(8,128)(2,1)} collective-permute-done((bf16[256,1024]{1,0:T(8,128)(2,1)}, bf16[256,1024]{1,0:T(8,128)(2,1)}, u32[]{:S(2)}, u32[]{:S(2)}) %collective-permute-start.21) | collective-permute-done | bytes 524320 | tf_op jit(solution)/shard_map/ppermute | solution.py:655
  267.1 13.2 %collective-permute-done.20.refs_24_.refs_29_ = bf16[256,1024]{1,0:T(8,128)(2,1)} collective-permute-done((bf16[256,1024]{1,0:T(8,128)(2,1)}, bf16[256,1024]{1,0:T(8,128)(2,1)}, u32[]{:S(2)}, u32[]{:S(2)}) %collective-permute-start.20) | collective-permute-done | bytes 524320 | tf_op jit(solution)/shard_map/ppermute | solution.py:655
  281.0 10.5 %collective-permute-done.22.refs_30_.refs_35_ = bf16[256,1024]{1,0:T(8,128)(2,1)} collective-permute-done((bf16[256,1024]{1,0:T(8,128)(2,1)S(1)}, bf16[256,1024]{1,0:T(8,128)(2,1)}, u32[]{:S(2)}, u32[]{:S(2)}) %collective-permute-start.22) | collective-permute-done | bytes 524320 | tf_op jit(solution)/shard_map/ppermute | solution.py:655
  299.6 7.6 %shard_map.438 = (bf16[256,1024]{1,0:T(8,128)(2,1)S(1)}, f32[256,128]{1,0:T(8,128)S(1)}) custom-call(s32[1]{0:T(128)} %bitcast.36.refs_0_, s32[1,9]{1,0:T(1,128)S(1)} %bitcast.193, s32[1,9]{1,0:T(1,128)S(1)} %get-tuple-element.252.refs_2_, s32[1,9]{1,0:T(1,128)S(1)} %get-tuple-element.251.refs_3_, bf16[256,1024]{1,0:T(8,128)(2,1)S(1)} %bitcast.191, ...), custom_call_target="tpu_custom_call" | custom-call | flops 2415919104 | bytes 6291456 | tf_op jit(solution)/shard_map/pallas_call | solution.py:163
  322.0 5.5 shard_map.439
  345.1 10.2 %collective-permute-done.32.refs_4_ = bf16[128,2048]{1,0:T(8,128)(2,1)} collective-permute-done((bf16[128,2048]{1,0:T(8,128)(2,1)}, bf16[128,2048]{1,0:T(8,128)(2,1)}, u32[]{:S(2)}, u32[]{:S(2)}) %collective-permute-start.32) | collective-permute-done | bytes 524320 | tf_op jit(solution)/shard_map/ppermute | solution.py:712
  358.0 16.9 %shard_map.441 = (bf16[512,256]{1,0:T(8,128)(2,1)}, bf16[512,1024]{1,0:T(8,128)(2,1)}, bf16[512,1024]{1,0:T(8,128)(2,1)}, bf16[512,1024]{1,0:T(8,128)(2,1)}, bf16[512,2176]{1,0:T(8,128)(2,1)}) custom-call(s32[16]{0:T(128)} %stack.155.refs_0_, bf16[128,2048]{1,0:T(8,128)(2,1)} %collective-permute-done.35.refs_1_, ...), custom_call_target="tpu_custom_call" | custom-call | flops 6442450944 | bytes 20971520 | tf_op jit(solution)/shard_map/pallas_call | solution.py:490
  375.5 16.8 %shard_map.440 = (bf16[512,256]{1,0:T(8,128)(2,1)}, bf16[512,1024]{1,0:T(8,128)(2,1)}, bf16[512,1024]{1,0:T(8,128)(2,1)}, bf16[512,1024]{1,0:T(8,128)(2,1)}, bf16[512,2176]{1,0:T(8,128)(2,1)}) custom-call(s32[16]{0:T(128)} %stack.155.refs_0_, bf16[128,2048]{1,0:T(8,128)(2,1)} %get-tuple-element.124.refs_1_.refs_10_, ...), custom_call_target="tpu_custom_call" | custom-call | flops 6442450944 | bytes 20971520 | tf_op jit(solution)/shard_map/pallas_call | solution.py:490
  399.5 12.6 %collective-permute-done.40.near_ref = bf16[128,2176]{1,0:T(8,128)(2,1)} collective-permute-done((bf16[128,2176]{1,0:T(8,128)(2,1)}, bf16[128,2176]{1,0:T(8,128)(2,1)}, u32[]{:S(2)}, u32[]{:S(2)}) %collective-permute-start.40) | collective-permute-done | bytes 557088 | tf_op jit(solution)/shard_map/ppermute | solution.py:712
  412.1 11.2 %collective-permute-done.41.y_ref = bf16[128,2176]{1,0:T(8,128)(2,1)} collective-permute-done((bf16[128,2176]{1,0:T(8,128)(2,1)S(1)}, bf16[128,2176]{1,0:T(8,128)(2,1)}, u32[]{:S(2)}, u32[]{:S(2)}) %collective-permute-start.41) | collective-permute-done | bytes 557088 | tf_op jit(solution)/shard_map/ppermute | solution.py:712
  423.5 6.7 shard_map.442
  433.7 10.7 %collective-permute-done.44.refs_2_ = bf16[128,2048]{1,0:T(8,128)(2,1)S(1)} collective-permute-done((bf16[128,2048]{1,0:T(8,128)(2,1)}, bf16[128,2048]{1,0:T(8,128)(2,1)S(1)}, u32[]{:S(2)}, u32[]{:S(2)}) %collective-permute-start.44) | collective-permute-done | bytes 524320 | tf_op jit(solution)/shard_map/ppermute | solution.py:712
  446.6 9.9 %collective-permute-done.46.refs_4_ = bf16[128,2048]{1,0:T(8,128)(2,1)S(1)} collective-permute-done((bf16[128,2048]{1,0:T(8,128)(2,1)}, bf16[128,2048]{1,0:T(8,128)(2,1)S(1)}, u32[]{:S(2)}, u32[]{:S(2)}) %collective-permute-start.46) | collective-permute-done | bytes 524320 | tf_op jit(solution)/shard_map/ppermute | solution.py:712
  459.8 17.8 %shard_map.443 = (bf16[512,2304]{1,0:T(8,128)(2,1)}, f32[3,128,1024]{2,1,0:T(8,128)}) custom-call(s32[16]{0:T(128)} %stack.155.refs_0_, bf16[128,2048]{1,0:T(8,128)(2,1)} %copy-done.81, bf16[128,2048]{1,0:T(8,128)(2,1)} %copy-done.82, bf16[128,2048]{1,0:T(8,128)(2,1)} %copy-done.83, bf16[128,2048]{1,0:T(8,128)(2,1)} %copy-done.84, ...), custom_call_target="tpu_custom_call" | custom-call | flops 6442450944 | bytes 20971520 | tf_op jit(solution)/shard_map/pallas_call | solution.py:490
  478.2 17.4 %shard_map.444 = (bf16[512,2304]{1,0:T(8,128)(2,1)}, f32[3,128,1024]{2,1,0:T(8,128)}) custom-call(s32[16]{0:T(128)} %stack.155.refs_0_, bf16[128,2048]{1,0:T(8,128)(2,1)} %get-tuple-element.146.refs_1_, bf16[128,2048]{1,0:T(8,128)(2,1)} %copy-done.78, bf16[128,2048]{1,0:T(8,128)(2,1)} %copy-done.79, bf16[128,2048]{1,0:T(8,128)(2,1)} %copy-done.80, ...), custom_call_target="tpu_custom_call" | custom-call | flops 6442450944 | bytes 20971520 | tf_op jit(solution)/shard_map/pallas_call | solution.py:490
  516.3 11.7 %collective-permute-done.53.refs_3_ = bf16[128,2304]{1,0:T(8,128)(2,1)S(1)} collective-permute-done((bf16[128,2304]{1,0:T(8,128)(2,1)}, bf16[128,2304]{1,0:T(8,128)(2,1)S(1)}, u32[]{:S(2)}, u32[]{:S(2)}) %collective-permute-start.53) | collective-permute-done | bytes 589856 | tf_op jit(solution)/shard_map/ppermute | solution.py:712
  528.9 7.9 %shard_map.445 = (bf16[128,2176]{1,0:T(8,128)(2,1)}, f32[128,2048]{1,0:T(8,128)}, f32[128,2048]{1,0:T(8,128)}, bf16[3,16,2048]{2,1,0:T(8,128)(2,1)}) custom-call(s32[16]{0:T(128)} %stack.182.refs_0_, s32[1]{0:T(128)} %bitcast.3.pick_ref.refs_1_, bf16[128,2304]{1,0:T(8,128)(2,1)} %copy-done.31, bf16[128,2304]{1,0:T(8,128)(2,1)} %copy-done.32, ...), custom_call_target="tpu_custom_call" | custom-call | flops 1000000000 | bytes 9322496 | tf_op jit(solution)/shard_map/pallas_call | solution.py:247
  541.0 6.2 all-to-all-start
  557.2 17.9 %shard_map.446 = (f32[256,1024]{1,0:T(8,128)S(1)}, bf16[8,1,256,256]{3,2,1,0:T(8,128)(2,1)S(1)}, bf16[8,1,256,256]{3,2,1,0:T(8,128)(2,1)}, bf16[8,1,256,256]{3,2,1,0:T(8,128)(2,1)S(1)}, bf16[8,1,256,256]{3,2,1,0:T(8,128)(2,1)}) custom-call(s32[1]{0:T(128)} %bitcast.36.refs_0_, s32[1,9]{1,0:T(1,128)S(1)} %bitcast.194, s32[1,9]{1,0:T(1,128)S(1)} %get-tuple-element.252.refs_2_, ...), custom_call_target="tpu_custom_call" | custom-call | flops 6039797760 | bytes 12582912 | tf_op jit(solution)/shard_map/pallas_call | solution.py:192
  597.9 5.6 collective-permute-done.80
  613.5 7.4 %collective-permute-done.57 = bf16[4,1,256,256]{3,2,1,0:T(8,128)(2,1)S(1)} collective-permute-done((bf16[4,1,256,256]{3,2,1,0:T(8,128)(2,1)S(1)}, bf16[4,1,256,256]{3,2,1,0:T(8,128)(2,1)S(1)}, u32[]{:S(2)}, u32[]{:S(2)}) %collective-permute-start.57) | collective-permute-done | bytes 524320 | tf_op jit(solution)/shard_map/ppermute | solution.py:655
  631.6 9.9 %collective-permute-done.60 = bf16[1,256,256]{2,1,0:T(8,128)(2,1)S(1)} collective-permute-done((bf16[1,256,256]{2,1,0:T(8,128)(2,1)S(1)}, bf16[1,256,256]{2,1,0:T(8,128)(2,1)S(1)}, u32[]{:S(2)}, u32[]{:S(2)}) %collective-permute-start.60) | collective-permute-done | bytes 131104 | tf_op jit(solution)/shard_map/ppermute | solution.py:1115
  669.3 7.8 %collective-permute-done.71 = bf16[2,20,2048]{2,1,0:T(8,128)(2,1)S(1)} collective-permute-done((bf16[2,20,2048]{2,1,0:T(8,128)(2,1)S(1)}, bf16[2,20,2048]{2,1,0:T(8,128)(2,1)S(1)}, u32[]{:S(2)}, u32[]{:S(2)}) %collective-permute-start.71) | collective-permute-done | bytes 163872 | tf_op jit(solution)/shard_map/ppermute | solution.py:1201
  677.1 5.3 collective-permute-done.72
  (497 shorter events, 262.6 us)
Async XLA Ops:
  7.2 148.5 %all-gather.3.cloned.1.call-start = ((), (), s32[]{:S(2)}) async-start(), calls=%async_computation.1 | async-start | bytes 6684672 | tf_op jit(solution)/shard_map/all_gather | solution.py:898
  9.2 288.2 %all-gather.5.cloned.1.call-start = ((), (), s32[]{:S(2)}) async-start(), calls=%async_computation.2 | async-start | bytes 4456448 | tf_op jit(solution)/shard_map/all_gather | solution.py:919
  12.3 30.0 %collective-permute-start.7 = (bf16[128,1024]{1,0:T(8,128)(2,1)S(1)}, bf16[128,1024]{1,0:T(8,128)(2,1)S(1)}, u32[]{:S(2)}, u32[]{:S(2)}) collective-permute-start(bf16[128,1024]{1,0:T(8,128)(2,1)S(1)} %get-tuple-element.206), channel_id=1, source_target_pairs={{0,4},{2,6},{4,0},{6,2},{8,12},{10,14},{12,8},{14,10},{16,20},{18,... | collective-permute-start | bytes 786440 | tf_op jit(solution)/shard_map/ppermute | solution.py:712
  15.9 31.6 %collective-permute-start.10 = (bf16[128,1024]{1,0:T(8,128)(2,1)S(1)}, bf16[128,1024]{1,0:T(8,128)(2,1)S(1)}, u32[]{:S(2)}, u32[]{:S(2)}) collective-permute-start(bf16[128,1024]{1,0:T(8,128)(2,1)S(1)} %get-tuple-element.208), channel_id=1, source_target_pairs={{0,8},{2,10},{4,12},{6,14},{8,0},{10,2},{12,4},{14,6},{16,24},{18,... | collective-permute-start | bytes 786440 | tf_op jit(solution)/shard_map/ppermute | solution.py:712
  22.5 28.0 %collective-permute-start.11 = (bf16[128,1024]{1,0:T(8,128)(2,1)S(1)}, bf16[128,1024]{1,0:T(8,128)(2,1)S(1)}, u32[]{:S(2)}, u32[]{:S(2)}) collective-permute-start(bf16[128,1024]{1,0:T(8,128)(2,1)S(1)} %get-tuple-element.205), channel_id=1, source_target_pairs={{0,12},{2,14},{4,8},{6,10},{8,4},{10,6},{12,0},{14,2},{16,28},{18,... | collective-permute-start | bytes 786440 | tf_op jit(solution)/shard_map/ppermute | solution.py:712
  32.5 65.0 %collective-permute-start.1 = (bf16[256,1024]{1,0:T(8,128)(2,1)S(1)}, bf16[256,1024]{1,0:T(8,128)(2,1)}, u32[]{:S(2)}, u32[]{:S(2)}) collective-permute-start(bf16[256,1024]{1,0:T(8,128)(2,1)S(1)} %pad_maximum_fusion.4.refs_10_.refs_15_), channel_id=1, source_target_pairs={{0,16},{2,18},{4,20},{6,22},{8,24},{10,26},{12,28},{14,30},{16,0},... | collective-permute-start | bytes 1572872 | tf_op jit(solution)/shard_map/ppermute | solution.py:655
  43.9 57.1 %collective-permute-start.9 = (bf16[256,1024]{1,0:T(8,128)(2,1)S(1)}, bf16[256,1024]{1,0:T(8,128)(2,1)}, u32[]{:S(2)}, u32[]{:S(2)}) collective-permute-start(bf16[256,1024]{1,0:T(8,128)(2,1)S(1)} %pad_maximum_fusion.5.refs_18_.refs_23_), channel_id=1, source_target_pairs={{0,2},{2,0},{4,6},{6,4},{8,10},{10,8},{12,14},{14,12},{16,18},{18,... | collective-permute-start | bytes 1572872 | tf_op jit(solution)/shard_map/ppermute | solution.py:655
  47.5 75.2 %collective-permute-start.4 = (bf16[256,1024]{1,0:T(8,128)(2,1)}, bf16[256,1024]{1,0:T(8,128)(2,1)}, u32[]{:S(2)}, u32[]{:S(2)}) collective-permute-start(bf16[256,1024]{1,0:T(8,128)(2,1)} %constant_dynamic-update-slice_fusion.3.refs_11_.refs_16_), channel_id=1, source_target_pairs={{0,16},{2,18},{4,20},{6,22},{8,24},{10,26},{12,28},{14,30},{16,0},... | collective-permute-start | bytes 1572872 | tf_op jit(solution)/shard_map/ppermute | solution.py:655
  53.0 69.7 %collective-permute-start.12 = (bf16[256,1024]{1,0:T(8,128)(2,1)S(1)}, bf16[256,1024]{1,0:T(8,128)(2,1)S(1)}, u32[]{:S(2)}, u32[]{:S(2)}) collective-permute-start(bf16[256,1024]{1,0:T(8,128)(2,1)S(1)} %constant_dynamic-update-slice_fusion.5.refs_19_.refs_24_), channel_id=1, source_target_pairs={{0,2},{2,0},{4,6},{6,4},{8,10},{10,8},{12,14},{14,12},{16,18},{18,... | collective-permute-start | bytes 1572872 | tf_op jit(solution)/shard_map/ppermute | solution.py:655
  97.5 55.3 %collective-permute-start.8 = (bf16[256,1024]{1,0:T(8,128)(2,1)S(1)}, bf16[256,1024]{1,0:T(8,128)(2,1)}, u32[]{:S(2)}, u32[]{:S(2)}) collective-permute-start(bf16[256,1024]{1,0:T(8,128)(2,1)S(1)} %pad_maximum_fusion.5.refs_18_.refs_23_), channel_id=1, source_target_pairs={{0,16},{2,18},{4,20},{6,22},{8,24},{10,26},{12,28},{14,30},{16,0},... | collective-permute-start | bytes 1572872 | tf_op jit(solution)/shard_map/ppermute | solution.py:655
  101.0 51.8 %collective-permute-start.13 = (bf16[256,1024]{1,0:T(8,128)(2,1)}, bf16[256,1024]{1,0:T(8,128)(2,1)}, u32[]{:S(2)}, u32[]{:S(2)}) collective-permute-start(bf16[256,1024]{1,0:T(8,128)(2,1)} %collective-permute-done.1.refs_12_.refs_17_), channel_id=1, source_target_pairs={{0,2},{2,0},{4,6},{6,4},{8,10},{10,8},{12,14},{14,12},{16,18},{18,... | collective-permute-start | bytes 1572872 | tf_op jit(solution)/shard_map/ppermute | solution.py:655
  173.2 28.7 %collective-permute-start.18 = (bf16[256,1024]{0,1:T(8,128)(2,1)}, bf16[256,1024]{0,1:T(8,128)(2,1)S(1)}, u32[]{:S(2)}, u32[]{:S(2)}) collective-permute-start(bf16[256,1024]{0,1:T(8,128)(2,1)} %pad_maximum_fusion.7), channel_id=1, source_target_pairs={{0,16},{2,18},{4,20},{6,22},{8,24},{10,26},{12,28},{14,30},{16,0},... | collective-permute-start | bytes 1572872 | tf_op jit(solution)/shard_map/ppermute | solution.py:655
  177.9 59.9 %collective-permute-start.14 = (bf16[128,1024]{1,0:T(8,128)(2,1)}, bf16[128,1024]{1,0:T(8,128)(2,1)}, u32[]{:S(2)}, u32[]{:S(2)}) collective-permute-start(bf16[128,1024]{1,0:T(8,128)(2,1)} %bitcast.44), channel_id=1, source_target_pairs={{0,4},{2,6},{4,0},{6,2},{8,12},{10,14},{12,8},{14,10},{16,20},{18,... | collective-permute-start | bytes 786440 | tf_op jit(solution)/shard_map/ppermute | solution.py:712
  178.8 57.3 %collective-permute-start.24 = (bf16[128,1024]{1,0:T(8,128)(2,1)}, bf16[128,1024]{1,0:T(8,128)(2,1)}, u32[]{:S(2)}, u32[]{:S(2)}) collective-permute-start(bf16[128,1024]{1,0:T(8,128)(2,1)} %bitcast.46), channel_id=1, source_target_pairs={{0,8},{2,10},{4,12},{6,14},{8,0},{10,2},{12,4},{14,6},{16,24},{18,... | collective-permute-start | bytes 786440 | tf_op jit(solution)/shard_map/ppermute | solution.py:712
  180.4 60.0 %collective-permute-start.25 = (bf16[128,1024]{1,0:T(8,128)(2,1)}, bf16[128,1024]{1,0:T(8,128)(2,1)}, u32[]{:S(2)}, u32[]{:S(2)}) collective-permute-start(bf16[128,1024]{1,0:T(8,128)(2,1)} %bitcast.47), channel_id=1, source_target_pairs={{0,12},{2,14},{4,8},{6,10},{8,4},{10,6},{12,0},{14,2},{16,28},{18,... | collective-permute-start | bytes 786440 | tf_op jit(solution)/shard_map/ppermute | solution.py:712
  202.0 32.5 %collective-permute-start.19 = (bf16[512,1024]{0,1:T(8,128)(2,1)S(1)}, bf16[512,1024]{0,1:T(8,128)(2,1)S(1)}, u32[]{:S(2)}, u32[]{:S(2)}) collective-permute-start(bf16[512,1024]{0,1:T(8,128)(2,1)S(1)} %pad_maximum_fusion.3), channel_id=1, source_target_pairs={{0,2},{2,0},{4,6},{6,4},{8,10},{10,8},{12,14},{14,12},{16,18},{18,... | collective-permute-start | bytes 3145736 | tf_op jit(solution)/shard_map/ppermute | solution.py:655
  208.3 33.8 %collective-permute-start.15 = (bf16[256,1024]{1,0:T(8,128)(2,1)}, bf16[256,1024]{1,0:T(8,128)(2,1)}, u32[]{:S(2)}, u32[]{:S(2)}) collective-permute-start(bf16[256,1024]{1,0:T(8,128)(2,1)} %copy-done.49), channel_id=1, source_target_pairs={{0,16},{2,18},{4,20},{6,22},{8,24},{10,26},{12,28},{14,30},{16,0},... | collective-permute-start | bytes 1572872 | tf_op jit(solution)/shard_map/ppermute | solution.py:655
  236.1 72.6 %collective-permute-start.23 = (bf16[1024,1024]{0,1:T(8,128)(2,1)}, bf16[1024,1024]{0,1:T(8,128)(2,1)}, u32[]{:S(2)}, u32[]{:S(2)}) collective-permute-start(bf16[1024,1024]{0,1:T(8,128)(2,1)} %pad_maximum_fusion.2), channel_id=1, source_target_pairs={{0,4},{2,6},{4,0},{6,2},{8,12},{10,14},{12,8},{14,10},{16,20},{18,... | collective-permute-start | bytes 6291464 | tf_op jit(solution)/shard_map/ppermute | solution.py:655
  238.8 26.3 %collective-permute-start.21 = (bf16[256,1024]{1,0:T(8,128)(2,1)}, bf16[256,1024]{1,0:T(8,128)(2,1)}, u32[]{:S(2)}, u32[]{:S(2)}) collective-permute-start(bf16[256,1024]{1,0:T(8,128)(2,1)} %collective-permute-done.4.refs_13_.refs_18_), channel_id=1, source_target_pairs={{0,2},{2,0},{4,6},{6,4},{8,10},{10,8},{12,14},{14,12},{16,18},{18,... | collective-permute-start | bytes 1572872 | tf_op jit(solution)/shard_map/ppermute | solution.py:655
  242.1 55.3 %collective-permute-start.16 = (bf16[256,1024]{1,0:T(8,128)(2,1)S(1)}, bf16[256,1024]{1,0:T(8,128)(2,1)}, u32[]{:S(2)}, u32[]{:S(2)}) collective-permute-start(bf16[256,1024]{1,0:T(8,128)(2,1)S(1)} %pad_maximum_fusion.6.refs_26_.refs_31_), channel_id=1, source_target_pairs={{0,16},{2,18},{4,20},{6,22},{8,24},{10,26},{12,28},{14,30},{16,0},... | collective-permute-start | bytes 1572872 | tf_op jit(solution)/shard_map/ppermute | solution.py:655
  244.5 64.1 %collective-permute-start.26 = (bf16[256,1024]{1,0:T(8,128)(2,1)}, bf16[256,1024]{1,0:T(8,128)(2,1)}, u32[]{:S(2)}, u32[]{:S(2)}) collective-permute-start(bf16[256,1024]{1,0:T(8,128)(2,1)} %constant_dynamic-update-slice_fusion.7.refs_27_.refs_32_), channel_id=1, source_target_pairs={{0,16},{2,18},{4,20},{6,22},{8,24},{10,26},{12,28},{14,30},{16,0},... | collective-permute-start | bytes 1572872 | tf_op jit(solution)/shard_map/ppermute | solution.py:655
  245.0 35.2 %collective-permute-start.20 = (bf16[256,1024]{1,0:T(8,128)(2,1)}, bf16[256,1024]{1,0:T(8,128)(2,1)}, u32[]{:S(2)}, u32[]{:S(2)}) collective-permute-start(bf16[256,1024]{1,0:T(8,128)(2,1)} %collective-permute-done.8.refs_20_.refs_25_), channel_id=1, source_target_pairs={{0,2},{2,0},{4,6},{6,4},{8,10},{10,8},{12,14},{14,12},{16,18},{18,... | collective-permute-start | bytes 1572872 | tf_op jit(solution)/shard_map/ppermute | solution.py:655
  265.2 26.3 %collective-permute-start.22 = (bf16[256,1024]{1,0:T(8,128)(2,1)S(1)}, bf16[256,1024]{1,0:T(8,128)(2,1)}, u32[]{:S(2)}, u32[]{:S(2)}) collective-permute-start(bf16[256,1024]{1,0:T(8,128)(2,1)S(1)} %pad_maximum_fusion.6.refs_26_.refs_31_), channel_id=1, source_target_pairs={{0,2},{2,0},{4,6},{6,4},{8,10},{10,8},{12,14},{14,12},{16,18},{18,... | collective-permute-start | bytes 1572872 | tf_op jit(solution)/shard_map/ppermute | solution.py:655
  280.2 28.4 %collective-permute-start.28 = (bf16[256,1024]{1,0:T(8,128)(2,1)}, bf16[256,1024]{1,0:T(8,128)(2,1)}, u32[]{:S(2)}, u32[]{:S(2)}) collective-permute-start(bf16[256,1024]{1,0:T(8,128)(2,1)} %constant_dynamic-update-slice_fusion.7.refs_27_.refs_32_), channel_id=1, source_target_pairs={{0,2},{2,0},{4,6},{6,4},{8,10},{10,8},{12,14},{14,12},{16,18},{18,... | collective-permute-start | bytes 1572872 | tf_op jit(solution)/shard_map/ppermute | solution.py:655
  477.8 35.6 %collective-permute-start.43 = (bf16[128,2048]{1,0:T(8,128)(2,1)}, bf16[128,2048]{1,0:T(8,128)(2,1)}, u32[]{:S(2)}, u32[]{:S(2)}) collective-permute-start(bf16[128,2048]{1,0:T(8,128)(2,1)} %get-tuple-element.144), channel_id=1, source_target_pairs={{0,1},{1,0},{2,3},{3,2},{4,5},{5,4},{6,7},{7,6},{8,9},{9,8},{10,11... | collective-permute-start | bytes 1572872 | tf_op jit(solution)/shard_map/ppermute | solution.py:658
  500.2 27.8 %collective-permute-start.53 = (bf16[128,2304]{1,0:T(8,128)(2,1)}, bf16[128,2304]{1,0:T(8,128)(2,1)S(1)}, u32[]{:S(2)}, u32[]{:S(2)}) collective-permute-start(bf16[128,2304]{1,0:T(8,128)(2,1)} %get-tuple-element.189), channel_id=1, source_target_pairs={{0,4},{2,6},{4,0},{6,2},{8,12},{10,14},{12,8},{14,10},{16,20},{18,... | collective-permute-start | bytes 1769480 | tf_op jit(solution)/shard_map/ppermute | solution.py:712
  541.0 65.7 %all-to-all-start = ((bf16[16,24,1024]{2,1,0:T(8,128)(2,1)}), bf16[16,24,1024]{2,1,0:T(8,128)(2,1)}, u32[]{:S(2)}, u32[]{:S(2)}) async-start(bf16[16,24,1024]{2,1,0:T(8,128)(2,1)} %copy_bitcast_fusion), calls=%async_computation | async-start | bytes 1572864 | tf_op jit(solution)/shard_map/all_to_all | solution.py:1171
  548.6 43.5 %collective-permute-start.77 = (bf16[2,24,2048]{2,1,0:T(8,128)(2,1)}, bf16[2,24,2048]{2,1,0:T(8,128)(2,1)}, u32[]{:S(2)}, u32[]{:S(2)}) collective-permute-start(bf16[2,24,2048]{2,1,0:T(8,128)(2,1)} %fusion.43), channel_id=1, source_target_pairs={{0,8},{2,10},{4,12},{6,14},{8,0},{10,2},{12,4},{14,6},{16,24},{18,... | collective-permute-start | bytes 589832 | tf_op jit(solution)/shard_map/ppermute | solution.py:1201
  550.1 42.0 %collective-permute-start.78 = (bf16[2,24,2048]{2,1,0:T(8,128)(2,1)}, bf16[2,24,2048]{2,1,0:T(8,128)(2,1)}, u32[]{:S(2)}, u32[]{:S(2)}) collective-permute-start(bf16[2,24,2048]{2,1,0:T(8,128)(2,1)} %fusion.43), channel_id=1, source_target_pairs={{0,16},{2,18},{4,20},{6,22},{8,24},{10,26},{12,28},{14,30},{16,0},... | collective-permute-start | bytes 589832 | tf_op jit(solution)/shard_map/ppermute | solution.py:1201
  550.7 41.5 %collective-permute-start.79 = (bf16[2,24,2048]{2,1,0:T(8,128)(2,1)}, bf16[2,24,2048]{2,1,0:T(8,128)(2,1)}, u32[]{:S(2)}, u32[]{:S(2)}) collective-permute-start(bf16[2,24,2048]{2,1,0:T(8,128)(2,1)} %fusion.43), channel_id=1, source_target_pairs={{0,24},{2,26},{4,28},{6,30},{8,16},{10,18},{12,20},{14,22},{16,8},... | collective-permute-start | bytes 589832 | tf_op jit(solution)/shard_map/ppermute | solution.py:1201
  575.2 32.8 %collective-permute-start.56 = (bf16[8,1,256,256]{3,2,1,0:T(8,128)(2,1)}, bf16[8,1,256,256]{3,2,1,0:T(8,128)(2,1)}, u32[]{:S(2)}, u32[]{:S(2)}) collective-permute-start(bf16[8,1,256,256]{3,2,1,0:T(8,128)(2,1)} %get-tuple-element.170), channel_id=1, source_target_pairs={{0,4},{2,6},{4,0},{6,2},{8,12},{10,14},{12,8},{14,10},{16,20},{18,... | collective-permute-start | bytes 3145736 | tf_op jit(solution)/shard_map/ppermute | solution.py:655
  575.2 35.8 %collective-permute-start.61 = (bf16[8,1,256,256]{3,2,1,0:T(8,128)(2,1)}, bf16[8,1,256,256]{3,2,1,0:T(8,128)(2,1)}, u32[]{:S(2)}, u32[]{:S(2)}) collective-permute-start(bf16[8,1,256,256]{3,2,1,0:T(8,128)(2,1)} %get-tuple-element.172), channel_id=1, source_target_pairs={{0,2},{2,0},{4,6},{6,4},{8,10},{10,8},{12,14},{14,12},{16,18},{18,... | collective-permute-start | bytes 3145736 | tf_op jit(solution)/shard_map/ppermute | solution.py:655
  (144 other events, 2884.2 us)
Sparse Core Ops, SparseCore 0:
  11.4 144.2 all-gather.2
  161.2 134.6 all-gather.4

commit v4 on v3

--- a/solution.py
+++ b/solution.py
@@ -432,6 +432,12 @@
     return copies
 
 
+def put_halves(refs, value, start, table_ref, block):
+    half = refs[0].shape[0]
+    for i, ref in enumerate(refs):
+        put_columns(ref, value[i * half : (i + 1) * half], start, table_ref, block)
+
+
 def put_columns(out_ref, value, start, table_ref, block):
     size = value.shape[1]
     if block % 128:
@@ -445,7 +451,7 @@
 def feed_kernel(order_ref, *refs, pieces, width, count):
     parts, (select_ref, shrink_ref, gexp_ref, uexp_ref, dshr_ref), refs = refs[:4], refs[4:9], refs[9:]
     gates, ups, downs = refs[:pieces], refs[pieces : 2 * pieces], refs[2 * pieces : 3 * pieces]
-    rank_ref, act_ref, slope_ref, hid_ref, part_ref, x_ref, gate_w, up_w, down_w, sems = refs[3 * pieces :]
+    rank_ref, act_ref, slope_ref, hid_ref, near_ref, far_ref, x_ref, gate_w, up_w, down_w, sems = refs[3 * pieces :]
     arriving = bring(gates, gate_w, sems.at[0]) + bring(ups, up_w, sems.at[1])
     arriving_down = bring(downs, down_w, sems.at[2])
     ranks = select_ref.shape[1]
@@ -473,11 +479,13 @@
     @pl.loop(0, width // step)
     def _(i):
         start = pl.multiple_of(i * step, step)
-        put_columns(
-            part_ref, against(hid_ref[...], down_w[pl.ds(start, step), :]), start, order_ref, width // count
-        )
-
-    part_ref[:, width:] = (select_ref[...] * against(hid_ref[...], dshr_ref[...])).astype(part_ref.dtype)
+        found = against(hid_ref[...], down_w[pl.ds(start, step), :])
+        put_halves((near_ref, far_ref), found, start, order_ref, width // count)
+
+    found = low(select_ref[...] * against(hid_ref[...], dshr_ref[...]))
+    half = near_ref.shape[0]
+    near_ref[:, width:] = found[:half]
+    far_ref[:, width:] = found[half:]
 
 
 def feed_call(kernel, order, parts, inputs, weights, outputs, scratch, flops):
@@ -504,7 +512,7 @@
     )(order, *parts, *inputs, *pieces)
 
 
-def feed(order, parts, select, shrink, gexp, uexp, dshr, gates, ups, downs, out_dtype):
+def feed(order, parts, select, shrink, gexp, uexp, dshr, gates, ups, downs):
     rows, width = 4 * parts[0].shape[0], parts[0].shape[1]
     hidden, ranks = gexp.shape[1], select.shape[1]
     low_hidden = jax.ShapeDtypeStruct((rows, hidden), BF16)
@@ -519,7 +527,7 @@
             low_hidden,
             low_hidden,
             low_hidden,
-            jax.ShapeDtypeStruct((rows, width + ranks), out_dtype),
+            *[jax.ShapeDtypeStruct((rows // 2, width + ranks), BF16)] * 2,
         ),
         (pltpu.VMEM((rows, width), BF16),),
         6 * rows * width * hidden,
@@ -541,7 +549,7 @@
         dshr_ref,
     ), refs = refs[:10], refs[10:]
     gates, ups, downs = refs[:pieces], refs[pieces : 2 * pieces], refs[2 * pieces : 3 * pieces]
-    part_ref, grads_ref, g_ref, down_rank, gate_grad, up_grad, gate_w, up_w, down_w, sems = refs[3 * pieces :]
+    near_ref, far_ref, grads_ref, g_ref, down_rank, gate_grad, up_grad, gate_w, up_w, down_w, sems = refs[3 * pieces :]
     arriving = bring(downs, down_w, sems.at[2])
     arriving_next = bring(gates, gate_w, sems.at[0]) + bring(ups, up_w, sems.at[1])
     ranks = select_ref.shape[1]
@@ -574,14 +582,18 @@
         found = against(gate_grad[...], gate_w[pl.ds(start, step), :]) + against(
             up_grad[...], up_w[pl.ds(start, step), :]
         )
-        put_columns(part_ref, found, start, order_ref, width // count)
+        put_halves((near_ref, far_ref), found, start, order_ref, width // count)
 
     select = select_ref[...]
-    part_ref[:, width : width + ranks] = (select * against(gate_grad[...], gexp_ref[...])).astype(part_ref.dtype)
-    part_ref[:, width + ranks :] = (select * against(up_grad[...], uexp_ref[...])).astype(part_ref.dtype)
-
-
-def feed_back(order, parts, select, dexp, start, kept, gexp, uexp, dshr, gates, ups, downs, out_dtype):
+    gate_found = low(select * against(gate_grad[...], gexp_ref[...]))
+    up_found = low(select * against(up_grad[...], uexp_ref[...]))
+    half = near_ref.shape[0]
+    for i, ref in enumerate((near_ref, far_ref)):
+        ref[:, width : width + ranks] = gate_found[i * half : (i + 1) * half]
+        ref[:, width + ranks :] = up_found[i * half : (i + 1) * half]
+
+
+def feed_back(order, parts, select, dexp, start, kept, gexp, uexp, dshr, gates, ups, downs):
     rows, width = 4 * parts[0].shape[0], parts[0].shape[1]
     hidden, ranks = gexp.shape[1], select.shape[1]
     low_hidden = pltpu.VMEM((rows, hidden), BF16)
@@ -592,7 +604,7 @@
         (select, dexp, kept[0], start, *kept[1:], gexp, uexp, dshr),
         (gates, ups, downs),
         (
-            jax.ShapeDtypeStruct((rows, width + 2 * ranks), out_dtype),
+            *[jax.ShapeDtypeStruct((rows // 2, width + 2 * ranks), BF16)] * 2,
             jax.ShapeDtypeStruct((3, ranks, hidden), F32),
         ),
         (pltpu.VMEM((rows, width), BF16), pltpu.VMEM((rows, ranks), BF16), low_hidden, low_hidden),
@@ -761,8 +773,15 @@
     select = select_rows(picks_at(me))
     select_own = own_half(select)
     team_select = [select_rows(picks_at(me ^ (2 * t))) for t in range(4)]
-    select_near = jnp.concatenate([own_half(part) for part in team_select], axis=0)
-    select_far = jnp.concatenate([other_half(part) for part in team_select], axis=0)
+
+    def select_of(members):
+        return jnp.concatenate(
+            [own_half(team_select[m]) for m in members] + [other_half(team_select[m]) for m in members],
+            axis=0,
+        )
+
+    beside, across = (1, 2), (0, 3)
+    select_beside, select_across = select_of(beside), select_of(across)
 
     my_block = jnp.sum(jnp.where(device_ids[:, None] == me, block_of, 0), axis=0)
     positions = (
@@ -989,17 +1008,27 @@
         (down_far_near_a, down_far_near_b),
     )
 
-    def team_gather(value):
-        near_parts = [to_member(value, member) for member in range(4)]
-        return near_parts, [other_core(part) for part in near_parts]
-
-    def team_sum(near_part, far_part):
-        arrived = other_core(far_part).astype(F32)
-        parts = []
-        for member in (3, 1, 2, 0):
-            rows = slice(member * half_rows, (member + 1) * half_rows)
-            parts.append(to_member(low(near_part[rows].astype(F32) + arrived[rows]), member))
-        return parts
+    def in_two_calls(value, call):
+        near_parts = [to_member(value, member) for member in (1, 2, 3)]
+        first_rows = near_parts[:2] + [other_core(part) for part in near_parts[:2]]
+        near_sum, far_sum, *kept_first = call(0, first_rows, None)
+        near_sum, far_sum, kept_first, last_part = step(
+            (near_sum, far_sum, tuple(kept_first), near_parts[2])
+        )
+        arrived = other_core(far_sum)
+        totals = [
+            low(near_sum[i * half_rows : (i + 1) * half_rows].astype(F32) + arrived[i * half_rows : (i + 1) * half_rows])
+            for i in range(2)
+        ]
+        second_rows = [value, last_part, other_core(value), other_core(last_part)]
+        totals, second_rows, kept_first = step((totals, second_rows, kept_first))
+        beside_parts = [to_member(total, member) for total, member in zip(totals, (1, 2))]
+        near_sum, far_sum, *kept_second = call(1, second_rows, kept_first)
+        far_sum, beside_parts = step((far_sum, beside_parts))
+        arrived = other_core(far_sum)
+        over = low(near_sum[half_rows:].astype(F32) + arrived[half_rows:])
+        own = low(near_sum[:half_rows].astype(F32) + arrived[:half_rows])
+        return [own] + beside_parts + [to_member(over, 3)], kept_first, kept_second
 
     def hidden_columns(value):
         return lax.dynamic_slice_in_dim(value, team_place * hidden_slice, hidden_slice, 1)
@@ -1009,14 +1038,15 @@
     slices = tuple(hidden_columns(value) for value in (gate_expand, up_expand, down_shrink))
     pieces = (gate_pieces, up_pieces, down_pieces)
 
-    second_near, second_far = team_gather(moved(second_low, team_order))
-    *kept_far, part_far = feed(
-        team_order_table, second_far, select_far, feed_maps, *slices, *pieces, BF16
-    )
-    *kept_near, part_near = feed(
-        team_order_table, second_near, select_near, feed_maps, *slices, *pieces, BF16
-    )
-    ffn_parts = team_sum(part_near, part_far)
+    selects = select_beside, select_across
+
+    def forward(index, rows, earlier):
+        *kept, near_part, far_part = feed(
+            team_order_table, rows, selects[index], feed_maps, *slices, *pieces
+        )
+        return near_part, far_part, *kept
+
+    ffn_parts, *kept_calls = in_two_calls(moved(second_low, team_order), forward)
 
     result_own, layer_input_own, grad_after, grad_ffn, down_expand_grad = whole_call(
         layer_kernel,
@@ -1045,15 +1075,21 @@
         },
     )
 
-    grad_near, grad_far = team_gather(moved(grad_ffn, team_order))
     nothing = jnp.zeros((3, adapter_width, hidden_slice), F32)
-    back_far, team_grads = feed_back(
-        team_order_table, grad_far, select_far, down_map, nothing, kept_far, *slices, *pieces, BF16
-    )
-    back_near, team_grads = feed_back(
-        team_order_table, grad_near, select_near, down_map, team_grads, kept_near, *slices, *pieces, BF16
-    )
-    second_parts = team_sum(back_near, back_far)
+
+    def backward(index, rows, earlier):
+        return feed_back(
+            team_order_table,
+            rows,
+            selects[index],
+            down_map,
+            nothing if earlier is None else earlier[0],
+            kept_calls[index],
+            *slices,
+            *pieces,
+        )
+
+    second_parts, _, (team_grads,) = in_two_calls(moved(grad_ffn, team_order), backward)
     second_parts, team_grads = step((second_parts, team_grads))
     grad_sent, grad_scaled, grad_first, own_grads = whole_call(
         lambda *refs: turn_kernel(*refs, **style),

time: 710 us -> 697 us (0.982)
  waiting for transfers between devices: 323 us -> 296 us
  starting transfers between devices: 105 us -> 113 us
    ppermute x21, waiting for transfers between devices: 84.8 us -> 38.1 us  [to_member(): lax.ppermute(value, 'ctx', [(d, d ^ 2 * member) for d in range(count_ctx)])]
    ppermute x18 -> x20, waiting for transfers between devices: 4.34 us -> 14.2 us  [other_core(): return lax.ppermute(value, 'wt', SWAP)]
    ppermute x26, waiting for transfers between devices: 191 us -> 200 us  [flip(): lax.ppermute(value, 'ctx', [(i, i ^ 1 << bit) for i in range(count_ctx)])]
    convert_element_type x15 -> x17, other arithmetic: 12.4 us -> 17.3 us  [low(): return value.astype(BF16)]
    unnamed x194 -> x202, local copies, waits for them, and re-layouts: 17.8 us -> 15.4 us
  transfers between devices with their start and end apart: 86 -> 88, of which waited for: 45 -> 43; matrix products, arithmetic and copies ran while one was open for 12% -> 14% of each run, Pallas kernels for 10% -> 14%
where the time goes in v4:
time: 697 us; the launch traced here: 687 us
  waiting for transfers between devices  296 us (42%)
  Pallas kernels  124 us (18%)
  starting transfers between devices  113 us (16%)
  other arithmetic  52.7 us (8%)
  local copies, waits for them, and re-layouts  45.4 us (7%)
  between operations  28.7 us (4%)
  matrix products  26.5 us (4%)
    ppermute x26, waiting for transfers between devices, flip(): lax.ppermute(value, 'ctx', [(i, i ^ 1 << bit) for i in range(count_ctx)])  200 us
    pallas_call x4, Pallas kernels, feed_call(): pl.pallas_call(lambda *refs: kernel(*refs, pieces=len(weights[0]), width=...  70.2 us
    ppermute x26, starting transfers between devices, flip(): lax.ppermute(value, 'ctx', [(i, i ^ 1 << bit) for i in range(count_ctx)])  48.8 us
    ppermute x21, waiting for transfers between devices, to_member(): lax.ppermute(value, 'ctx', [(d, d ^ 2 * member) for d in range(count_ctx)])  38.1 us
    ppermute x21, starting transfers between devices, to_member(): lax.ppermute(value, 'ctx', [(d, d ^ 2 * member) for d in range(count_ctx)])  32.6 us
    pallas_call x5, Pallas kernels, whole_call(): pl.pallas_call(kernel, grid_spec=pltpu.PrefetchScalarGridSpec(num_scalar_...  28.2 us
    pallas_call x1, Pallas kernels, attend_back(): pl.pallas_call(lambda *refs: attend_back_kernel(*refs, heads=heads, dim=d...  18 us
    convert_element_type x17, other arithmetic, low(): return value.astype(BF16)  17.3 us
  transfers between devices with their start and end apart: 88, of which 43 were waited for; matrix products, arithmetic and copies ran while one was open for 14% of the time, Pallas kernels for 14%

profile of v4, /device:TPU:16, one launch (start us, length us, event | category | flops | bytes accessed | tf_op | source)
XLA Modules:
  0.0 686.5 jit_solution(7142949035592813282)
XLA Ops:
  26.8 5.7 collective-permute-done.3
  32.5 9.2 %collective-permute-start.1 = (bf16[256,1024]{1,0:T(8,128)(2,1)S(1)}, bf16[256,1024]{1,0:T(8,128)(2,1)}, u32[]{:S(2)}, u32[]{:S(2)}) collective-permute-start(bf16[256,1024]{1,0:T(8,128)(2,1)S(1)} %pad_maximum_fusion.4.refs_10_.refs_15_), channel_id=1, source_target_pairs={{0,16},{2,18},{4,20},{6,22},{8,24},{10,26},{12,28},{14,30},{16,0},... | collective-permute-start | bytes 1572872 | tf_op jit(solution)/shard_map/ppermute | solution.py:667
  54.4 43.1 %collective-permute-done.1.refs_12_.refs_17_ = bf16[256,1024]{1,0:T(8,128)(2,1)} collective-permute-done((bf16[256,1024]{1,0:T(8,128)(2,1)S(1)}, bf16[256,1024]{1,0:T(8,128)(2,1)}, u32[]{:S(2)}, u32[]{:S(2)}) %collective-permute-start.1) | collective-permute-done | bytes 524320 | tf_op jit(solution)/shard_map/ppermute | solution.py:667
  107.3 15.4 %collective-permute-done.4.refs_13_.refs_18_ = bf16[256,1024]{1,0:T(8,128)(2,1)} collective-permute-done((bf16[256,1024]{1,0:T(8,128)(2,1)}, bf16[256,1024]{1,0:T(8,128)(2,1)}, u32[]{:S(2)}, u32[]{:S(2)}) %collective-permute-start.4) | collective-permute-done | bytes 524320 | tf_op jit(solution)/shard_map/ppermute | solution.py:667
  122.7 30.1 %collective-permute-done.8.refs_20_.refs_25_ = bf16[256,1024]{1,0:T(8,128)(2,1)} collective-permute-done((bf16[256,1024]{1,0:T(8,128)(2,1)S(1)}, bf16[256,1024]{1,0:T(8,128)(2,1)}, u32[]{:S(2)}, u32[]{:S(2)}) %collective-permute-start.8) | collective-permute-done | bytes 524320 | tf_op jit(solution)/shard_map/ppermute | solution.py:667
  161.1 4.7 collective-permute-start.17
  165.8 6.5 collective-permute-done.17
  184.6 17.3 %collective-permute-done.18 = bf16[256,1024]{0,1:T(8,128)(2,1)S(1)} collective-permute-done((bf16[256,1024]{0,1:T(8,128)(2,1)}, bf16[256,1024]{0,1:T(8,128)(2,1)S(1)}, u32[]{:S(2)}, u32[]{:S(2)}) %collective-permute-start.18) | collective-permute-done | bytes 524320 | tf_op jit(solution)/shard_map/ppermute | solution.py:667
  211.5 22.9 %collective-permute-done.19 = bf16[512,1024]{0,1:T(8,128)(2,1)S(1)} collective-permute-done((bf16[512,1024]{0,1:T(8,128)(2,1)S(1)}, bf16[512,1024]{0,1:T(8,128)(2,1)S(1)}, u32[]{:S(2)}, u32[]{:S(2)}) %collective-permute-start.19) | collective-permute-done | bytes 1048608 | tf_op jit(solution)/shard_map/ppermute | solution.py:667
  252.2 11.7 %collective-permute-done.21.refs_17_.refs_22_ = bf16[256,1024]{1,0:T(8,128)(2,1)} collective-permute-done((bf16[256,1024]{1,0:T(8,128)(2,1)}, bf16[256,1024]{1,0:T(8,128)(2,1)}, u32[]{:S(2)}, u32[]{:S(2)}) %collective-permute-start.21) | collective-permute-done | bytes 524320 | tf_op jit(solution)/shard_map/ppermute | solution.py:667
  267.3 12.9 %collective-permute-done.20.refs_24_.refs_29_ = bf16[256,1024]{1,0:T(8,128)(2,1)} collective-permute-done((bf16[256,1024]{1,0:T(8,128)(2,1)}, bf16[256,1024]{1,0:T(8,128)(2,1)}, u32[]{:S(2)}, u32[]{:S(2)}) %collective-permute-start.20) | collective-permute-done | bytes 524320 | tf_op jit(solution)/shard_map/ppermute | solution.py:667
  281.7 9.7 %collective-permute-done.22.refs_30_.refs_35_ = bf16[256,1024]{1,0:T(8,128)(2,1)} collective-permute-done((bf16[256,1024]{1,0:T(8,128)(2,1)S(1)}, bf16[256,1024]{1,0:T(8,128)(2,1)}, u32[]{:S(2)}, u32[]{:S(2)}) %collective-permute-start.22) | collective-permute-done | bytes 524320 | tf_op jit(solution)/shard_map/ppermute | solution.py:667
  293.7 5.0 collective-permute-done.16.refs_28_.refs_33_
  300.9 7.6 %shard_map.438 = (bf16[256,1024]{1,0:T(8,128)(2,1)S(1)}, f32[256,128]{1,0:T(8,128)S(1)}) custom-call(s32[1]{0:T(128)} %bitcast.36.refs_0_, s32[1,9]{1,0:T(1,128)S(1)} %bitcast.193, s32[1,9]{1,0:T(1,128)S(1)} %get-tuple-element.328.refs_2_, s32[1,9]{1,0:T(1,128)S(1)} %get-tuple-element.327.refs_3_, bf16[256,1024]{1,0:T(8,128)(2,1)S(1)} %bitcast.191, ...), custom_call_target="tpu_custom_call" | custom-call | flops 2415919104 | bytes 6291456 | tf_op jit(solution)/shard_map/pallas_call | solution.py:163
  321.8 5.4 shard_map.439
  351.5 9.9 %collective-permute-done.34.refs_32_.refs_37_ = bf16[256,1024]{1,0:T(8,128)(2,1)} collective-permute-done((bf16[256,1024]{1,0:T(8,128)(2,1)}, bf16[256,1024]{1,0:T(8,128)(2,1)}, u32[]{:S(2)}, u32[]{:S(2)}) %collective-permute-start.34) | collective-permute-done | bytes 524320 | tf_op jit(solution)/shard_map/ppermute | solution.py:667
  361.4 17.1 %shard_map.440 = (bf16[512,256]{1,0:T(8,128)(2,1)}, bf16[512,1024]{1,0:T(8,128)(2,1)}, bf16[512,1024]{1,0:T(8,128)(2,1)}, bf16[512,1024]{1,0:T(8,128)(2,1)}, bf1...) custom-call(s32[16]{0:T(128)} %stack.155.refs_0_, bf16[128,2048]{1,0:T(8,128)(2,1)} %collective-permute-done.30.refs_1_, ...), custom_call_target="tpu_custom_call" | custom-call | flops 6442450944 | bytes 20971520 | tf_op jit(solution)/shard_map/pallas_call | solution.py:498
  384.0 16.9 %shard_map.441 = (bf16[512,256]{1,0:T(8,128)(2,1)}, bf16[512,1024]{1,0:T(8,128)(2,1)}, bf16[512,1024]{1,0:T(8,128)(2,1)}, bf16[512,1024]{1,0:T(8,128)(2,1)}, bf1...) custom-call(s32[16]{0:T(128)} %stack.155.refs_0_, bf16[128,2048]{1,0:T(8,128)(2,1)} %get-tuple-element.192.refs_1_.refs_10_, ...), custom_call_target="tpu_custom_call" | custom-call | flops 6442450944 | bytes 20971520 | tf_op jit(solution)/shard_map/pallas_call | solution.py:498
  409.5 12.5 %collective-permute-done.43.yz_ref = bf16[128,2176]{1,0:T(8,128)(2,1)} collective-permute-done((bf16[128,2176]{1,0:T(8,128)(2,1)S(1)}, bf16[128,2176]{1,0:T(8,128)(2,1)}, u32[]{:S(2)}, u32[]{:S(2)}) %collective-permute-start.43) | collective-permute-done | bytes 557088 | tf_op jit(solution)/shard_map/ppermute | solution.py:724
  422.0 6.7 shard_map.442
  431.9 10.2 %collective-permute-done.45.refs_1_ = bf16[128,2048]{1,0:T(8,128)(2,1)S(1)} collective-permute-done((bf16[128,2048]{1,0:T(8,128)(2,1)}, bf16[128,2048]{1,0:T(8,128)(2,1)S(1)}, u32[]{:S(2)}, u32[]{:S(2)}) %collective-permute-start.45) | collective-permute-done | bytes 524320 | tf_op jit(solution)/shard_map/ppermute | solution.py:724
  446.7 18.2 %shard_map.443 = (bf16[256,2304]{1,0:T(8,128)(2,1)}, bf16[256,2304]{1,0:T(8,128)(2,1)}, f32[3,128,1024]{2,1,0:T(8,128)}) custom-call(s32[16]{0:T(128)} %stack.155.refs_0_, bf16[128,2048]{1,0:T(8,128)(2,1)} %copy-done.83, bf16[128,2048]{1,0:T(8,128)(2,1)} %copy-done.85, bf16[128,2048]{1,0:T(8,128)(2,1)} %copy-done.87, bf16[128,2048]{1,0:T(8,128)(2,1)} %copy-done.88, ...), custom_call_target="tpu_custom_call" | custom-call | flops 6442450944 | bytes 20971520 | tf_op jit(solution)/shard_map/pallas_call | solution.py:498
  473.6 18.0 %shard_map.444 = (bf16[256,2304]{1,0:T(8,128)(2,1)}, bf16[256,2304]{1,0:T(8,128)(2,1)}, f32[3,128,1024]{2,1,0:T(8,128)}) custom-call(s32[16]{0:T(128)} %stack.155.refs_0_, bf16[128,2048]{1,0:T(8,128)(2,1)} %get-tuple-element.218.refs_1_, bf16[128,2048]{1,0:T(8,128)(2,1)} %copy-done.79, bf16[128,2048]{1,0:T(8,128)(2,1)} %copy-done.81, ...), custom_call_target="tpu_custom_call" | custom-call | flops 6442450944 | bytes 20971520 | tf_op jit(solution)/shard_map/pallas_call | solution.py:498
  514.8 7.8 %shard_map.445 = (bf16[128,2176]{1,0:T(8,128)(2,1)}, f32[128,2048]{1,0:T(8,128)}, f32[128,2048]{1,0:T(8,128)}, bf16[3,16,2048]{2,1,0:T(8,128)(2,1)}) custom-call(s32[16]{0:T(128)} %stack.182.refs_0_, s32[1]{0:T(128)} %bitcast.3.pick_ref.refs_1_, bf16[128,2304]{1,0:T(8,128)(2,1)} %get-tuple-element.235.refs_2_, bf16[128,2304]{1,0:T(8,128)(2,1)} %copy-done.29, ...), custom_call_target="tpu_custom_call" | custom-call | flops 1000000000 | bytes 9322496 | tf_op jit(solution)/shard_map/pallas_call | solution.py:247
  526.8 6.6 all-to-all-start
  543.4 18.0 %shard_map.446 = (f32[256,1024]{1,0:T(8,128)S(1)}, bf16[8,1,256,256]{3,2,1,0:T(8,128)(2,1)S(1)}, bf16[8,1,256,256]{3,2,1,0:T(8,128)(2,1)}, bf16[8,1,256,256]{3,2,1,0:T(8,128)(2,1)S(1)}, bf16[8,1,256,256]{3,2,1,0:T(8,128)(2,1)}) custom-call(s32[1]{0:T(128)} %bitcast.36.refs_0_, s32[1,9]{1,0:T(1,128)S(1)} %bitcast.194, s32[1,9]{1,0:T(1,128)S(1)} %get-tuple-element.328.refs_2_, ...), custom_call_target="tpu_custom_call" | custom-call | flops 6039797760 | bytes 12582912 | tf_op jit(solution)/shard_map/pallas_call | solution.py:192
  582.8 7.0 %collective-permute-done.82 = bf16[24,2048]{1,0:T(8,128)(2,1)S(1)} collective-permute-done((bf16[24,2048]{1,0:T(8,128)(2,1)S(1)}, bf16[24,2048]{1,0:T(8,128)(2,1)S(1)}, u32[]{:S(2)}, u32[]{:S(2)}) %collective-permute-start.82) | collective-permute-done | bytes 98336 | tf_op jit(solution)/shard_map/ppermute | solution.py:1257
  599.8 6.5 collective-permute-done.59
  619.3 8.5 %collective-permute-done.62 = bf16[1,256,256]{2,1,0:T(8,128)(2,1)S(1)} collective-permute-done((bf16[1,256,256]{2,1,0:T(8,128)(2,1)S(1)}, bf16[1,256,256]{2,1,0:T(8,128)(2,1)S(1)}, u32[]{:S(2)}, u32[]{:S(2)}) %collective-permute-start.62) | collective-permute-done | bytes 131104 | tf_op jit(solution)/shard_map/ppermute | solution.py:1151
  639.6 4.8 shard_map.447
  655.4 7.9 %collective-permute-done.73 = bf16[2,20,2048]{2,1,0:T(8,128)(2,1)S(1)} collective-permute-done((bf16[2,20,2048]{2,1,0:T(8,128)(2,1)S(1)}, bf16[2,20,2048]{2,1,0:T(8,128)(2,1)S(1)}, u32[]{:S(2)}, u32[]{:S(2)}) %collective-permute-start.73) | collective-permute-done | bytes 163872 | tf_op jit(solution)/shard_map/ppermute | solution.py:1237
  663.4 4.9 collective-permute-done.74
  (510 shorter events, 269.1 us)
Async XLA Ops:
  7.2 148.5 %all-gather.3.cloned.1.call-start = ((), (), s32[]{:S(2)}) async-start(), calls=%async_computation.1 | async-start | bytes 6684672 | tf_op jit(solution)/shard_map/all_gather | solution.py:917
  9.2 289.5 %all-gather.5.cloned.1.call-start = ((), (), s32[]{:S(2)}) async-start(), calls=%async_computation.2 | async-start | bytes 4456448 | tf_op jit(solution)/shard_map/all_gather | solution.py:938
  12.3 30.0 %collective-permute-start.7 = (bf16[128,1024]{1,0:T(8,128)(2,1)S(1)}, bf16[128,1024]{1,0:T(8,128)(2,1)S(1)}, u32[]{:S(2)}, u32[]{:S(2)}) collective-permute-start(bf16[128,1024]{1,0:T(8,128)(2,1)S(1)} %get-tuple-element.282), channel_id=1, source_target_pairs={{0,4},{2,6},{4,0},{6,2},{8,12},{10,14},{12,8},{14,10},{16,20},{18,... | collective-permute-start | bytes 786440 | tf_op jit(solution)/shard_map/ppermute | solution.py:724
  15.9 31.5 %collective-permute-start.10 = (bf16[128,1024]{1,0:T(8,128)(2,1)S(1)}, bf16[128,1024]{1,0:T(8,128)(2,1)S(1)}, u32[]{:S(2)}, u32[]{:S(2)}) collective-permute-start(bf16[128,1024]{1,0:T(8,128)(2,1)S(1)} %get-tuple-element.284), channel_id=1, source_target_pairs={{0,8},{2,10},{4,12},{6,14},{8,0},{10,2},{12,4},{14,6},{16,24},{18,... | collective-permute-start | bytes 786440 | tf_op jit(solution)/shard_map/ppermute | solution.py:724
  22.5 28.0 %collective-permute-start.11 = (bf16[128,1024]{1,0:T(8,128)(2,1)S(1)}, bf16[128,1024]{1,0:T(8,128)(2,1)S(1)}, u32[]{:S(2)}, u32[]{:S(2)}) collective-permute-start(bf16[128,1024]{1,0:T(8,128)(2,1)S(1)} %get-tuple-element.281), channel_id=1, source_target_pairs={{0,12},{2,14},{4,8},{6,10},{8,4},{10,6},{12,0},{14,2},{16,28},{18,... | collective-permute-start | bytes 786440 | tf_op jit(solution)/shard_map/ppermute | solution.py:724
  32.5 65.0 %collective-permute-start.1 = (bf16[256,1024]{1,0:T(8,128)(2,1)S(1)}, bf16[256,1024]{1,0:T(8,128)(2,1)}, u32[]{:S(2)}, u32[]{:S(2)}) collective-permute-start(bf16[256,1024]{1,0:T(8,128)(2,1)S(1)} %pad_maximum_fusion.4.refs_10_.refs_15_), channel_id=1, source_target_pairs={{0,16},{2,18},{4,20},{6,22},{8,24},{10,26},{12,28},{14,30},{16,0},... | collective-permute-start | bytes 1572872 | tf_op jit(solution)/shard_map/ppermute | solution.py:667
  43.9 57.1 %collective-permute-start.9 = (bf16[256,1024]{1,0:T(8,128)(2,1)S(1)}, bf16[256,1024]{1,0:T(8,128)(2,1)}, u32[]{:S(2)}, u32[]{:S(2)}) collective-permute-start(bf16[256,1024]{1,0:T(8,128)(2,1)S(1)} %pad_maximum_fusion.5.refs_18_.refs_23_), channel_id=1, source_target_pairs={{0,2},{2,0},{4,6},{6,4},{8,10},{10,8},{12,14},{14,12},{16,18},{18,... | collective-permute-start | bytes 1572872 | tf_op jit(solution)/shard_map/ppermute | solution.py:667
  47.4 75.3 %collective-permute-start.4 = (bf16[256,1024]{1,0:T(8,128)(2,1)}, bf16[256,1024]{1,0:T(8,128)(2,1)}, u32[]{:S(2)}, u32[]{:S(2)}) collective-permute-start(bf16[256,1024]{1,0:T(8,128)(2,1)} %constant_dynamic-update-slice_fusion.3.refs_11_.refs_16_), channel_id=1, source_target_pairs={{0,16},{2,18},{4,20},{6,22},{8,24},{10,26},{12,28},{14,30},{16,0},... | collective-permute-start | bytes 1572872 | tf_op jit(solution)/shard_map/ppermute | solution.py:667
  52.9 69.8 %collective-permute-start.12 = (bf16[256,1024]{1,0:T(8,128)(2,1)S(1)}, bf16[256,1024]{1,0:T(8,128)(2,1)S(1)}, u32[]{:S(2)}, u32[]{:S(2)}) collective-permute-start(bf16[256,1024]{1,0:T(8,128)(2,1)S(1)} %constant_dynamic-update-slice_fusion.5.refs_19_.refs_24_), channel_id=1, source_target_pairs={{0,2},{2,0},{4,6},{6,4},{8,10},{10,8},{12,14},{14,12},{16,18},{18,... | collective-permute-start | bytes 1572872 | tf_op jit(solution)/shard_map/ppermute | solution.py:667
  97.5 55.3 %collective-permute-start.8 = (bf16[256,1024]{1,0:T(8,128)(2,1)S(1)}, bf16[256,1024]{1,0:T(8,128)(2,1)}, u32[]{:S(2)}, u32[]{:S(2)}) collective-permute-start(bf16[256,1024]{1,0:T(8,128)(2,1)S(1)} %pad_maximum_fusion.5.refs_18_.refs_23_), channel_id=1, source_target_pairs={{0,16},{2,18},{4,20},{6,22},{8,24},{10,26},{12,28},{14,30},{16,0},... | collective-permute-start | bytes 1572872 | tf_op jit(solution)/shard_map/ppermute | solution.py:667
  101.0 51.8 %collective-permute-start.13 = (bf16[256,1024]{1,0:T(8,128)(2,1)}, bf16[256,1024]{1,0:T(8,128)(2,1)}, u32[]{:S(2)}, u32[]{:S(2)}) collective-permute-start(bf16[256,1024]{1,0:T(8,128)(2,1)} %collective-permute-done.1.refs_12_.refs_17_), channel_id=1, source_target_pairs={{0,2},{2,0},{4,6},{6,4},{8,10},{10,8},{12,14},{14,12},{16,18},{18,... | collective-permute-start | bytes 1572872 | tf_op jit(solution)/shard_map/ppermute | solution.py:667
  173.2 28.7 %collective-permute-start.18 = (bf16[256,1024]{0,1:T(8,128)(2,1)}, bf16[256,1024]{0,1:T(8,128)(2,1)S(1)}, u32[]{:S(2)}, u32[]{:S(2)}) collective-permute-start(bf16[256,1024]{0,1:T(8,128)(2,1)} %pad_maximum_fusion.7), channel_id=1, source_target_pairs={{0,16},{2,18},{4,20},{6,22},{8,24},{10,26},{12,28},{14,30},{16,0},... | collective-permute-start | bytes 1572872 | tf_op jit(solution)/shard_map/ppermute | solution.py:667
  177.9 59.8 %collective-permute-start.14 = (bf16[128,1024]{1,0:T(8,128)(2,1)}, bf16[128,1024]{1,0:T(8,128)(2,1)}, u32[]{:S(2)}, u32[]{:S(2)}) collective-permute-start(bf16[128,1024]{1,0:T(8,128)(2,1)} %bitcast.44), channel_id=1, source_target_pairs={{0,4},{2,6},{4,0},{6,2},{8,12},{10,14},{12,8},{14,10},{16,20},{18,... | collective-permute-start | bytes 786440 | tf_op jit(solution)/shard_map/ppermute | solution.py:724
  178.8 57.2 %collective-permute-start.24 = (bf16[128,1024]{1,0:T(8,128)(2,1)}, bf16[128,1024]{1,0:T(8,128)(2,1)}, u32[]{:S(2)}, u32[]{:S(2)}) collective-permute-start(bf16[128,1024]{1,0:T(8,128)(2,1)} %bitcast.46), channel_id=1, source_target_pairs={{0,8},{2,10},{4,12},{6,14},{8,0},{10,2},{12,4},{14,6},{16,24},{18,... | collective-permute-start | bytes 786440 | tf_op jit(solution)/shard_map/ppermute | solution.py:724
  180.4 60.0 %collective-permute-start.25 = (bf16[128,1024]{1,0:T(8,128)(2,1)}, bf16[128,1024]{1,0:T(8,128)(2,1)}, u32[]{:S(2)}, u32[]{:S(2)}) collective-permute-start(bf16[128,1024]{1,0:T(8,128)(2,1)} %bitcast.47), channel_id=1, source_target_pairs={{0,12},{2,14},{4,8},{6,10},{8,4},{10,6},{12,0},{14,2},{16,28},{18,... | collective-permute-start | bytes 786440 | tf_op jit(solution)/shard_map/ppermute | solution.py:724
  202.0 32.4 %collective-permute-start.19 = (bf16[512,1024]{0,1:T(8,128)(2,1)S(1)}, bf16[512,1024]{0,1:T(8,128)(2,1)S(1)}, u32[]{:S(2)}, u32[]{:S(2)}) collective-permute-start(bf16[512,1024]{0,1:T(8,128)(2,1)S(1)} %pad_maximum_fusion.3), channel_id=1, source_target_pairs={{0,2},{2,0},{4,6},{6,4},{8,10},{10,8},{12,14},{14,12},{16,18},{18,... | collective-permute-start | bytes 3145736 | tf_op jit(solution)/shard_map/ppermute | solution.py:667
  208.2 33.9 %collective-permute-start.15 = (bf16[256,1024]{1,0:T(8,128)(2,1)}, bf16[256,1024]{1,0:T(8,128)(2,1)}, u32[]{:S(2)}, u32[]{:S(2)}) collective-permute-start(bf16[256,1024]{1,0:T(8,128)(2,1)} %copy-done.49), channel_id=1, source_target_pairs={{0,16},{2,18},{4,20},{6,22},{8,24},{10,26},{12,28},{14,30},{16,0},... | collective-permute-start | bytes 1572872 | tf_op jit(solution)/shard_map/ppermute | solution.py:667
  236.0 73.9 %collective-permute-start.23 = (bf16[1024,1024]{0,1:T(8,128)(2,1)}, bf16[1024,1024]{0,1:T(8,128)(2,1)}, u32[]{:S(2)}, u32[]{:S(2)}) collective-permute-start(bf16[1024,1024]{0,1:T(8,128)(2,1)} %pad_maximum_fusion.2), channel_id=1, source_target_pairs={{0,4},{2,6},{4,0},{6,2},{8,12},{10,14},{12,8},{14,10},{16,20},{18,... | collective-permute-start | bytes 6291464 | tf_op jit(solution)/shard_map/ppermute | solution.py:667
  238.8 25.1 %collective-permute-start.21 = (bf16[256,1024]{1,0:T(8,128)(2,1)}, bf16[256,1024]{1,0:T(8,128)(2,1)}, u32[]{:S(2)}, u32[]{:S(2)}) collective-permute-start(bf16[256,1024]{1,0:T(8,128)(2,1)} %collective-permute-done.4.refs_13_.refs_18_), channel_id=1, source_target_pairs={{0,2},{2,0},{4,6},{6,4},{8,10},{10,8},{12,14},{14,12},{16,18},{18,... | collective-permute-start | bytes 1572872 | tf_op jit(solution)/shard_map/ppermute | solution.py:667
  242.1 56.6 %collective-permute-start.16 = (bf16[256,1024]{1,0:T(8,128)(2,1)S(1)}, bf16[256,1024]{1,0:T(8,128)(2,1)}, u32[]{:S(2)}, u32[]{:S(2)}) collective-permute-start(bf16[256,1024]{1,0:T(8,128)(2,1)S(1)} %pad_maximum_fusion.6.refs_26_.refs_31_), channel_id=1, source_target_pairs={{0,16},{2,18},{4,20},{6,22},{8,24},{10,26},{12,28},{14,30},{16,0},... | collective-permute-start | bytes 1572872 | tf_op jit(solution)/shard_map/ppermute | solution.py:667
  245.4 64.5 %collective-permute-start.26 = (bf16[256,1024]{1,0:T(8,128)(2,1)}, bf16[256,1024]{1,0:T(8,128)(2,1)}, u32[]{:S(2)}, u32[]{:S(2)}) collective-permute-start(bf16[256,1024]{1,0:T(8,128)(2,1)} %constant_dynamic-update-slice_fusion.7.refs_27_.refs_32_), channel_id=1, source_target_pairs={{0,16},{2,18},{4,20},{6,22},{8,24},{10,26},{12,28},{14,30},{16,0},... | collective-permute-start | bytes 1572872 | tf_op jit(solution)/shard_map/ppermute | solution.py:667
  245.4 34.8 %collective-permute-start.20 = (bf16[256,1024]{1,0:T(8,128)(2,1)}, bf16[256,1024]{1,0:T(8,128)(2,1)}, u32[]{:S(2)}, u32[]{:S(2)}) collective-permute-start(bf16[256,1024]{1,0:T(8,128)(2,1)} %collective-permute-done.8.refs_20_.refs_25_), channel_id=1, source_target_pairs={{0,2},{2,0},{4,6},{6,4},{8,10},{10,8},{12,14},{14,12},{16,18},{18,... | collective-permute-start | bytes 1572872 | tf_op jit(solution)/shard_map/ppermute | solution.py:667
  263.9 27.6 %collective-permute-start.22 = (bf16[256,1024]{1,0:T(8,128)(2,1)S(1)}, bf16[256,1024]{1,0:T(8,128)(2,1)}, u32[]{:S(2)}, u32[]{:S(2)}) collective-permute-start(bf16[256,1024]{1,0:T(8,128)(2,1)S(1)} %pad_maximum_fusion.6.refs_26_.refs_31_), channel_id=1, source_target_pairs={{0,2},{2,0},{4,6},{6,4},{8,10},{10,8},{12,14},{14,12},{16,18},{18,... | collective-permute-start | bytes 1572872 | tf_op jit(solution)/shard_map/ppermute | solution.py:667
  280.2 29.7 %collective-permute-start.28 = (bf16[256,1024]{1,0:T(8,128)(2,1)}, bf16[256,1024]{1,0:T(8,128)(2,1)}, u32[]{:S(2)}, u32[]{:S(2)}) collective-permute-start(bf16[256,1024]{1,0:T(8,128)(2,1)} %constant_dynamic-update-slice_fusion.7.refs_27_.refs_32_), channel_id=1, source_target_pairs={{0,2},{2,0},{4,6},{6,4},{8,10},{10,8},{12,14},{14,12},{16,18},{18,... | collective-permute-start | bytes 1572872 | tf_op jit(solution)/shard_map/ppermute | solution.py:667
  345.8 32.7 %collective-permute-start.36 = (bf16[128,2048]{1,0:T(8,128)(2,1)}, bf16[128,2048]{1,0:T(8,128)(2,1)S(1)}, u32[]{:S(2)}, u32[]{:S(2)}) collective-permute-start(bf16[128,2048]{1,0:T(8,128)(2,1)} %get-tuple-element.192.refs_1_.refs_10_), channel_id=1, source_target_pairs={{0,12},{2,14},{4,8},{6,10},{8,4},{10,6},{12,0},{14,2},{16,28},{18,... | collective-permute-start | bytes 1572872 | tf_op jit(solution)/shard_map/ppermute | solution.py:724
  526.8 65.4 %all-to-all-start = ((bf16[16,24,1024]{2,1,0:T(8,128)(2,1)}), bf16[16,24,1024]{2,1,0:T(8,128)(2,1)}, u32[]{:S(2)}, u32[]{:S(2)}) async-start(bf16[16,24,1024]{2,1,0:T(8,128)(2,1)} %copy_bitcast_fusion), calls=%async_computation | async-start | bytes 1572864 | tf_op jit(solution)/shard_map/all_to_all | solution.py:1207
  534.9 42.1 %collective-permute-start.79 = (bf16[2,24,2048]{2,1,0:T(8,128)(2,1)}, bf16[2,24,2048]{2,1,0:T(8,128)(2,1)}, u32[]{:S(2)}, u32[]{:S(2)}) collective-permute-start(bf16[2,24,2048]{2,1,0:T(8,128)(2,1)} %fusion.35), channel_id=1, source_target_pairs={{0,8},{2,10},{4,12},{6,14},{8,0},{10,2},{12,4},{14,6},{16,24},{18,... | collective-permute-start | bytes 589832 | tf_op jit(solution)/shard_map/ppermute | solution.py:1237
  536.3 40.7 %collective-permute-start.80 = (bf16[2,24,2048]{2,1,0:T(8,128)(2,1)}, bf16[2,24,2048]{2,1,0:T(8,128)(2,1)}, u32[]{:S(2)}, u32[]{:S(2)}) collective-permute-start(bf16[2,24,2048]{2,1,0:T(8,128)(2,1)} %fusion.35), channel_id=1, source_target_pairs={{0,16},{2,18},{4,20},{6,22},{8,24},{10,26},{12,28},{14,30},{16,0},... | collective-permute-start | bytes 589832 | tf_op jit(solution)/shard_map/ppermute | solution.py:1237
  536.9 40.1 %collective-permute-start.81 = (bf16[2,24,2048]{2,1,0:T(8,128)(2,1)}, bf16[2,24,2048]{2,1,0:T(8,128)(2,1)}, u32[]{:S(2)}, u32[]{:S(2)}) collective-permute-start(bf16[2,24,2048]{2,1,0:T(8,128)(2,1)} %fusion.35), channel_id=1, source_target_pairs={{0,24},{2,26},{4,28},{6,30},{8,16},{10,18},{12,20},{14,22},{16,8},... | collective-permute-start | bytes 589832 | tf_op jit(solution)/shard_map/ppermute | solution.py:1237
  561.4 32.0 %collective-permute-start.58 = (bf16[8,1,256,256]{3,2,1,0:T(8,128)(2,1)}, bf16[8,1,256,256]{3,2,1,0:T(8,128)(2,1)}, u32[]{:S(2)}, u32[]{:S(2)}) collective-permute-start(bf16[8,1,256,256]{3,2,1,0:T(8,128)(2,1)} %get-tuple-element.246), channel_id=1, source_target_pairs={{0,4},{2,6},{4,0},{6,2},{8,12},{10,14},{12,8},{14,10},{16,20},{18,... | collective-permute-start | bytes 3145736 | tf_op jit(solution)/shard_map/ppermute | solution.py:667
  561.4 34.8 %collective-permute-start.63 = (bf16[8,1,256,256]{3,2,1,0:T(8,128)(2,1)}, bf16[8,1,256,256]{3,2,1,0:T(8,128)(2,1)}, u32[]{:S(2)}, u32[]{:S(2)}) collective-permute-start(bf16[8,1,256,256]{3,2,1,0:T(8,128)(2,1)} %get-tuple-element.248), channel_id=1, source_target_pairs={{0,2},{2,0},{4,6},{6,4},{8,10},{10,8},{12,14},{14,12},{16,18},{18,... | collective-permute-start | bytes 3145736 | tf_op jit(solution)/shard_map/ppermute | solution.py:667
  651.7 26.3 %collective-permute-start.69 = (f32[128,2048]{1,0:T(8,128)S(1)}, f32[128,2048]{1,0:T(8,128)S(1)}, u32[]{:S(2)}, u32[]{:S(2)}) collective-permute-start(f32[128,2048]{1,0:T(8,128)S(1)} %copy-done.20), channel_id=1, source_target_pairs={{0,1},{1,0},{2,3},{3,2},{4,5},{5,4},{6,7},{7,6},{8,9},{9,8},{10,11... | collective-permute-start | bytes 3145736 | tf_op jit(solution)/shard_map/ppermute | solution.py:670
  (150 other events, 2780.7 us)
Sparse Core Ops, SparseCore 0:
  11.4 144.2 all-gather.2
  161.2 136.2 all-gather.4

commit v5 on v4

--- a/solution.py
+++ b/solution.py
@@ -968,7 +968,7 @@
     attn_total, laurel_back, mid_stream, second_low, rank_out = whole_call(
         lambda *refs: middle_kernel(*refs, **style),
         (
-            moved_back(own_half(attn_part), weight_back),
+            moved_back(attn_part, weight_back),
             moved_back(other_core(other_half(attn_part)), weight_back),
             tokens,
             gains,
@@ -985,7 +985,10 @@
         ),
         scratch=(work_space,),
         tables=(half, weight_back_table),
-        specs={2: half_spec},
+        specs={
+            0: pl.BlockSpec((half_rows, width + adapter_width), lambda i, half, *_: (half[0], 0)),
+            2: half_spec,
+        },
     )
 
     def in_order(own, far, near_own, near_far):
@@ -1174,7 +1177,7 @@
     input_own, first_grads = whole_call(
         last_kernel,
         (
-            own_half(first_part),
+            first_part,
             other_core(low(other_half(first_part))),
             tokens,
             gains,
@@ -1185,7 +1188,10 @@
         (wide_f32, jax.ShapeDtypeStruct((3, grad_rows, width), grad_type)),
         scratch=(kept_space,),
         tables=(half, own_pick),
-        specs={2: half_spec},
+        specs={
+            0: pl.BlockSpec((half_rows, width + 3 * adapter_width), lambda i, half, *_: (half[0], 0)),
+            2: half_spec,
+        },
     )
 
     def scatter_split(grads):

time: 697 us -> 697 us (level)
  Pallas kernels: 124 us -> 106 us
  starting transfers between devices: 113 us -> 127 us
    ppermute x26, starting transfers between devices: 48.8 us -> 60.9 us  [flip(): lax.ppermute(value, 'ctx', [(i, i ^ 1 << bit) for i in range(count_ctx)])]
    pallas_call x1, Pallas kernels: 18 us -> 6.1 us  [attend_back(): pl.pallas_call(lambda *refs: attend_back_kernel(*refs, heads=heads, dim=d...]
    unnamed x202 -> x206, local copies, waits for them, and re-layouts: 15.4 us -> 17.2 us
  transfers between devices with their start and end apart: 88 -> 88, of which waited for: 43 -> 42; matrix products, arithmetic and copies ran while one was open for 14% -> 13% of each run, Pallas kernels for 14% -> 12%
where the time goes in v5:
time: 697 us; the launch traced here: 687 us
  waiting for transfers between devices  301 us (43%)
  starting transfers between devices  127 us (18%)
  Pallas kernels  106 us (15%)
  other arithmetic  52.9 us (8%)
  local copies, waits for them, and re-layouts  45.3 us (6%)
  between operations  28.7 us (4%)
  matrix products  26.4 us (4%)
    ppermute x26, waiting for transfers between devices, flip(): lax.ppermute(value, 'ctx', [(i, i ^ 1 << bit) for i in range(count_ctx)])  206 us
    pallas_call x4, Pallas kernels, feed_call(): pl.pallas_call(lambda *refs: kernel(*refs, pieces=len(weights[0]), width=...  69.9 us
    ppermute x26, starting transfers between devices, flip(): lax.ppermute(value, 'ctx', [(i, i ^ 1 << bit) for i in range(count_ctx)])  60.9 us
    ppermute x21, waiting for transfers between devices, to_member(): lax.ppermute(value, 'ctx', [(d, d ^ 2 * member) for d in range(count_ctx)])  38.1 us
    ppermute x21, starting transfers between devices, to_member(): lax.ppermute(value, 'ctx', [(d, d ^ 2 * member) for d in range(count_ctx)])  32.6 us
    pallas_call x5, Pallas kernels, whole_call(): pl.pallas_call(kernel, grid_spec=pltpu.PrefetchScalarGridSpec(num_scalar_...  28.4 us
    convert_element_type x17, other arithmetic, low(): return value.astype(BF16)  17.5 us
    unnamed x206, local copies, waits for them, and re-layouts  17.2 us
  transfers between devices with their start and end apart: 88, of which 42 were waited for; matrix products, arithmetic and copies ran while one was open for 13% of the time, Pallas kernels for 12%

profile of v5, /device:TPU:16, one launch (start us, length us, event | category | flops | bytes accessed | tf_op | source)
XLA Modules:
  0.0 687.2 jit_solution(11667292856511246308)
XLA Ops:
  26.7 5.7 collective-permute-done.3
  32.5 9.2 %collective-permute-start.1 = (bf16[256,1024]{1,0:T(8,128)(2,1)S(1)}, bf16[256,1024]{1,0:T(8,128)(2,1)}, u32[]{:S(2)}, u32[]{:S(2)}) collective-permute-start(bf16[256,1024]{1,0:T(8,128)(2,1)S(1)} %pad_maximum_fusion.4.refs_10_.refs_15_), channel_id=1, source_target_pairs={{0,16},{2,18},{4,20},{6,22},{8,24},{10,26},{12,28},{14,30},{16,0},... | collective-permute-start | bytes 1572872 | tf_op jit(solution)/shard_map/ppermute | solution.py:667
  54.3 43.2 %collective-permute-done.1.refs_12_.refs_17_ = bf16[256,1024]{1,0:T(8,128)(2,1)} collective-permute-done((bf16[256,1024]{1,0:T(8,128)(2,1)S(1)}, bf16[256,1024]{1,0:T(8,128)(2,1)}, u32[]{:S(2)}, u32[]{:S(2)}) %collective-permute-start.1) | collective-permute-done | bytes 524320 | tf_op jit(solution)/shard_map/ppermute | solution.py:667
  107.3 15.4 %collective-permute-done.4.refs_13_.refs_18_ = bf16[256,1024]{1,0:T(8,128)(2,1)} collective-permute-done((bf16[256,1024]{1,0:T(8,128)(2,1)}, bf16[256,1024]{1,0:T(8,128)(2,1)}, u32[]{:S(2)}, u32[]{:S(2)}) %collective-permute-start.4) | collective-permute-done | bytes 524320 | tf_op jit(solution)/shard_map/ppermute | solution.py:667
  122.7 30.1 %collective-permute-done.8.refs_20_.refs_25_ = bf16[256,1024]{1,0:T(8,128)(2,1)} collective-permute-done((bf16[256,1024]{1,0:T(8,128)(2,1)S(1)}, bf16[256,1024]{1,0:T(8,128)(2,1)}, u32[]{:S(2)}, u32[]{:S(2)}) %collective-permute-start.8) | collective-permute-done | bytes 524320 | tf_op jit(solution)/shard_map/ppermute | solution.py:667
  165.8 6.5 collective-permute-done.17
  184.6 17.3 %collective-permute-done.18 = bf16[256,1024]{0,1:T(8,128)(2,1)S(1)} collective-permute-done((bf16[256,1024]{0,1:T(8,128)(2,1)}, bf16[256,1024]{0,1:T(8,128)(2,1)S(1)}, u32[]{:S(2)}, u32[]{:S(2)}) %collective-permute-start.18) | collective-permute-done | bytes 524320 | tf_op jit(solution)/shard_map/ppermute | solution.py:667
  211.5 22.9 %collective-permute-done.19 = bf16[512,1024]{0,1:T(8,128)(2,1)S(1)} collective-permute-done((bf16[512,1024]{0,1:T(8,128)(2,1)S(1)}, bf16[512,1024]{0,1:T(8,128)(2,1)S(1)}, u32[]{:S(2)}, u32[]{:S(2)}) %collective-permute-start.19) | collective-permute-done | bytes 1048608 | tf_op jit(solution)/shard_map/ppermute | solution.py:667
  252.1 11.7 %collective-permute-done.21.refs_17_.refs_22_ = bf16[256,1024]{1,0:T(8,128)(2,1)} collective-permute-done((bf16[256,1024]{1,0:T(8,128)(2,1)}, bf16[256,1024]{1,0:T(8,128)(2,1)}, u32[]{:S(2)}, u32[]{:S(2)}) %collective-permute-start.21) | collective-permute-done | bytes 524320 | tf_op jit(solution)/shard_map/ppermute | solution.py:667
  267.3 12.9 %collective-permute-done.20.refs_24_.refs_29_ = bf16[256,1024]{1,0:T(8,128)(2,1)} collective-permute-done((bf16[256,1024]{1,0:T(8,128)(2,1)}, bf16[256,1024]{1,0:T(8,128)(2,1)}, u32[]{:S(2)}, u32[]{:S(2)}) %collective-permute-start.20) | collective-permute-done | bytes 524320 | tf_op jit(solution)/shard_map/ppermute | solution.py:667
  281.7 9.7 %collective-permute-done.22.refs_30_.refs_35_ = bf16[256,1024]{1,0:T(8,128)(2,1)} collective-permute-done((bf16[256,1024]{1,0:T(8,128)(2,1)S(1)}, bf16[256,1024]{1,0:T(8,128)(2,1)}, u32[]{:S(2)}, u32[]{:S(2)}) %collective-permute-start.22) | collective-permute-done | bytes 524320 | tf_op jit(solution)/shard_map/ppermute | solution.py:667
  293.6 5.0 collective-permute-done.16.refs_28_.refs_33_
  302.7 7.1 %collective-permute-done.26.refs_29_.refs_34_ = bf16[256,1024]{1,0:T(8,128)(2,1)} collective-permute-done((bf16[256,1024]{1,0:T(8,128)(2,1)}, bf16[256,1024]{1,0:T(8,128)(2,1)}, u32[]{:S(2)}, u32[]{:S(2)}) %collective-permute-start.26) | collective-permute-done | bytes 524320 | tf_op jit(solution)/shard_map/ppermute | solution.py:667
  322.6 5.5 shard_map.439
  352.4 9.9 %collective-permute-done.34.refs_32_.refs_37_ = bf16[256,1024]{1,0:T(8,128)(2,1)} collective-permute-done((bf16[256,1024]{1,0:T(8,128)(2,1)}, bf16[256,1024]{1,0:T(8,128)(2,1)}, u32[]{:S(2)}, u32[]{:S(2)}) %collective-permute-start.34) | collective-permute-done | bytes 524320 | tf_op jit(solution)/shard_map/ppermute | solution.py:667
  362.3 17.0 %shard_map.440 = (bf16[512,256]{1,0:T(8,128)(2,1)}, bf16[512,1024]{1,0:T(8,128)(2,1)}, bf16[512,1024]{1,0:T(8,128)(2,1)}, bf16[512,1024]{1,0:T(8,128)(2,1)}, bf1...) custom-call(s32[16]{0:T(128)} %stack.155.refs_0_, bf16[128,2048]{1,0:T(8,128)(2,1)} %collective-permute-done.30.refs_1_, ...), custom_call_target="tpu_custom_call" | custom-call | flops 6442450944 | bytes 20971520 | tf_op jit(solution)/shard_map/pallas_call | solution.py:498
  384.9 16.8 %shard_map.441 = (bf16[512,256]{1,0:T(8,128)(2,1)}, bf16[512,1024]{1,0:T(8,128)(2,1)}, bf16[512,1024]{1,0:T(8,128)(2,1)}, bf16[512,1024]{1,0:T(8,128)(2,1)}, bf1...) custom-call(s32[16]{0:T(128)} %stack.155.refs_0_, bf16[128,2048]{1,0:T(8,128)(2,1)} %get-tuple-element.192.refs_1_.refs_10_, ...), custom_call_target="tpu_custom_call" | custom-call | flops 6442450944 | bytes 20971520 | tf_op jit(solution)/shard_map/pallas_call | solution.py:498
  410.3 12.5 %collective-permute-done.43.yz_ref = bf16[128,2176]{1,0:T(8,128)(2,1)} collective-permute-done((bf16[128,2176]{1,0:T(8,128)(2,1)S(1)}, bf16[128,2176]{1,0:T(8,128)(2,1)}, u32[]{:S(2)}, u32[]{:S(2)}) %collective-permute-start.43) | collective-permute-done | bytes 557088 | tf_op jit(solution)/shard_map/ppermute | solution.py:724
  422.8 6.7 shard_map.442
  432.7 10.1 %collective-permute-done.45.refs_1_ = bf16[128,2048]{1,0:T(8,128)(2,1)S(1)} collective-permute-done((bf16[128,2048]{1,0:T(8,128)(2,1)}, bf16[128,2048]{1,0:T(8,128)(2,1)S(1)}, u32[]{:S(2)}, u32[]{:S(2)}) %collective-permute-start.45) | collective-permute-done | bytes 524320 | tf_op jit(solution)/shard_map/ppermute | solution.py:724
  447.5 18.2 %shard_map.443 = (bf16[256,2304]{1,0:T(8,128)(2,1)}, bf16[256,2304]{1,0:T(8,128)(2,1)}, f32[3,128,1024]{2,1,0:T(8,128)}) custom-call(s32[16]{0:T(128)} %stack.155.refs_0_, bf16[128,2048]{1,0:T(8,128)(2,1)} %copy-done.85, bf16[128,2048]{1,0:T(8,128)(2,1)} %copy-done.87, bf16[128,2048]{1,0:T(8,128)(2,1)} %copy-done.89, bf16[128,2048]{1,0:T(8,128)(2,1)} %copy-done.90, ...), custom_call_target="tpu_custom_call" | custom-call | flops 6442450944 | bytes 20971520 | tf_op jit(solution)/shard_map/pallas_call | solution.py:498
  474.3 17.8 %shard_map.444 = (bf16[256,2304]{1,0:T(8,128)(2,1)}, bf16[256,2304]{1,0:T(8,128)(2,1)}, f32[3,128,1024]{2,1,0:T(8,128)}) custom-call(s32[16]{0:T(128)} %stack.155.refs_0_, bf16[128,2048]{1,0:T(8,128)(2,1)} %get-tuple-element.218.refs_1_, bf16[128,2048]{1,0:T(8,128)(2,1)} %copy-done.81, bf16[128,2048]{1,0:T(8,128)(2,1)} %copy-done.83, ...), custom_call_target="tpu_custom_call" | custom-call | flops 6442450944 | bytes 20971520 | tf_op jit(solution)/shard_map/pallas_call | solution.py:498
  515.2 7.9 %shard_map.445 = (bf16[128,2176]{1,0:T(8,128)(2,1)}, f32[128,2048]{1,0:T(8,128)}, f32[128,2048]{1,0:T(8,128)}, bf16[3,16,2048]{2,1,0:T(8,128)(2,1)}) custom-call(s32[16]{0:T(128)} %stack.182.refs_0_, s32[1]{0:T(128)} %bitcast.3.pick_ref.refs_1_, bf16[128,2304]{1,0:T(8,128)(2,1)} %get-tuple-element.235.refs_2_, bf16[128,2304]{1,0:T(8,128)(2,1)} %copy-done.31, ...), custom_call_target="tpu_custom_call" | custom-call | flops 1000000000 | bytes 9322496 | tf_op jit(solution)/shard_map/pallas_call | solution.py:247
  527.3 6.7 all-to-all-start
  544.0 6.1 shard_map.446
  553.1 10.4 %collective-permute-start.63 = (bf16[8,1,256,256]{3,2,1,0:T(8,128)(2,1)}, bf16[8,1,256,256]{3,2,1,0:T(8,128)(2,1)}, u32[]{:S(2)}, u32[]{:S(2)}) collective-permute-start(bf16[8,1,256,256]{3,2,1,0:T(8,128)(2,1)} %get-tuple-element.248), channel_id=1, source_target_pairs={{0,2},{2,0},{4,6},{6,4},{8,10},{10,8},{12,14},{14,12},{16,18},{18,... | collective-permute-start | bytes 3145736 | tf_op jit(solution)/shard_map/ppermute | solution.py:667
  583.4 6.7 collective-permute-done.82
  600.5 6.4 collective-permute-done.59
  619.1 10.4 %collective-permute-done.62 = bf16[1,256,256]{2,1,0:T(8,128)(2,1)S(1)} collective-permute-done((bf16[1,256,256]{2,1,0:T(8,128)(2,1)S(1)}, bf16[1,256,256]{2,1,0:T(8,128)(2,1)S(1)}, u32[]{:S(2)}, u32[]{:S(2)}) %collective-permute-start.62) | collective-permute-done | bytes 131104 | tf_op jit(solution)/shard_map/ppermute | solution.py:1154
  640.9 4.8 shard_map.447
  656.5 7.8 %collective-permute-done.73 = bf16[2,20,2048]{2,1,0:T(8,128)(2,1)S(1)} collective-permute-done((bf16[2,20,2048]{2,1,0:T(8,128)(2,1)S(1)}, bf16[2,20,2048]{2,1,0:T(8,128)(2,1)S(1)}, u32[]{:S(2)}, u32[]{:S(2)}) %collective-permute-start.73) | collective-permute-done | bytes 163872 | tf_op jit(solution)/shard_map/ppermute | solution.py:1243
  664.4 5.2 collective-permute-done.74
  (513 shorter events, 274.6 us)
Async XLA Ops:
  7.2 148.5 %all-gather.3.cloned.1.call-start = ((), (), s32[]{:S(2)}) async-start(), calls=%async_computation.1 | async-start | bytes 6684672 | tf_op jit(solution)/shard_map/all_gather | solution.py:917
  9.2 289.5 %all-gather.5.cloned.1.call-start = ((), (), s32[]{:S(2)}) async-start(), calls=%async_computation.2 | async-start | bytes 4456448 | tf_op jit(solution)/shard_map/all_gather | solution.py:938
  12.3 30.0 %collective-permute-start.7 = (bf16[128,1024]{1,0:T(8,128)(2,1)S(1)}, bf16[128,1024]{1,0:T(8,128)(2,1)S(1)}, u32[]{:S(2)}, u32[]{:S(2)}) collective-permute-start(bf16[128,1024]{1,0:T(8,128)(2,1)S(1)} %get-tuple-element.280), channel_id=1, source_target_pairs={{0,4},{2,6},{4,0},{6,2},{8,12},{10,14},{12,8},{14,10},{16,20},{18,... | collective-permute-start | bytes 786440 | tf_op jit(solution)/shard_map/ppermute | solution.py:724
  15.9 31.5 %collective-permute-start.10 = (bf16[128,1024]{1,0:T(8,128)(2,1)S(1)}, bf16[128,1024]{1,0:T(8,128)(2,1)S(1)}, u32[]{:S(2)}, u32[]{:S(2)}) collective-permute-start(bf16[128,1024]{1,0:T(8,128)(2,1)S(1)} %get-tuple-element.282), channel_id=1, source_target_pairs={{0,8},{2,10},{4,12},{6,14},{8,0},{10,2},{12,4},{14,6},{16,24},{18,... | collective-permute-start | bytes 786440 | tf_op jit(solution)/shard_map/ppermute | solution.py:724
  22.5 28.0 %collective-permute-start.11 = (bf16[128,1024]{1,0:T(8,128)(2,1)S(1)}, bf16[128,1024]{1,0:T(8,128)(2,1)S(1)}, u32[]{:S(2)}, u32[]{:S(2)}) collective-permute-start(bf16[128,1024]{1,0:T(8,128)(2,1)S(1)} %get-tuple-element.279), channel_id=1, source_target_pairs={{0,12},{2,14},{4,8},{6,10},{8,4},{10,6},{12,0},{14,2},{16,28},{18,... | collective-permute-start | bytes 786440 | tf_op jit(solution)/shard_map/ppermute | solution.py:724
  32.5 65.0 %collective-permute-start.1 = (bf16[256,1024]{1,0:T(8,128)(2,1)S(1)}, bf16[256,1024]{1,0:T(8,128)(2,1)}, u32[]{:S(2)}, u32[]{:S(2)}) collective-permute-start(bf16[256,1024]{1,0:T(8,128)(2,1)S(1)} %pad_maximum_fusion.4.refs_10_.refs_15_), channel_id=1, source_target_pairs={{0,16},{2,18},{4,20},{6,22},{8,24},{10,26},{12,28},{14,30},{16,0},... | collective-permute-start | bytes 1572872 | tf_op jit(solution)/shard_map/ppermute | solution.py:667
  43.9 57.1 %collective-permute-start.9 = (bf16[256,1024]{1,0:T(8,128)(2,1)S(1)}, bf16[256,1024]{1,0:T(8,128)(2,1)}, u32[]{:S(2)}, u32[]{:S(2)}) collective-permute-start(bf16[256,1024]{1,0:T(8,128)(2,1)S(1)} %pad_maximum_fusion.5.refs_18_.refs_23_), channel_id=1, source_target_pairs={{0,2},{2,0},{4,6},{6,4},{8,10},{10,8},{12,14},{14,12},{16,18},{18,... | collective-permute-start | bytes 1572872 | tf_op jit(solution)/shard_map/ppermute | solution.py:667
  47.4 75.3 %collective-permute-start.4 = (bf16[256,1024]{1,0:T(8,128)(2,1)}, bf16[256,1024]{1,0:T(8,128)(2,1)}, u32[]{:S(2)}, u32[]{:S(2)}) collective-permute-start(bf16[256,1024]{1,0:T(8,128)(2,1)} %constant_dynamic-update-slice_fusion.3.refs_11_.refs_16_), channel_id=1, source_target_pairs={{0,16},{2,18},{4,20},{6,22},{8,24},{10,26},{12,28},{14,30},{16,0},... | collective-permute-start | bytes 1572872 | tf_op jit(solution)/shard_map/ppermute | solution.py:667
  52.8 69.8 %collective-permute-start.12 = (bf16[256,1024]{1,0:T(8,128)(2,1)S(1)}, bf16[256,1024]{1,0:T(8,128)(2,1)S(1)}, u32[]{:S(2)}, u32[]{:S(2)}) collective-permute-start(bf16[256,1024]{1,0:T(8,128)(2,1)S(1)} %constant_dynamic-update-slice_fusion.5.refs_19_.refs_24_), channel_id=1, source_target_pairs={{0,2},{2,0},{4,6},{6,4},{8,10},{10,8},{12,14},{14,12},{16,18},{18,... | collective-permute-start | bytes 1572872 | tf_op jit(solution)/shard_map/ppermute | solution.py:667
  97.5 55.3 %collective-permute-start.8 = (bf16[256,1024]{1,0:T(8,128)(2,1)S(1)}, bf16[256,1024]{1,0:T(8,128)(2,1)}, u32[]{:S(2)}, u32[]{:S(2)}) collective-permute-start(bf16[256,1024]{1,0:T(8,128)(2,1)S(1)} %pad_maximum_fusion.5.refs_18_.refs_23_), channel_id=1, source_target_pairs={{0,16},{2,18},{4,20},{6,22},{8,24},{10,26},{12,28},{14,30},{16,0},... | collective-permute-start | bytes 1572872 | tf_op jit(solution)/shard_map/ppermute | solution.py:667
  101.0 51.8 %collective-permute-start.13 = (bf16[256,1024]{1,0:T(8,128)(2,1)}, bf16[256,1024]{1,0:T(8,128)(2,1)}, u32[]{:S(2)}, u32[]{:S(2)}) collective-permute-start(bf16[256,1024]{1,0:T(8,128)(2,1)} %collective-permute-done.1.refs_12_.refs_17_), channel_id=1, source_target_pairs={{0,2},{2,0},{4,6},{6,4},{8,10},{10,8},{12,14},{14,12},{16,18},{18,... | collective-permute-start | bytes 1572872 | tf_op jit(solution)/shard_map/ppermute | solution.py:667
  173.2 28.7 %collective-permute-start.18 = (bf16[256,1024]{0,1:T(8,128)(2,1)}, bf16[256,1024]{0,1:T(8,128)(2,1)S(1)}, u32[]{:S(2)}, u32[]{:S(2)}) collective-permute-start(bf16[256,1024]{0,1:T(8,128)(2,1)} %pad_maximum_fusion.7), channel_id=1, source_target_pairs={{0,16},{2,18},{4,20},{6,22},{8,24},{10,26},{12,28},{14,30},{16,0},... | collective-permute-start | bytes 1572872 | tf_op jit(solution)/shard_map/ppermute | solution.py:667
  177.9 59.8 %collective-permute-start.14 = (bf16[128,1024]{1,0:T(8,128)(2,1)}, bf16[128,1024]{1,0:T(8,128)(2,1)}, u32[]{:S(2)}, u32[]{:S(2)}) collective-permute-start(bf16[128,1024]{1,0:T(8,128)(2,1)} %bitcast.44), channel_id=1, source_target_pairs={{0,4},{2,6},{4,0},{6,2},{8,12},{10,14},{12,8},{14,10},{16,20},{18,... | collective-permute-start | bytes 786440 | tf_op jit(solution)/shard_map/ppermute | solution.py:724
  178.8 57.2 %collective-permute-start.24 = (bf16[128,1024]{1,0:T(8,128)(2,1)}, bf16[128,1024]{1,0:T(8,128)(2,1)}, u32[]{:S(2)}, u32[]{:S(2)}) collective-permute-start(bf16[128,1024]{1,0:T(8,128)(2,1)} %bitcast.46), channel_id=1, source_target_pairs={{0,8},{2,10},{4,12},{6,14},{8,0},{10,2},{12,4},{14,6},{16,24},{18,... | collective-permute-start | bytes 786440 | tf_op jit(solution)/shard_map/ppermute | solution.py:724
  180.4 60.0 %collective-permute-start.25 = (bf16[128,1024]{1,0:T(8,128)(2,1)}, bf16[128,1024]{1,0:T(8,128)(2,1)}, u32[]{:S(2)}, u32[]{:S(2)}) collective-permute-start(bf16[128,1024]{1,0:T(8,128)(2,1)} %bitcast.47), channel_id=1, source_target_pairs={{0,12},{2,14},{4,8},{6,10},{8,4},{10,6},{12,0},{14,2},{16,28},{18,... | collective-permute-start | bytes 786440 | tf_op jit(solution)/shard_map/ppermute | solution.py:724
  202.0 32.4 %collective-permute-start.19 = (bf16[512,1024]{0,1:T(8,128)(2,1)S(1)}, bf16[512,1024]{0,1:T(8,128)(2,1)S(1)}, u32[]{:S(2)}, u32[]{:S(2)}) collective-permute-start(bf16[512,1024]{0,1:T(8,128)(2,1)S(1)} %pad_maximum_fusion.3), channel_id=1, source_target_pairs={{0,2},{2,0},{4,6},{6,4},{8,10},{10,8},{12,14},{14,12},{16,18},{18,... | collective-permute-start | bytes 3145736 | tf_op jit(solution)/shard_map/ppermute | solution.py:667
  208.2 33.9 %collective-permute-start.15 = (bf16[256,1024]{1,0:T(8,128)(2,1)}, bf16[256,1024]{1,0:T(8,128)(2,1)}, u32[]{:S(2)}, u32[]{:S(2)}) collective-permute-start(bf16[256,1024]{1,0:T(8,128)(2,1)} %copy-done.51), channel_id=1, source_target_pairs={{0,16},{2,18},{4,20},{6,22},{8,24},{10,26},{12,28},{14,30},{16,0},... | collective-permute-start | bytes 1572872 | tf_op jit(solution)/shard_map/ppermute | solution.py:667
  236.0 73.9 %collective-permute-start.23 = (bf16[1024,1024]{0,1:T(8,128)(2,1)}, bf16[1024,1024]{0,1:T(8,128)(2,1)}, u32[]{:S(2)}, u32[]{:S(2)}) collective-permute-start(bf16[1024,1024]{0,1:T(8,128)(2,1)} %pad_maximum_fusion.2), channel_id=1, source_target_pairs={{0,4},{2,6},{4,0},{6,2},{8,12},{10,14},{12,8},{14,10},{16,20},{18,... | collective-permute-start | bytes 6291464 | tf_op jit(solution)/shard_map/ppermute | solution.py:667
  238.8 25.0 %collective-permute-start.21 = (bf16[256,1024]{1,0:T(8,128)(2,1)}, bf16[256,1024]{1,0:T(8,128)(2,1)}, u32[]{:S(2)}, u32[]{:S(2)}) collective-permute-start(bf16[256,1024]{1,0:T(8,128)(2,1)} %collective-permute-done.4.refs_13_.refs_18_), channel_id=1, source_target_pairs={{0,2},{2,0},{4,6},{6,4},{8,10},{10,8},{12,14},{14,12},{16,18},{18,... | collective-permute-start | bytes 1572872 | tf_op jit(solution)/shard_map/ppermute | solution.py:667
  242.0 56.7 %collective-permute-start.16 = (bf16[256,1024]{1,0:T(8,128)(2,1)S(1)}, bf16[256,1024]{1,0:T(8,128)(2,1)}, u32[]{:S(2)}, u32[]{:S(2)}) collective-permute-start(bf16[256,1024]{1,0:T(8,128)(2,1)S(1)} %pad_maximum_fusion.6.refs_26_.refs_31_), channel_id=1, source_target_pairs={{0,16},{2,18},{4,20},{6,22},{8,24},{10,26},{12,28},{14,30},{16,0},... | collective-permute-start | bytes 1572872 | tf_op jit(solution)/shard_map/ppermute | solution.py:667
  245.3 64.6 %collective-permute-start.26 = (bf16[256,1024]{1,0:T(8,128)(2,1)}, bf16[256,1024]{1,0:T(8,128)(2,1)}, u32[]{:S(2)}, u32[]{:S(2)}) collective-permute-start(bf16[256,1024]{1,0:T(8,128)(2,1)} %constant_dynamic-update-slice_fusion.7.refs_27_.refs_32_), channel_id=1, source_target_pairs={{0,16},{2,18},{4,20},{6,22},{8,24},{10,26},{12,28},{14,30},{16,0},... | collective-permute-start | bytes 1572872 | tf_op jit(solution)/shard_map/ppermute | solution.py:667
  245.3 34.8 %collective-permute-start.20 = (bf16[256,1024]{1,0:T(8,128)(2,1)}, bf16[256,1024]{1,0:T(8,128)(2,1)}, u32[]{:S(2)}, u32[]{:S(2)}) collective-permute-start(bf16[256,1024]{1,0:T(8,128)(2,1)} %collective-permute-done.8.refs_20_.refs_25_), channel_id=1, source_target_pairs={{0,2},{2,0},{4,6},{6,4},{8,10},{10,8},{12,14},{14,12},{16,18},{18,... | collective-permute-start | bytes 1572872 | tf_op jit(solution)/shard_map/ppermute | solution.py:667
  263.8 27.6 %collective-permute-start.22 = (bf16[256,1024]{1,0:T(8,128)(2,1)S(1)}, bf16[256,1024]{1,0:T(8,128)(2,1)}, u32[]{:S(2)}, u32[]{:S(2)}) collective-permute-start(bf16[256,1024]{1,0:T(8,128)(2,1)S(1)} %pad_maximum_fusion.6.refs_26_.refs_31_), channel_id=1, source_target_pairs={{0,2},{2,0},{4,6},{6,4},{8,10},{10,8},{12,14},{14,12},{16,18},{18,... | collective-permute-start | bytes 1572872 | tf_op jit(solution)/shard_map/ppermute | solution.py:667
  280.2 29.7 %collective-permute-start.28 = (bf16[256,1024]{1,0:T(8,128)(2,1)}, bf16[256,1024]{1,0:T(8,128)(2,1)}, u32[]{:S(2)}, u32[]{:S(2)}) collective-permute-start(bf16[256,1024]{1,0:T(8,128)(2,1)} %constant_dynamic-update-slice_fusion.7.refs_27_.refs_32_), channel_id=1, source_target_pairs={{0,2},{2,0},{4,6},{6,4},{8,10},{10,8},{12,14},{14,12},{16,18},{18,... | collective-permute-start | bytes 1572872 | tf_op jit(solution)/shard_map/ppermute | solution.py:667
  346.7 32.7 %collective-permute-start.36 = (bf16[128,2048]{1,0:T(8,128)(2,1)}, bf16[128,2048]{1,0:T(8,128)(2,1)S(1)}, u32[]{:S(2)}, u32[]{:S(2)}) collective-permute-start(bf16[128,2048]{1,0:T(8,128)(2,1)} %get-tuple-element.192.refs_1_.refs_10_), channel_id=1, source_target_pairs={{0,12},{2,14},{4,8},{6,10},{8,4},{10,6},{12,0},{14,2},{16,28},{18,... | collective-permute-start | bytes 1572872 | tf_op jit(solution)/shard_map/ppermute | solution.py:724
  527.3 65.2 %all-to-all-start = ((bf16[16,24,1024]{2,1,0:T(8,128)(2,1)}), bf16[16,24,1024]{2,1,0:T(8,128)(2,1)}, u32[]{:S(2)}, u32[]{:S(2)}) async-start(bf16[16,24,1024]{2,1,0:T(8,128)(2,1)} %copy_bitcast_fusion), calls=%async_computation | async-start | bytes 1572864 | tf_op jit(solution)/shard_map/all_to_all | solution.py:1213
  535.5 42.1 %collective-permute-start.79 = (bf16[2,24,2048]{2,1,0:T(8,128)(2,1)}, bf16[2,24,2048]{2,1,0:T(8,128)(2,1)}, u32[]{:S(2)}, u32[]{:S(2)}) collective-permute-start(bf16[2,24,2048]{2,1,0:T(8,128)(2,1)} %fusion.35), channel_id=1, source_target_pairs={{0,8},{2,10},{4,12},{6,14},{8,0},{10,2},{12,4},{14,6},{16,24},{18,... | collective-permute-start | bytes 589832 | tf_op jit(solution)/shard_map/ppermute | solution.py:1243
  536.9 40.6 %collective-permute-start.80 = (bf16[2,24,2048]{2,1,0:T(8,128)(2,1)}, bf16[2,24,2048]{2,1,0:T(8,128)(2,1)}, u32[]{:S(2)}, u32[]{:S(2)}) collective-permute-start(bf16[2,24,2048]{2,1,0:T(8,128)(2,1)} %fusion.35), channel_id=1, source_target_pairs={{0,16},{2,18},{4,20},{6,22},{8,24},{10,26},{12,28},{14,30},{16,0},... | collective-permute-start | bytes 589832 | tf_op jit(solution)/shard_map/ppermute | solution.py:1243
  537.5 40.1 %collective-permute-start.81 = (bf16[2,24,2048]{2,1,0:T(8,128)(2,1)}, bf16[2,24,2048]{2,1,0:T(8,128)(2,1)}, u32[]{:S(2)}, u32[]{:S(2)}) collective-permute-start(bf16[2,24,2048]{2,1,0:T(8,128)(2,1)} %fusion.35), channel_id=1, source_target_pairs={{0,24},{2,26},{4,28},{6,30},{8,16},{10,18},{12,20},{14,22},{16,8},... | collective-permute-start | bytes 589832 | tf_op jit(solution)/shard_map/ppermute | solution.py:1243
  550.1 43.6 %collective-permute-start.58 = (bf16[8,1,256,256]{3,2,1,0:T(8,128)(2,1)}, bf16[8,1,256,256]{3,2,1,0:T(8,128)(2,1)}, u32[]{:S(2)}, u32[]{:S(2)}) collective-permute-start(bf16[8,1,256,256]{3,2,1,0:T(8,128)(2,1)} %get-tuple-element.246), channel_id=1, source_target_pairs={{0,4},{2,6},{4,0},{6,2},{8,12},{10,14},{12,8},{14,10},{16,20},{18,... | collective-permute-start | bytes 3145736 | tf_op jit(solution)/shard_map/ppermute | solution.py:667
  553.1 43.8 %collective-permute-start.63 = (bf16[8,1,256,256]{3,2,1,0:T(8,128)(2,1)}, bf16[8,1,256,256]{3,2,1,0:T(8,128)(2,1)}, u32[]{:S(2)}, u32[]{:S(2)}) collective-permute-start(bf16[8,1,256,256]{3,2,1,0:T(8,128)(2,1)} %get-tuple-element.248), channel_id=1, source_target_pairs={{0,2},{2,0},{4,6},{6,4},{8,10},{10,8},{12,14},{14,12},{16,18},{18,... | collective-permute-start | bytes 3145736 | tf_op jit(solution)/shard_map/ppermute | solution.py:667
  653.0 25.6 %collective-permute-start.69 = (f32[128,2048]{1,0:T(8,128)S(1)}, f32[128,2048]{1,0:T(8,128)S(1)}, u32[]{:S(2)}, u32[]{:S(2)}) collective-permute-start(f32[128,2048]{1,0:T(8,128)S(1)} %copy-done.22), channel_id=1, source_target_pairs={{0,1},{1,0},{2,3},{3,2},{4,5},{5,4},{6,7},{7,6},{8,9},{9,8},{10,11... | collective-permute-start | bytes 3145736 | tf_op jit(solution)/shard_map/ppermute | solution.py:670
  (152 other events, 2805.7 us)
Sparse Core Ops, SparseCore 0:
  11.4 144.2 all-gather.2
  161.2 136.2 all-gather.4
